TPU v7x, 128 devices: a whole 4x4x4 slice. The times are simulated.
128 devices in a mesh: section: 8 (over x, core), row: 4 (over y), col: 4 (over z).
Axes of the slice: x: 4, y: 4, z: 4, core: 2. Of those that a mesh axis runs over, the one named last changes fastest.
Arguments:
- gate_grad: bfloat16 [16384, 5632], P('section', ('row', 'col')), parts along dimension 0, may hold values from -4 to 4
- up_grad: bfloat16 [16384, 5632], P('section', ('row', 'col')), parts along dimension 0, may hold values from -4 to 4
Outputs:
- gate_next: bfloat16 [16384, 5632], P('section', ('row', 'col')), parts along dimension 0
- up_next: bfloat16 [16384, 5632], P('section', ('row', 'col')), parts along dimension 0
There are 8 independent parts, one for each index of `section`. A program takes and returns all parts, laid end to end along the dimension named above; each array names one. Nothing has to cross between parts.
All inputs are finite; a program needn't handle non-finite values.
Results may differ from a plain program's by a relative error of at most 0.022.
Values may be sent and summed in bfloat16 or wider, within the bound.
No kernel may reach another device: no remote copies, remote signals or barrier semaphores. Data moves between devices by JAX's collectives and lax.ppermute only.
A program may use at most 128 MiB of HBM per device.

v0:
```python
import jax
import jax.numpy as jnp
from jax import lax
from jax.sharding import PartitionSpec as P

COEF_A = 3.4445
COEF_B = -4.775
COEF_C = 2.0315


def from_behind(shard, axis, by):
    size = lax.axis_size(axis)
    return lax.ppermute(shard, axis, [(i, (i + by) % size) for i in range(size)])


def per_device(gate_grad, up_grad):
    stacked = jnp.stack([gate_grad, up_grad])
    grid_side = lax.axis_size("row")
    total_rows = stacked.shape[1]
    block_rows = total_rows // grid_side
    dev_cols = stacked.shape[2]
    inverse_cols = 1.0 / (dev_cols * grid_side * grid_side)
    my_row = lax.axis_index("row")
    my_col = lax.axis_index("col")

    def one_piece(offset):
        top_row = offset // grid_side * block_rows
        left_row = offset % grid_side * block_rows
        upper_slab = lax.dynamic_slice_in_dim(stacked, top_row, block_rows, 1)
        lower_slab = lax.dynamic_slice_in_dim(stacked, left_row, block_rows, 1)
        return (
            jnp.einsum("mic,mjc->imj", upper_slab, lower_slab, preferred_element_type=jnp.float32)
            * inverse_cols
        )

    pieces = lax.map(
        one_piece,
        jnp.arange(block_rows * lax.axis_size(("row", "col")) // block_rows, dtype=jnp.int32),
    )
    summed = lax.psum_scatter(
        pieces.reshape(block_rows * lax.axis_size(("row", "col")), 2, block_rows).astype(
            jnp.bfloat16
        ),
        ("row", "col"),
        scatter_dimension=0,
        tiled=True,
    ).astype(jnp.float32)
    gram_block = jnp.transpose(summed, (1, 0, 2))
    gram_low = gram_block.astype(jnp.bfloat16)
    squared = jnp.zeros((2, block_rows, block_rows), jnp.float32)
    left_block = gram_low
    right_block = gram_low
    bit_count = grid_side.bit_length() - 1
    for bit_index in range(bit_count):
        reach = 1 << bit_index
        shifted = from_behind(left_block, "col", -reach)
        left_block = jnp.where(my_row >> bit_index & 1 == 1, shifted, left_block)
        shifted = from_behind(right_block, "row", -reach)
        right_block = jnp.where(my_col >> bit_index & 1 == 1, shifted, right_block)
    for step_index in range(grid_side):
        squared = squared + jnp.einsum(
            "mij,mjk->mik", left_block, right_block, preferred_element_type=jnp.float32
        )
        if step_index + 1 < grid_side:
            left_block = from_behind(left_block, "col", -1)
            right_block = from_behind(right_block, "row", -1)
    mixing = (COEF_B * gram_block + COEF_C * squared).astype(jnp.bfloat16)
    columns_all = lax.all_gather(stacked, "row", axis=2, tiled=True)
    product = jnp.einsum(
        "mij,mjk->mik",
        lax.all_gather(mixing, "col", axis=2, tiled=True),
        columns_all,
        preferred_element_type=jnp.float32,
    )
    own_part = lax.dynamic_slice_in_dim(columns_all, my_row * block_rows, block_rows, 1)
    updated = (COEF_A * own_part.astype(jnp.float32) + product).astype(jnp.bfloat16)
    returned_rows = lax.all_to_all(updated, "row", split_axis=2, concat_axis=1, tiled=True)
    return (returned_rows[0], returned_rows[1])


def solution(mesh):
    placed = (P("section", ("row", "col")), P("section", ("row", "col")))
    return jax.shard_map(
        per_device,
        mesh=mesh,
        in_specs=placed,
        out_specs=(P("section", ("row", "col")), P("section", ("row", "col"))),
        check_vma=False,
    )
```

profile of v0, /device:TPU:1, one launch (start us, length us, event | category | flops | bytes accessed | tf_op | source)
XLA Modules:
  0.0 572.6 jit_solution(18440825185282715366)
XLA Ops:
  8.1 2.1 pad_maximum_fusion
  10.1 79.5 %while.12 = (s32[]{:T(128)}, bf16[16,512,2,512]{1,3,2,0:T(8,128)(2,1)}, s32[16]{0:T(128)S(1)}, bf16[2,2048,352]{1,2,0:T(8,128)(2,1)S(1)}, s32[]{:T(128)}, /*inde...) while((s32[]{:T(128)}, ...), condition=%wide.region_1.2_spmd, body=%wide.region_0.1_spmd.sunk | while | flops 369623072 | bytes 3539872 | solution.py:36
  13.3 1.8 bitcast_dynamic-update-slice_fusion.2
  18.3 1.7 bitcast_dynamic-update-slice_fusion.2
  23.2 1.7 bitcast_dynamic-update-slice_fusion.2
  28.2 1.8 bitcast_dynamic-update-slice_fusion.2
  33.2 1.7 bitcast_dynamic-update-slice_fusion.2
  38.1 1.8 bitcast_dynamic-update-slice_fusion.2
  43.1 1.7 bitcast_dynamic-update-slice_fusion.2
  48.0 1.8 bitcast_dynamic-update-slice_fusion.2
  53.0 1.8 bitcast_dynamic-update-slice_fusion.2
  58.0 1.8 bitcast_dynamic-update-slice_fusion.2
  63.0 1.8 bitcast_dynamic-update-slice_fusion.2
  68.0 1.8 bitcast_dynamic-update-slice_fusion.2
  72.9 1.8 bitcast_dynamic-update-slice_fusion.2
  77.9 1.8 bitcast_dynamic-update-slice_fusion.2
  82.9 1.8 bitcast_dynamic-update-slice_fusion.2
  87.8 1.8 bitcast_dynamic-update-slice_fusion.2
  89.6 22.4 %copy.8 = bf16[16,512,2,512]{3,1,0,2:T(8,128)(2,1)} copy(bf16[16,512,2,512]{1,3,2,0:T(8,128)(2,1)} %get-tuple-element.58) | data formatting | bytes 33554432 | tf_op jit(solution)/shard_map/convert_element_type | solution.py:41
  112.7 205.7 %reduce-scatter.2.cloned.1.call-done = bf16[512,2,512]{2,0,1:T(8,128)(2,1)} async-done(((bf16[8192,2,512]{2,0,1:T(8,128)(2,1)}), bf16[512,2,512]{2,0,1:T(8,128)(2,1)}) %reduce-scatter.2.cloned.1.call-update) | async-done | bytes 1048592 | tf_op jit(solution)/shard_map/reduce_scatter | solution.py:40
  318.4 2.6 collective-permute-start
  321.6 21.6 %collective-permute-done = bf16[2,512,512]{2,1,0:T(8,128)(2,1)S(1)} collective-permute-done((bf16[2,512,512]{2,1,0:T(8,128)(2,1)}, bf16[2,512,512]{2,1,0:T(8,128)(2,1)S(1)}, u32[]{:S(2)}, u32[]{:S(2)}) %collective-permute-start) | collective-permute-done | bytes 1048608 | tf_op jit(solution)/shard_map/ppermute | solution.py:13
  343.2 1.9 collective-permute-done.2
  345.1 1.4 broadcast_select_fusion
  347.1 1.4 collective-permute-start.3
  348.5 22.5 %collective-permute-done.1 = bf16[2,512,512]{2,1,0:T(8,128)(2,1)} collective-permute-done((bf16[2,512,512]{2,1,0:T(8,128)(2,1)S(1)}, bf16[2,512,512]{2,1,0:T(8,128)(2,1)}, u32[]{:S(2)}, u32[]{:S(2)}) %collective-permute-start.1) | collective-permute-done | bytes 1048608 | tf_op jit(solution)/shard_map/ppermute | solution.py:13
  371.2 2.1 collective-permute-start.4
  373.4 2.2 collective-permute-start.5
  375.6 17.8 %collective-permute-done.4 = bf16[2,512,512]{2,1,0:T(8,128)(2,1)S(1)} collective-permute-done((bf16[2,512,512]{2,1,0:T(8,128)(2,1)S(1)}, bf16[2,512,512]{2,1,0:T(8,128)(2,1)S(1)}, u32[]{:S(2)}, u32[]{:S(2)}) %collective-permute-start.4) | collective-permute-done | bytes 1048608 | tf_op jit(solution)/shard_map/ppermute | solution.py:13
  393.4 3.4 collective-permute-start.6
  396.8 1.8 collective-permute-start.7
  398.6 17.3 %collective-permute-done.6 = bf16[2,512,512]{2,1,0:T(8,128)(2,1)S(1)} collective-permute-done((bf16[2,512,512]{2,1,0:T(8,128)(2,1)S(1)}, bf16[2,512,512]{2,1,0:T(8,128)(2,1)S(1)}, u32[]{:S(2)}, u32[]{:S(2)}) %collective-permute-start.6) | collective-permute-done | bytes 1048608 | tf_op jit(solution)/shard_map/ppermute | solution.py:13
  415.9 3.4 collective-permute-start.8
  419.3 1.5 collective-permute-start.9
  421.5 0.7 fusion.6
  422.2 0.7 fusion.7
  422.9 14.6 %collective-permute-done.8 = bf16[2,512,512]{2,1,0:T(8,128)(2,1)S(1)} collective-permute-done((bf16[2,512,512]{2,1,0:T(8,128)(2,1)S(1)}, bf16[2,512,512]{2,1,0:T(8,128)(2,1)S(1)}, u32[]{:S(2)}, u32[]{:S(2)}) %collective-permute-start.8) | collective-permute-done | bytes 1048608 | tf_op jit(solution)/shard_map/ppermute | solution.py:13
  437.5 1.9 collective-permute-done.9
  439.5 1.9 fusion.3
  441.4 53.3 %all-gather.5.cloned.1.call-done = bf16[2,512,2048]{2,1,0:T(8,128)(2,1)} async-done(((bf16[2,512,512]{2,1,0:T(8,128)(2,1)}), bf16[2,512,2048]{2,1,0:T(8,128)(2,1)}) %all-gather.5.cloned.1.call-update) | async-done | bytes 4194320 | tf_op jit(solution)/shard_map/all_gather | solution.py:71
  494.7 10.7 %add_convert_fusion = bf16[2,512,1408]{1,2,0:T(8,128)(2,1)S(1)} fusion(bf16[2,512,2048]{2,1,0:T(8,128)(2,1)} %all-gather.5.cloned.1.call-done, bf16[2,2048,1408]{1,2,0:T(8,128)(2,1)} %all-gather.3.cloned.1.call-done, s32[]{:T(128)S(6)} %select_n.60), kind=kOutput, calls=%fused_computation.4 | convolution fusion | flops 5911347200 | bytes 21495812 | tf_op jit(solution)/shard_map/mij,mjk->mik/dot_general | solution.py:69
  505.4 11.3 %copy.10 = bf16[2,512,1408]{1,0,2:T(2,128)(2,1)S(1)} copy(bf16[2,512,1408]{1,2,0:T(8,128)(2,1)S(1)} %add_convert_fusion) | data formatting | bytes 5767168 | tf_op jit(solution)/shard_map/convert_element_type | solution.py:76
  516.8 37.6 %all_to_all.15 = bf16[2,512,1408]{1,0,2:T(2,128)(2,1)S(1)} all-to-all(bf16[2,512,1408]{1,0,2:T(2,128)(2,1)S(1)} %copy.10), channel_id=1, replica_groups=mesh['section'=8,'row'=4,'col'=4] {'row'}, dimensions={2} | all-to-all | bytes 5767168 | tf_op jit(solution)/shard_map/all_to_all | solution.py:77
  554.3 4.1 fusion.4
  558.4 1.9 copy.11
  560.3 1.5 copy.14
  561.8 1.9 copy.12
  563.7 1.5 copy.15
  (37 shorter events, 12.1 us)
Async XLA Ops:
  8.0 310.4 %reduce-scatter.2.cloned.1.call-start = ((), (), s32[]{:S(2)}) async-start(), calls=%async_computation.3 | async-start | bytes 17825792 | tf_op jit(solution)/shard_map/reduce_scatter | solution.py:40
  89.6 22.4 %copy-start = (bf16[2,2048,352]{1,2,0:T(8,128)(2,1)}, bf16[2,2048,352]{1,2,0:T(8,128)(2,1)S(1)}, u32[]{:S(2)}) copy-start(bf16[2,2048,352]{1,2,0:T(8,128)(2,1)S(1)} %get-tuple-element.137) | copy-start | bytes 8650756
  112.0 329.4 %all-gather.3.cloned.1.call-start = ((), (), s32[]{:S(2)}) async-start(), calls=%async_computation.2 | async-start | bytes 14417920 | tf_op jit(solution)/shard_map/all_gather | solution.py:68
  112.6 382.1 %all-gather.5.cloned.1.call-start = ((), (), s32[]{:S(2)}) async-start(), calls=%async_computation.4 | async-start | bytes 5242880 | tf_op jit(solution)/shard_map/all_gather | solution.py:71
  318.4 24.8 %collective-permute-start = (bf16[2,512,512]{2,1,0:T(8,128)(2,1)}, bf16[2,512,512]{2,1,0:T(8,128)(2,1)S(1)}, u32[]{:S(2)}, u32[]{:S(2)}) collective-permute-start(bf16[2,512,512]{2,1,0:T(8,128)(2,1)} %bitcast.46), channel_id=1, source_target_pairs={{0,3},{1,0},{2,1},{3,2},{4,7},{5,4},{6,5},{7,6},{8,11},{9,8},{10,9... | collective-permute-start | bytes 3145736 | tf_op jit(solution)/shard_map/ppermute | solution.py:13
  321.0 24.1 %collective-permute-start.2 = (bf16[2,512,512]{2,1,0:T(8,128)(2,1)}, bf16[2,512,512]{2,1,0:T(8,128)(2,1)}, u32[]{:S(2)}, u32[]{:S(2)}) collective-permute-start(bf16[2,512,512]{2,1,0:T(8,128)(2,1)} %bitcast.47), channel_id=1, source_target_pairs={{0,12},{4,0},{8,4},{12,8},{1,13},{5,1},{9,5},{13,9},{2,14},{6,2},{... | collective-permute-start | bytes 3145736 | tf_op jit(solution)/shard_map/ppermute | solution.py:13
  346.5 24.5 %collective-permute-start.1 = (bf16[2,512,512]{2,1,0:T(8,128)(2,1)S(1)}, bf16[2,512,512]{2,1,0:T(8,128)(2,1)}, u32[]{:S(2)}, u32[]{:S(2)}) collective-permute-start(bf16[2,512,512]{2,1,0:T(8,128)(2,1)S(1)} %get-tuple-element.70), channel_id=1, source_target_pairs={{0,2},{1,3},{2,0},{3,1},{4,6},{5,7},{6,4},{7,5},{8,10},{9,11},{10,... | collective-permute-start | bytes 3145736 | tf_op jit(solution)/shard_map/ppermute | solution.py:13
  347.1 26.2 %collective-permute-start.3 = (bf16[2,512,512]{2,1,0:T(8,128)(2,1)S(1)}, bf16[2,512,512]{2,1,0:T(8,128)(2,1)S(1)}, u32[]{:S(2)}, u32[]{:S(2)}) collective-permute-start(bf16[2,512,512]{2,1,0:T(8,128)(2,1)S(1)} %get-tuple-element.69), channel_id=1, source_target_pairs={{0,8},{4,12},{8,0},{12,4},{1,9},{5,13},{9,1},{13,5},{2,10},{6,14},... | collective-permute-start | bytes 3145736 | tf_op jit(solution)/shard_map/ppermute | solution.py:13
  371.2 22.2 %collective-permute-start.4 = (bf16[2,512,512]{2,1,0:T(8,128)(2,1)S(1)}, bf16[2,512,512]{2,1,0:T(8,128)(2,1)S(1)}, u32[]{:S(2)}, u32[]{:S(2)}) collective-permute-start(bf16[2,512,512]{2,1,0:T(8,128)(2,1)S(1)} %broadcast_select_fusion.3), channel_id=1, source_target_pairs={{0,3},{1,0},{2,1},{3,2},{4,7},{5,4},{6,5},{7,6},{8,11},{9,8},{10,9... | collective-permute-start | bytes 3145736 | tf_op jit(solution)/shard_map/ppermute | solution.py:13
  373.4 23.4 %collective-permute-start.5 = (bf16[2,512,512]{2,1,0:T(8,128)(2,1)S(1)}, bf16[2,512,512]{2,1,0:T(8,128)(2,1)S(1)}, u32[]{:S(2)}, u32[]{:S(2)}) collective-permute-start(bf16[2,512,512]{2,1,0:T(8,128)(2,1)S(1)} %broadcast_select_fusion.1), channel_id=1, source_target_pairs={{0,12},{4,0},{8,4},{12,8},{1,13},{5,1},{9,5},{13,9},{2,14},{6,2},{... | collective-permute-start | bytes 3145736 | tf_op jit(solution)/shard_map/ppermute | solution.py:13
  393.4 22.5 %collective-permute-start.6 = (bf16[2,512,512]{2,1,0:T(8,128)(2,1)S(1)}, bf16[2,512,512]{2,1,0:T(8,128)(2,1)S(1)}, u32[]{:S(2)}, u32[]{:S(2)}) collective-permute-start(bf16[2,512,512]{2,1,0:T(8,128)(2,1)S(1)} %collective-permute-done.4), channel_id=1, source_target_pairs={{0,3},{1,0},{2,1},{3,2},{4,7},{5,4},{6,5},{7,6},{8,11},{9,8},{10,9... | collective-permute-start | bytes 3145736 | tf_op jit(solution)/shard_map/ppermute | solution.py:13
  396.8 22.5 %collective-permute-start.7 = (bf16[2,512,512]{2,1,0:T(8,128)(2,1)S(1)}, bf16[2,512,512]{2,1,0:T(8,128)(2,1)S(1)}, u32[]{:S(2)}, u32[]{:S(2)}) collective-permute-start(bf16[2,512,512]{2,1,0:T(8,128)(2,1)S(1)} %collective-permute-done.5), channel_id=1, source_target_pairs={{0,12},{4,0},{8,4},{12,8},{1,13},{5,1},{9,5},{13,9},{2,14},{6,2},{... | collective-permute-start | bytes 3145736 | tf_op jit(solution)/shard_map/ppermute | solution.py:13
  415.9 21.6 %collective-permute-start.8 = (bf16[2,512,512]{2,1,0:T(8,128)(2,1)S(1)}, bf16[2,512,512]{2,1,0:T(8,128)(2,1)S(1)}, u32[]{:S(2)}, u32[]{:S(2)}) collective-permute-start(bf16[2,512,512]{2,1,0:T(8,128)(2,1)S(1)} %collective-permute-done.6), channel_id=1, source_target_pairs={{0,3},{1,0},{2,1},{3,2},{4,7},{5,4},{6,5},{7,6},{8,11},{9,8},{10,9... | collective-permute-start | bytes 3145736 | tf_op jit(solution)/shard_map/ppermute | solution.py:13
  419.3 20.1 %collective-permute-start.9 = (bf16[2,512,512]{2,1,0:T(8,128)(2,1)S(1)}, bf16[2,512,512]{2,1,0:T(8,128)(2,1)S(1)}, u32[]{:S(2)}, u32[]{:S(2)}) collective-permute-start(bf16[2,512,512]{2,1,0:T(8,128)(2,1)S(1)} %collective-permute-done.7), channel_id=1, source_target_pairs={{0,12},{4,0},{8,4},{12,8},{1,13},{5,1},{9,5},{13,9},{2,14},{6,2},{... | collective-permute-start | bytes 3145736 | tf_op jit(solution)/shard_map/ppermute | solution.py:13
  422.2 17.3 %copy-start.1 = (bf16[512,2,512]{2,0,1:T(8,128)(2,1)S(1)}, bf16[512,2,512]{2,0,1:T(8,128)(2,1)}, u32[]{:S(2)}) copy-start(bf16[512,2,512]{2,0,1:T(8,128)(2,1)} %reduce-scatter.2.cloned.1.call-done) | copy-start | bytes 3145732
Sparse Core Ops, SparseCore 0:
  112.2 206.1 reduce-scatter.1
Sparse Core Ops, SparseCore 1:
  114.2 125.8 all-gather.2
  441.4 53.2 all-gather.4
where the time goes:
time: 574 us; the launch traced here: 573 us
  waiting for transfers between devices  357 us (62%)
  local copies, waits for them, and re-layouts  53.9 us (9%)
  matrix products  42.9 us (7%)
  loops' own time  41.9 us (7%)
  blocking collectives  37.6 us (7%)
  starting transfers between devices  19.7 us (3%)
  between operations  15.6 us (3%)
    reduce_scatter x1, waiting for transfers between devices, per_device(): lax.psum_scatter(pieces.reshape(block_rows * lax.axis_size(('row', 'col')...  206 us
    ppermute x10, waiting for transfers between devices, from_behind(): lax.ppermute(shard, axis, [(i, (i + by) % size) for i in range(size)])  97.7 us
    all_gather x1, waiting for transfers between devices, per_device(): lax.all_gather(mixing, 'col', axis=2, tiled=True)  53.3 us
    another operation x1, loops' own time, per_device(): lax.map(one_piece, jnp.arange(block_rows * lax.axis_size(('row', 'col'))...  41.9 us
    all_to_all x1, blocking collectives, per_device(): lax.all_to_all(updated, 'row', split_axis=2, concat_axis=1, tiled=True)  37.6 us
    dot_general x16, matrix products, one_piece(): jnp.einsum('mic,mjc->imj', upper_slab, lower_slab, preferred_element_type...  28.2 us
    convert_element_type x1, local copies, waits for them, and re-layouts, per_device(): pieces.reshape(block_rows * lax.axis_size(('row', 'col')), 2, block_rows)  22.4 us
    ppermute x10, starting transfers between devices, from_behind(): lax.ppermute(shard, axis, [(i, (i + by) % size) for i in range(size)])  19.6 us
  transfers between devices with their start and end apart: 13, of which 9 were waited for; matrix products, arithmetic and copies ran while one was open for 1% of the time, Pallas kernels for 0%

commit v1 on v0

v1 whole, which is shorter than its diff:
```python
import functools

import jax
import jax.numpy as jnp
from jax import lax
from jax.experimental import pallas as pl
from jax.experimental.pallas import tpu as pltpu
from jax.sharding import PartitionSpec as P

COEF_A = 3.4445
COEF_B = -4.775
COEF_C = 2.0315

AXES = ("section", "row", "col")
BLOCK = 128
VMEM_LIMIT = 56 * 1024 * 1024


def device_pairs(route):
    pairs = []
    for x in range(4):
        for core in range(2):
            for y in range(4):
                for z in range(4):
                    target = route(core, y, z)
                    if target is not None:
                        to_core, to_y, to_z = target
                        pairs.append(
                            (((x * 2 + core) * 4 + y) * 4 + z, ((x * 2 + to_core) * 4 + to_y) * 4 + to_z)
                        )
    return pairs


def outer(i):
    return i in (0, 3)


OTHER_CORE = device_pairs(lambda c, y, z: (1 - c, y, z))
GATE_OUT = device_pairs(lambda c, y, z: (0, y ^ 1, z) if c == (1 if outer(y) else 0) else None)
UP_OUT = device_pairs(lambda c, y, z: (1, y, z ^ 1) if c == (1 if outer(z) else 0) else None)
GATE_BACK = [(b, a) for a, b in GATE_OUT]
UP_BACK = [(b, a) for a, b in UP_OUT]
HOP_1 = device_pairs(lambda c, y, z: (c, y, z ^ 1) if c == 0 else (c, y ^ 1, z))
HOP_2 = device_pairs(lambda c, y, z: (c, y, 3 - z) if c == 0 else (c, 3 - y, z))
HOP_3 = device_pairs(lambda c, y, z: (c, 3 - y, z) if c == 0 else (c, y, 3 - z))


def send(values, pairs):
    return lax.ppermute(values, AXES, pairs)


def extend(wide, columns):
    rows = columns.shape[0]
    wide[0:rows, :] = columns[...]
    wide[rows : rows + rows // 2, :] = columns[0 : rows // 2, :]


def block_row(wide, index, span):
    first = pl.multiple_of(index * BLOCK, BLOCK)
    return lax.dot_general(
        wide[pl.ds(first, BLOCK), :],
        wide[pl.ds(first, span), :],
        (((1,), (1,)), ((), ())),
        preferred_element_type=jnp.float32,
    )


def first_terms_kernel(order, columns, terms, wide):
    extend(wide, columns)
    blocks, _, span = terms.shape

    def one(k, carry):
        terms[k] = block_row(wide, order[k], span)
        return carry

    lax.fori_loop(0, blocks, one, 0)


def first_terms(order, columns, span):
    rows, dev_cols = columns.shape
    return pl.pallas_call(
        first_terms_kernel,
        out_shape=jax.ShapeDtypeStruct((order.shape[0], BLOCK, span), jnp.float32),
        in_specs=[
            pl.BlockSpec(memory_space=pltpu.SMEM),
            pl.BlockSpec(memory_space=pltpu.VMEM),
        ],
        out_specs=pl.BlockSpec(memory_space=pltpu.VMEM),
        scratch_shapes=[pltpu.VMEM((rows + rows // 2, dev_cols), jnp.bfloat16)],
        compiler_params=pltpu.CompilerParams(vmem_limit_bytes=VMEM_LIMIT),
        cost_estimate=pl.CostEstimate(
            flops=2 * order.shape[0] * BLOCK * span * dev_cols, bytes_accessed=12000000, transcendentals=0
        ),
    )(order, columns)


def add_terms_kernel(first_block, scale, order, columns, terms, total, wide):
    extend(wide, columns)
    blocks, _, span = total.shape

    def one(k, carry):
        value = terms[first_block + k] + block_row(wide, order[first_block + k], span)
        total[k] = (value * scale).astype(total.dtype)
        return carry

    lax.fori_loop(0, blocks, one, 0)


def add_terms(order, columns, terms, first_block, blocks, scale, dtype):
    rows, dev_cols = columns.shape
    span = terms.shape[2]
    return pl.pallas_call(
        functools.partial(add_terms_kernel, first_block, scale),
        out_shape=jax.ShapeDtypeStruct((blocks, BLOCK, span), dtype),
        in_specs=[
            pl.BlockSpec(memory_space=pltpu.SMEM),
            pl.BlockSpec(memory_space=pltpu.VMEM),
            pl.BlockSpec(memory_space=pltpu.VMEM),
        ],
        out_specs=pl.BlockSpec(memory_space=pltpu.VMEM),
        scratch_shapes=[pltpu.VMEM((rows + rows // 2, dev_cols), jnp.bfloat16)],
        compiler_params=pltpu.CompilerParams(vmem_limit_bytes=VMEM_LIMIT),
        cost_estimate=pl.CostEstimate(
            flops=2 * blocks * BLOCK * span * dev_cols, bytes_accessed=12000000, transcendentals=0
        ),
    )(order, columns, terms)


def step_kernel(order, columns, *rest):
    pieces, (result, gram, low, linear) = rest[:-4], rest[-4:]
    rows = columns.shape[0]
    count = rows // BLOCK
    place = 0
    for piece in pieces:
        span = piece.shape[2]
        for k in range(piece.shape[0]):
            index = order[place]
            place += 1
            top = pl.multiple_of(index * BLOCK, BLOCK)
            for shift in range(span // BLOCK):
                left = pl.multiple_of(((index + shift) % count) * BLOCK, BLOCK)
                block = piece[k, :, shift * BLOCK : (shift + 1) * BLOCK]
                gram[pl.ds(top, BLOCK), pl.ds(left, BLOCK)] = block
                if 0 < shift < span // BLOCK - 1:
                    gram[pl.ds(left, BLOCK), pl.ds(top, BLOCK)] = block.T
    tile = 256

    def multiply(t, carry):
        at = pl.ds(pl.multiple_of(t * tile, tile), tile)
        value = jnp.dot(gram[at, :], columns[...], preferred_element_type=jnp.float32)
        low[at, :] = value.astype(jnp.bfloat16)
        linear[at, :] = COEF_A * columns[at, :].astype(jnp.float32) + COEF_B * value
        return carry

    lax.fori_loop(0, rows // tile, multiply, 0)

    def again(t, carry):
        at = pl.ds(pl.multiple_of(t * tile, tile), tile)
        value = jnp.dot(gram[at, :], low[...], preferred_element_type=jnp.float32)
        result[at, :] = (linear[at, :] + COEF_C * value).astype(jnp.bfloat16)
        return carry

    lax.fori_loop(0, rows // tile, again, 0)


def newton_step(order, columns, pieces):
    rows, dev_cols = columns.shape
    return pl.pallas_call(
        step_kernel,
        out_shape=jax.ShapeDtypeStruct(columns.shape, jnp.bfloat16),
        in_specs=[pl.BlockSpec(memory_space=pltpu.SMEM)]
        + [pl.BlockSpec(memory_space=pltpu.VMEM)] * (1 + len(pieces)),
        out_specs=pl.BlockSpec(memory_space=pltpu.VMEM),
        scratch_shapes=[
            pltpu.VMEM((rows, rows), jnp.bfloat16),
            pltpu.VMEM((rows, dev_cols), jnp.bfloat16),
            pltpu.VMEM((rows, dev_cols), jnp.float32),
        ],
        compiler_params=pltpu.CompilerParams(vmem_limit_bytes=VMEM_LIMIT),
        cost_estimate=pl.CostEstimate(
            flops=4 * rows * rows * dev_cols, bytes_accessed=8000000, transcendentals=0
        ),
    )(order, columns, *pieces)


def per_device(gate_grad, up_grad):
    rows, dev_cols = gate_grad.shape
    span = rows // 2 + BLOCK
    scale = 1.0 / (dev_cols * lax.axis_size(("row", "col")))
    core = lax.axis_index("section") % 2
    y = lax.axis_index("row")
    z = lax.axis_index("col")
    gate_first = (y == 0) | (y == 3)
    up_first = (z == 0) | (z == 3)
    on_gate = core == 0

    y_low, y_high = ((y == 1) | (y == 2)).astype(jnp.int32), (y >= 2).astype(jnp.int32)
    z_low, z_high = ((z == 1) | (z == 2)).astype(jnp.int32), (z >= 2).astype(jnp.int32)
    p = jnp.where(on_gate, z_low, y_low)
    q = jnp.where(on_gate, z_high, y_high)
    r = jnp.where(on_gate, y_high, z_high)

    def block_a(dp, dq, dr):
        return 4 * (p ^ dp) + 2 * (q ^ dq) + (r ^ dr)

    def block_b(dp, dq, dr):
        return 8 + 4 * (q ^ dq) + 2 * (p ^ dp) + (r ^ dr)

    order = jnp.stack(
        [
            block(dp, dq, dr)
            for dp, dq in ((1, 1), (1, 0), (0, 1), (0, 0))
            for block in (block_a, block_b)
            for dr in (0, 1)
        ]
    )

    from_gate = send(gate_grad, GATE_OUT)
    from_up = send(up_grad, UP_OUT)
    from_core = send(jnp.where(on_gate, up_grad, gate_grad), OTHER_CORE)
    own = jnp.where(
        on_gate,
        jnp.where(gate_first, gate_grad, from_core),
        jnp.where(up_first, from_core, up_grad),
    )
    terms = first_terms(order, own, span)
    partner = jnp.where(on_gate, from_gate, from_up)

    corner = add_terms(order, partner, terms, 0, 4, scale, jnp.bfloat16)
    got_a = send(corner[0:2], HOP_1)
    got_b = send(corner[2:4], HOP_2)
    rest = add_terms(order, partner, terms, 4, 12, scale, jnp.float32)
    side_1 = jnp.concatenate(
        [rest[0:2].astype(jnp.bfloat16), (rest[2:4] + got_b.astype(jnp.float32)).astype(jnp.bfloat16)]
    )
    side_2 = jnp.concatenate(
        [(rest[4:6] + got_a.astype(jnp.float32)).astype(jnp.bfloat16), rest[6:8].astype(jnp.bfloat16)]
    )
    got_1 = send(side_1, HOP_1)
    got_2 = send(side_2, HOP_2)
    mine = (
        (rest[8:12] + got_1.astype(jnp.float32) + got_2.astype(jnp.float32))
    ).reshape(2, 2, BLOCK, span)
    got_3 = send(mine[:, 1].astype(jnp.bfloat16), HOP_3)
    done = (mine[:, 0] + got_3.astype(jnp.float32)).astype(jnp.bfloat16)

    far = send(done, HOP_3)
    both = jnp.stack([done, far], axis=1).reshape(4, BLOCK, span)
    all_1 = send(both, HOP_1)
    all_2 = send(both, HOP_2)
    last_a = send(all_2[0:2], HOP_1)
    last_b = send(all_1[2:4], HOP_2)
    pieces = (last_a, last_b, all_1, all_2, both)

    partner_next = newton_step(order, partner, pieces)
    gate_back = send(partner_next, GATE_BACK)
    up_back = send(partner_next, UP_BACK)
    own_next = newton_step(order, own, pieces)
    core_back = send(own_next, OTHER_CORE)

    gate_kept = jnp.where(on_gate, own_next, core_back)
    up_kept = jnp.where(on_gate, core_back, own_next)
    gate_next = jnp.where(gate_first == on_gate, gate_kept, gate_back)
    up_next = jnp.where(up_first == on_gate, up_kept, up_back)
    return gate_next, up_next


def solution(mesh):
    placed = (P("section", ("row", "col")), P("section", ("row", "col")))
    return jax.shard_map(
        per_device,
        mesh=mesh,
        in_specs=placed,
        out_specs=placed,
        check_vma=False,
    )
```

time: 574 us -> 224 us (0.39)
  waiting for transfers between devices: 357 us -> 74.2 us
  Pallas kernels: 0 us -> 66.8 us
  matrix products: 42.9 us -> 0 us
  loops' own time: 41.9 us -> 0 us
  blocking collectives: 37.6 us -> 0 us
  local copies, waits for them, and re-layouts: 53.9 us -> 32.7 us
  between operations: 15.6 us -> 0.87 us
  starting transfers between devices: 19.7 us -> 33.3 us
  other arithmetic: 3.68 us -> 15.6 us
    reduce_scatter x1 -> x0, waiting for transfers between devices: 206 us -> none  [per_device(): lax.psum_scatter(pieces.reshape(block_rows * lax.axis_size(('row', 'col')...]
    pallas_call x0 -> x5, Pallas kernels: none -> 66.8 us  [the longest x2 35.2 us: newton_step(): pl.pallas_call(step_kernel, out_shape=jax.ShapeDtypeStruct(columns.shape,...]
    all_gather x2 -> x0, waiting for transfers between devices: 53.4 us -> none  [the longest x1 53.3 us: per_device(): lax.all_gather(mixing, 'col', axis=2, tiled=True)]
    dot_general x21 -> x0, matrix products: 42.9 us -> none  [the longest x16 28.2 us: one_piece(): jnp.einsum('mic,mjc->imj', upper_slab, lower_slab, preferred_element_type...]
    another operation x1 -> x0, loops' own time: 41.9 us -> none  [per_device(): lax.map(one_piece, jnp.arange(block_rows * lax.axis_size(('row', 'col'))...]
    all_to_all x1 -> x0, blocking collectives: 37.6 us -> none  [per_device(): lax.all_to_all(updated, 'row', split_axis=2, concat_axis=1, tiled=True)]
    convert_element_type x2 -> x1, local copies, waits for them, and re-layouts: 33.7 us -> 0.06 us  [per_device(): got_3 = send(mine[:, 1].astype(jnp.bfloat16), HOP_3)]
    ppermute x10 -> x16, waiting for transfers between devices: 97.7 us -> 74.2 us  [send(): return lax.ppermute(values, AXES, pairs)]
  transfers between devices with their start and end apart: 13 -> 16, of which waited for: 9 -> 10; matrix products, arithmetic and copies ran while one was open for 1% -> 12% of each run, Pallas kernels for 0% -> 13%
where the time goes in v1:
time: 224 us
  waiting for transfers between devices  74.2 us (33%)
  Pallas kernels  66.8 us (30%)
  starting transfers between devices  33.3 us (15%)
  local copies, waits for them, and re-layouts  32.7 us (15%)
  other arithmetic  15.6 us (7%)
    ppermute x16, waiting for transfers between devices, send(): return lax.ppermute(values, AXES, pairs)  74.2 us
    pallas_call x2, Pallas kernels, newton_step(): pl.pallas_call(step_kernel, out_shape=jax.ShapeDtypeStruct(columns.shape,...  35.2 us
    ppermute x16, starting transfers between devices, send(): return lax.ppermute(values, AXES, pairs)  33.3 us
    pallas_call x2, Pallas kernels, add_terms(): pl.pallas_call(functools.partial(add_terms_kernel, first_block, scale), o...  19.5 us
    ppermute x6, local copies, waits for them, and re-layouts, send(): return lax.ppermute(values, AXES, pairs)  13.8 us
    pallas_call x1, Pallas kernels, first_terms(): pl.pallas_call(first_terms_kernel, out_shape=jax.ShapeDtypeStruct((order....  12.2 us
    unnamed x20, local copies, waits for them, and re-layouts  9.99 us
  transfers between devices with their start and end apart: 16, of which 10 were waited for; matrix products, arithmetic and copies ran while one was open for 12% of the time, Pallas kernels for 13%

profile of v1, /device:TPU:1, one launch (start us, length us, event | category | flops | bytes accessed | tf_op | source)
XLA Modules:
  0.0 223.6 jit_solution(3674788054700735059)
XLA Ops:
  0.6 5.7 %collective-permute-start.1 = (bf16[2048,352]{0,1:T(8,128)(2,1)}, bf16[2048,352]{0,1:T(8,128)(2,1)}, u32[]{:S(2)}, u32[]{:S(2)}) collective-permute-start(bf16[2048,352]{0,1:T(8,128)(2,1)} %param.2), channel_id=1, source_target_pairs={{4,0},{5,1},{6,2},{7,3},{8,12},{9,13},{10,14},{11,15},{16,4},{17,5... | collective-permute-start | bytes 4325384 | tf_op jit(solution)/shard_map/ppermute | solution.py:49
  6.3 3.5 %collective-permute-start.2 = (bf16[2048,352]{0,1:T(8,128)(2,1)}, bf16[2048,352]{0,1:T(8,128)(2,1)}, u32[]{:S(2)}, u32[]{:S(2)}) collective-permute-start(bf16[2048,352]{0,1:T(8,128)(2,1)} %param.3), channel_id=1, source_target_pairs={{1,16},{2,19},{5,20},{6,23},{9,24},{10,27},{13,28},{14,31},{16,17}... | collective-permute-start | bytes 4325384 | tf_op jit(solution)/shard_map/ppermute | solution.py:49
  9.9 1.9 copy.18
  11.8 1.9 copy.15
  13.6 1.4 broadcast_select_fusion.1
  15.0 2.5 %copy.17 = bf16[2048,352]{0,1:T(8,128)(2,1)} copy(bf16[2048,352]{1,0:T(8,128)(2,1)} %broadcast_select_fusion.1) | data formatting | bytes 2883584 | tf_op jit(solution)/shard_map/jit(_where)/select_n | solution.py:220
  18.2 3.3 %collective-permute-done.1 = bf16[2048,352]{0,1:T(8,128)(2,1)} collective-permute-done((bf16[2048,352]{0,1:T(8,128)(2,1)}, bf16[2048,352]{0,1:T(8,128)(2,1)}, u32[]{:S(2)}, u32[]{:S(2)}) %collective-permute-start.1) | collective-permute-done | bytes 1441824 | tf_op jit(solution)/shard_map/ppermute | solution.py:49
  21.5 2.6 %copy.22 = bf16[2048,352]{1,0:T(8,128)(2,1)} copy(bf16[2048,352]{0,1:T(8,128)(2,1)} %collective-permute-done.1) | data formatting | bytes 2883584 | tf_op jit(solution)/shard_map/ppermute | solution.py:49
  24.1 2.9 %collective-permute-done.2 = bf16[2048,352]{0,1:T(8,128)(2,1)} collective-permute-done((bf16[2048,352]{0,1:T(8,128)(2,1)}, bf16[2048,352]{0,1:T(8,128)(2,1)}, u32[]{:S(2)}, u32[]{:S(2)}) %collective-permute-start.2) | collective-permute-done | bytes 1441824 | tf_op jit(solution)/shard_map/ppermute | solution.py:49
  27.0 2.6 %copy.23 = bf16[2048,352]{1,0:T(8,128)(2,1)} copy(bf16[2048,352]{0,1:T(8,128)(2,1)} %collective-permute-done.2) | data formatting | bytes 2883584 | tf_op jit(solution)/shard_map/ppermute | solution.py:49
  29.6 2.8 %broadcast_select_fusion.columns = bf16[2048,352]{1,0:T(8,128)(2,1)} fusion(bf16[2048,352]{1,0:T(8,128)(2,1)} %copy.22, bf16[2048,352]{1,0:T(8,128)(2,1)} %copy.23, pred[]{:T(512)S(6)} %eq.37), kind=kLoop, calls=%fused_computation.5 | loop fusion | flops 720896 | bytes 4325377 | tf_op jit(solution)/shard_map/jit(_where)/select_n | solution.py:227
  32.3 2.6 %copy.19 = bf16[2048,352]{1,0:T(8,128)(2,1)} copy(bf16[2048,352]{0,1:T(8,128)(2,1)} %collective-permute-done) | data formatting | bytes 2883584 | tf_op jit(solution)/shard_map/ppermute | solution.py:49
  34.9 2.8 %select_select_fusion.2.columns = bf16[2048,352]{1,0:T(8,128)(2,1)} fusion(bf16[2048,352]{1,0:T(8,128)(2,1)} %copy.19, bf16[2048,352]{1,0:T(8,128)(2,1)S(1)} %copy.15, bf16[2048,352]{1,0:T(8,128)(2,1)S(1)} %copy.18, pred[]{:T(512)S(6)} %or.15, pred[]{:T(512)S(6)} %or.12, pred[]{:T(512)S(6)} %eq.37), kind=kLoop, calls=%fused_computation.4 | loop fusion | flops 2162688 | bytes 5767171 | tf_op jit(solution)/shard_map/jit(_where)/select_n | solution.py:221
  37.7 12.2 %shard_map.41.terms = f32[16,128,1152]{2,1,0:T(8,128)} custom-call(s32[16]{0:T(128)} %stack.76.order, bf16[2048,352]{1,0:T(8,128)(2,1)} %select_select_fusion.2.columns), custom_call_target="tpu_custom_call" | custom-call | flops 1660944384 | bytes 12000000 | tf_op jit(solution)/shard_map/pallas_call | solution.py:81
  49.9 7.1 %shard_map.43 = bf16[4,128,1152]{2,1,0:T(8,128)(2,1)} custom-call(s32[16]{0:T(128)} %stack.76.order, bf16[2048,352]{1,0:T(8,128)(2,1)} %broadcast_select_fusion.columns, f32[16,128,1152]{2,1,0:T(8,128)} %shard_map.41.terms), custom_call_target="tpu_custom_call" | custom-call | flops 415236096 | bytes 12000000 | tf_op jit(solution)/shard_map/pallas_call | solution.py:112
  57.0 1.3 fusion.7
  58.3 1.9 collective-permute-start.3
  60.2 12.4 %shard_map.42 = f32[12,128,1152]{2,1,0:T(8,128)} custom-call(s32[16]{0:T(128)} %stack.76.order, bf16[2048,352]{1,0:T(8,128)(2,1)} %broadcast_select_fusion.columns, f32[16,128,1152]{2,1,0:T(8,128)} %shard_map.41.terms), custom_call_target="tpu_custom_call" | custom-call | flops 1245708288 | bytes 12000000 | tf_op jit(solution)/shard_map/pallas_call | solution.py:112
  72.6 3.7 %convert.7 = bf16[12,128,1152]{2,1,0:T(8,128)(2,1)S(1)} convert(f32[12,128,1152]{2,1,0:T(8,128)} %shard_map.42) | non-fusion elementwise | flops 1769472 | bytes 10616832 | tf_op jit(solution)/shard_map/convert.2
  76.4 1.2 copy-done
  78.0 1.0 collective-permute-start.6
  79.1 0.9 collective-permute-start.4
  80.0 14.6 %collective-permute-done.6 = bf16[4,128,1152]{2,1,0:T(8,128)(2,1)S(1)} collective-permute-done((bf16[4,128,1152]{2,1,0:T(8,128)(2,1)S(1)}, bf16[4,128,1152]{2,1,0:T(8,128)(2,1)S(1)}, u32[]{:S(2)}, u32[]{:S(2)}) %collective-permute-start.6) | collective-permute-done | bytes 1179680 | tf_op jit(solution)/shard_map/ppermute | solution.py:49
  95.1 3.6 %collective-permute-start.7 = (bf16[2,128,1152]{2,1,0:T(8,128)(2,1)S(1)}, bf16[2,128,1152]{2,1,0:T(8,128)(2,1)S(1)}, u32[]{:S(2)}, u32[]{:S(2)}) collective-permute-start(bf16[2,128,1152]{2,1,0:T(8,128)(2,1)S(1)} %fusion.5), channel_id=1, source_target_pairs={{0,12},{1,13},{2,14},{3,15},{4,8},{5,9},{6,10},{7,11},{8,4},{9,5},... | collective-permute-start | bytes 1769480 | tf_op jit(solution)/shard_map/ppermute | solution.py:49
  98.6 7.6 %collective-permute-done.7 = bf16[2,128,1152]{2,1,0:T(8,128)(2,1)S(1)} collective-permute-done((bf16[2,128,1152]{2,1,0:T(8,128)(2,1)S(1)}, bf16[2,128,1152]{2,1,0:T(8,128)(2,1)S(1)}, u32[]{:S(2)}, u32[]{:S(2)}) %collective-permute-start.7) | collective-permute-done | bytes 589856 | tf_op jit(solution)/shard_map/ppermute | solution.py:49
  106.3 2.8 %collective-permute-start.8 = (bf16[2,128,1152]{2,1,0:T(8,128)(2,1)S(1)}, bf16[2,128,1152]{2,1,0:T(8,128)(2,1)S(1)}, u32[]{:S(2)}, u32[]{:S(2)}) collective-permute-start(bf16[2,128,1152]{2,1,0:T(8,128)(2,1)S(1)} %fusion.2), channel_id=1, source_target_pairs={{0,12},{1,13},{2,14},{3,15},{4,8},{5,9},{6,10},{7,11},{8,4},{9,5},... | collective-permute-start | bytes 1769480 | tf_op jit(solution)/shard_map/ppermute | solution.py:49
  109.1 7.6 %collective-permute-done.8 = bf16[2,128,1152]{2,1,0:T(8,128)(2,1)S(1)} collective-permute-done((bf16[2,128,1152]{2,1,0:T(8,128)(2,1)S(1)}, bf16[2,128,1152]{2,1,0:T(8,128)(2,1)S(1)}, u32[]{:S(2)}, u32[]{:S(2)}) %collective-permute-start.8) | collective-permute-done | bytes 589856 | tf_op jit(solution)/shard_map/ppermute | solution.py:49
  117.0 1.9 collective-permute-start.9
  118.9 13.3 %collective-permute-done.11.rest_2_ = bf16[4,128,1152]{2,1,0:T(8,128)(2,1)S(1)} collective-permute-done((bf16[4,128,1152]{2,1,0:T(8,128)(2,1)S(1)}, bf16[4,128,1152]{2,1,0:T(8,128)(2,1)S(1)}, u32[]{:S(2)}, u32[]{:S(2)}) %collective-permute-start.11) | collective-permute-done | bytes 1179680 | tf_op jit(solution)/shard_map/ppermute | solution.py:49
  132.3 2.0 collective-permute-start.12
  134.6 8.0 %collective-permute-done.12.rest_1_ = bf16[2,128,1152]{2,1,0:T(8,128)(2,1)S(1)} collective-permute-done((bf16[2,128,1152]{2,1,0:T(8,128)(2,1)S(1)}, bf16[2,128,1152]{2,1,0:T(8,128)(2,1)S(1)}, u32[]{:S(2)}, u32[]{:S(2)}) %collective-permute-start.12) | collective-permute-done | bytes 589856 | tf_op jit(solution)/shard_map/ppermute | solution.py:49
  142.6 1.0 collective-permute-done.10.rest_0_
  143.6 0.8 copy-done.7
  144.4 17.6 %shard_map.44 = bf16[2048,352]{1,0:T(8,128)(2,1)} custom-call(s32[16]{0:T(128)} %stack.76.order, bf16[2048,352]{1,0:T(8,128)(2,1)} %select_select_fusion.2.columns, bf16[2,128,1152]{2,1,0:T(8,128)(2,1)} %copy-done.7, bf16[2,128,1152]{2,1,0:T(8,128)(2,1)} %copy-done.6, bf16[4,128,1152]{2,1,0:T(8,128)(2,1)} %copy-done.4, bf16[4,128,1152]{2,1,0:T(8,128)(2,1)} %copy-done.5, ...), custom_call_target="tpu_custom_call" | custom-call | flops 5905580032 | bytes 8000000 | tf_op jit(solution)/shard_map/pallas_call | solution.py:168
  162.0 1.7 copy.27
  163.7 5.6 %collective-permute-start.13 = (bf16[2048,352]{0,1:T(8,128)(2,1)S(1)}, bf16[2048,352]{0,1:T(8,128)(2,1)S(1)}, u32[]{:S(2)}, u32[]{:S(2)}) collective-permute-start(bf16[2048,352]{0,1:T(8,128)(2,1)S(1)} %copy.27), channel_id=1, source_target_pairs={{0,16},{1,17},{2,18},{3,19},{4,20},{5,21},{6,22},{7,23},{8,24},{9,... | collective-permute-start | bytes 4325384 | tf_op jit(solution)/shard_map/ppermute | solution.py:49
  169.3 17.6 %shard_map.45 = bf16[2048,352]{1,0:T(8,128)(2,1)} custom-call(s32[16]{0:T(128)} %stack.76.order, bf16[2048,352]{1,0:T(8,128)(2,1)} %broadcast_select_fusion.columns, bf16[2,128,1152]{2,1,0:T(8,128)(2,1)} %copy-done.7, bf16[2,128,1152]{2,1,0:T(8,128)(2,1)} %copy-done.6, bf16[4,128,1152]{2,1,0:T(8,128)(2,1)} %copy-done.4, bf16[4,128,1152]{2,1,0:T(8,128)(2,1)} %copy-done.5, ...), custom_call_target="tpu_custom_call" | custom-call | flops 5905580032 | bytes 8000000 | tf_op jit(solution)/shard_map/pallas_call | solution.py:168
  186.9 2.5 %copy.29 = bf16[2048,352]{0,1:T(8,128)(2,1)} copy(bf16[2048,352]{1,0:T(8,128)(2,1)} %shard_map.45) | data formatting | bytes 2883584 | tf_op jit(solution)/shard_map/pallas_call | solution.py:168
  189.4 2.7 %collective-permute-start.15 = (bf16[2048,352]{0,1:T(8,128)(2,1)}, bf16[2048,352]{0,1:T(8,128)(2,1)}, u32[]{:S(2)}, u32[]{:S(2)}) collective-permute-start(bf16[2048,352]{0,1:T(8,128)(2,1)} %copy.29), channel_id=1, source_target_pairs={{16,1},{19,2},{20,5},{23,6},{24,9},{27,10},{28,13},{31,14},{17,16}... | collective-permute-start | bytes 4325384 | tf_op jit(solution)/shard_map/ppermute | solution.py:49
  192.2 1.3 collective-permute-start.14
  193.5 0.9 copy.28
  194.4 15.1 %collective-permute-done.15 = bf16[2048,352]{0,1:T(8,128)(2,1)} collective-permute-done((bf16[2048,352]{0,1:T(8,128)(2,1)}, bf16[2048,352]{0,1:T(8,128)(2,1)}, u32[]{:S(2)}, u32[]{:S(2)}) %collective-permute-start.15) | collective-permute-done | bytes 1441824 | tf_op jit(solution)/shard_map/ppermute | solution.py:49
  209.5 2.6 %copy.33 = bf16[2048,352]{1,0:T(8,128)(2,1)} copy(bf16[2048,352]{0,1:T(8,128)(2,1)} %collective-permute-done.15) | data formatting | bytes 2883584 | tf_op jit(solution)/shard_map/ppermute | solution.py:49
  212.1 0.7 collective-permute-done.14
  212.8 2.6 %copy.30 = bf16[2048,352]{1,0:T(8,128)(2,1)} copy(bf16[2048,352]{0,1:T(8,128)(2,1)} %collective-permute-done.14) | data formatting | bytes 2883584 | tf_op jit(solution)/shard_map/ppermute | solution.py:49
  215.4 3.9 %select_select_fusion = (bf16[2048,352]{1,0:T(8,128)(2,1)}, bf16[2048,352]{1,0:T(8,128)(2,1)}) fusion(bf16[2048,352]{1,0:T(8,128)(2,1)} %copy.33, bf16[2048,352]{1,0:T(8,128)(2,1)S(1)} %copy.28, bf16[2048,352]{1,0:T(8,128)(2,1)S(1)} %copy-done.1, pred[]{:T(512)S(6)} %eq.45, pred[]{:T(512)S(6)} %eq.37, bf16[2048,352]{1,0:T(8,128)(2,1)} %copy.30, pred[]{:T(512)S(6)} %eq.38), kind=kLoop, calls=%fused_computation.2 | loop fusion | flops 2883584 | bytes 8650755 | tf_op jit(solution)/shard_map/jit(_where)/select_n | solution.py:264
  219.3 2.7 %copy.35 = bf16[2048,352]{0,1:T(8,128)(2,1)} copy(bf16[2048,352]{1,0:T(8,128)(2,1)} %get-tuple-element.10) | data formatting | bytes 2883584
  222.0 1.6 copy.34
  (35 shorter events, 2.5 us)
Async XLA Ops:
  0.6 20.9 %collective-permute-start.1 = (bf16[2048,352]{0,1:T(8,128)(2,1)}, bf16[2048,352]{0,1:T(8,128)(2,1)}, u32[]{:S(2)}, u32[]{:S(2)}) collective-permute-start(bf16[2048,352]{0,1:T(8,128)(2,1)} %param.2), channel_id=1, source_target_pairs={{4,0},{5,1},{6,2},{7,3},{8,12},{9,13},{10,14},{11,15},{16,4},{17,5... | collective-permute-start | bytes 4325384 | tf_op jit(solution)/shard_map/ppermute | solution.py:49
  6.3 20.6 %collective-permute-start.2 = (bf16[2048,352]{0,1:T(8,128)(2,1)}, bf16[2048,352]{0,1:T(8,128)(2,1)}, u32[]{:S(2)}, u32[]{:S(2)}) collective-permute-start(bf16[2048,352]{0,1:T(8,128)(2,1)} %param.3), channel_id=1, source_target_pairs={{1,16},{2,19},{5,20},{6,23},{9,24},{10,27},{13,28},{14,31},{16,17}... | collective-permute-start | bytes 4325384 | tf_op jit(solution)/shard_map/ppermute | solution.py:49
  17.5 14.8 %collective-permute-start = (bf16[2048,352]{0,1:T(8,128)(2,1)}, bf16[2048,352]{0,1:T(8,128)(2,1)}, u32[]{:S(2)}, u32[]{:S(2)}) collective-permute-start(bf16[2048,352]{0,1:T(8,128)(2,1)} %copy.17), channel_id=1, source_target_pairs={{0,16},{1,17},{2,18},{3,19},{4,20},{5,21},{6,22},{7,23},{8,24},{9,... | collective-permute-start | bytes 4325384 | tf_op jit(solution)/shard_map/ppermute | solution.py:49
  58.3 18.0 %collective-permute-start.3 = (bf16[2,128,1152]{2,1,0:T(8,128)(2,1)S(1)}, bf16[2,128,1152]{2,1,0:T(8,128)(2,1)S(1)}, u32[]{:S(2)}, u32[]{:S(2)}) collective-permute-start(bf16[2,128,1152]{2,1,0:T(8,128)(2,1)S(1)} %get-tuple-element.12), channel_id=1, source_target_pairs={{0,3},{1,2},{2,1},{3,0},{4,7},{5,6},{6,5},{7,4},{8,11},{9,10},{10,... | collective-permute-start | bytes 1769480 | tf_op jit(solution)/shard_map/ppermute | solution.py:49
  60.2 16.2 %collective-permute-start.5 = (bf16[2,128,1152]{2,1,0:T(8,128)(2,1)S(1)}, bf16[2,128,1152]{2,1,0:T(8,128)(2,1)S(1)}, u32[]{:S(2)}, u32[]{:S(2)}) collective-permute-start(bf16[2,128,1152]{2,1,0:T(8,128)(2,1)S(1)} %get-tuple-element.13), channel_id=1, source_target_pairs={{0,1},{1,0},{2,3},{3,2},{4,5},{5,4},{6,7},{7,6},{8,9},{9,8},{10,11... | collective-permute-start | bytes 1769480 | tf_op jit(solution)/shard_map/ppermute | solution.py:49
  72.6 5.0 %copy-start = (f32[12,128,1152]{2,1,0:T(8,128)S(1)}, f32[12,128,1152]{2,1,0:T(8,128)}, u32[]{:S(2)}) copy-start(f32[12,128,1152]{2,1,0:T(8,128)} %shard_map.42) | copy-start | bytes 21233668
  78.0 16.6 %collective-permute-start.6 = (bf16[4,128,1152]{2,1,0:T(8,128)(2,1)S(1)}, bf16[4,128,1152]{2,1,0:T(8,128)(2,1)S(1)}, u32[]{:S(2)}, u32[]{:S(2)}) collective-permute-start(bf16[4,128,1152]{2,1,0:T(8,128)(2,1)S(1)} %pad_maximum_fusion.1), channel_id=1, source_target_pairs={{0,3},{1,2},{2,1},{3,0},{4,7},{5,6},{6,5},{7,4},{8,11},{9,10},{10,... | collective-permute-start | bytes 3538952 | tf_op jit(solution)/shard_map/ppermute | solution.py:49
  79.1 15.6 %collective-permute-start.4 = (bf16[4,128,1152]{2,1,0:T(8,128)(2,1)S(1)}, bf16[4,128,1152]{2,1,0:T(8,128)(2,1)S(1)}, u32[]{:S(2)}, u32[]{:S(2)}) collective-permute-start(bf16[4,128,1152]{2,1,0:T(8,128)(2,1)S(1)} %pad_maximum_fusion), channel_id=1, source_target_pairs={{0,1},{1,0},{2,3},{3,2},{4,5},{5,4},{6,7},{7,6},{8,9},{9,8},{10,11... | collective-permute-start | bytes 3538952 | tf_op jit(solution)/shard_map/ppermute | solution.py:49
  95.1 11.1 %collective-permute-start.7 = (bf16[2,128,1152]{2,1,0:T(8,128)(2,1)S(1)}, bf16[2,128,1152]{2,1,0:T(8,128)(2,1)S(1)}, u32[]{:S(2)}, u32[]{:S(2)}) collective-permute-start(bf16[2,128,1152]{2,1,0:T(8,128)(2,1)S(1)} %fusion.5), channel_id=1, source_target_pairs={{0,12},{1,13},{2,14},{3,15},{4,8},{5,9},{6,10},{7,11},{8,4},{9,5},... | collective-permute-start | bytes 1769480 | tf_op jit(solution)/shard_map/ppermute | solution.py:49
  106.3 10.3 %collective-permute-start.8 = (bf16[2,128,1152]{2,1,0:T(8,128)(2,1)S(1)}, bf16[2,128,1152]{2,1,0:T(8,128)(2,1)S(1)}, u32[]{:S(2)}, u32[]{:S(2)}) collective-permute-start(bf16[2,128,1152]{2,1,0:T(8,128)(2,1)S(1)} %fusion.2), channel_id=1, source_target_pairs={{0,12},{1,13},{2,14},{3,15},{4,8},{5,9},{6,10},{7,11},{8,4},{9,5},... | collective-permute-start | bytes 1769480 | tf_op jit(solution)/shard_map/ppermute | solution.py:49
  116.8 26.8 %copy-start.3 = (bf16[2,2,128,1152]{3,2,1,0:T(8,128)(2,1)}, bf16[2,2,128,1152]{3,2,1,0:T(8,128)(2,1)S(1)}, u32[]{:S(2)}) copy-start(bf16[2,2,128,1152]{3,2,1,0:T(8,128)(2,1)S(1)} %pad_maximum_fusion.2) | copy-start | bytes 3538948
  116.8 15.4 %collective-permute-start.11 = (bf16[4,128,1152]{2,1,0:T(8,128)(2,1)S(1)}, bf16[4,128,1152]{2,1,0:T(8,128)(2,1)S(1)}, u32[]{:S(2)}, u32[]{:S(2)}) collective-permute-start(bf16[4,128,1152]{2,1,0:T(8,128)(2,1)S(1)} %bitcast.33), channel_id=1, source_target_pairs={{0,1},{1,0},{2,3},{3,2},{4,5},{5,4},{6,7},{7,6},{8,9},{9,8},{10,11... | collective-permute-start | bytes 3538952 | tf_op jit(solution)/shard_map/ppermute | solution.py:49
  117.0 17.3 %collective-permute-start.9 = (bf16[4,128,1152]{2,1,0:T(8,128)(2,1)S(1)}, bf16[4,128,1152]{2,1,0:T(8,128)(2,1)S(1)}, u32[]{:S(2)}, u32[]{:S(2)}) collective-permute-start(bf16[4,128,1152]{2,1,0:T(8,128)(2,1)S(1)} %bitcast.34), channel_id=1, source_target_pairs={{0,3},{1,2},{2,1},{3,0},{4,7},{5,6},{6,5},{7,4},{8,11},{9,10},{10,... | collective-permute-start | bytes 3538952 | tf_op jit(solution)/shard_map/ppermute | solution.py:49
  132.2 11.4 %copy-start.4 = (bf16[4,128,1152]{2,1,0:T(8,128)(2,1)}, bf16[4,128,1152]{2,1,0:T(8,128)(2,1)S(1)}, u32[]{:S(2)}) copy-start(bf16[4,128,1152]{2,1,0:T(8,128)(2,1)S(1)} %collective-permute-done.11.rest_2_) | copy-start | bytes 3538948
  132.3 10.3 %collective-permute-start.12 = (bf16[2,128,1152]{2,1,0:T(8,128)(2,1)S(1)}, bf16[2,128,1152]{2,1,0:T(8,128)(2,1)S(1)}, u32[]{:S(2)}, u32[]{:S(2)}) collective-permute-start(bf16[2,128,1152]{2,1,0:T(8,128)(2,1)S(1)} %slice.57), channel_id=1, source_target_pairs={{0,3},{1,2},{2,1},{3,0},{4,7},{5,6},{6,5},{7,4},{8,11},{9,10},{10,... | collective-permute-start | bytes 1769480 | tf_op jit(solution)/shard_map/ppermute | solution.py:49
  134.2 9.3 %copy-start.5 = (bf16[4,128,1152]{2,1,0:T(8,128)(2,1)}, bf16[4,128,1152]{2,1,0:T(8,128)(2,1)S(1)}, u32[]{:S(2)}) copy-start(bf16[4,128,1152]{2,1,0:T(8,128)(2,1)S(1)} %collective-permute-done.9.rest_3_) | copy-start | bytes 3538948
  134.3 9.3 %collective-permute-start.10 = (bf16[2,128,1152]{2,1,0:T(8,128)(2,1)S(1)}, bf16[2,128,1152]{2,1,0:T(8,128)(2,1)S(1)}, u32[]{:S(2)}, u32[]{:S(2)}) collective-permute-start(bf16[2,128,1152]{2,1,0:T(8,128)(2,1)S(1)} %slice.56), channel_id=1, source_target_pairs={{0,1},{1,0},{2,3},{3,2},{4,5},{5,4},{6,7},{7,6},{8,9},{9,8},{10,11... | collective-permute-start | bytes 1769480 | tf_op jit(solution)/shard_map/ppermute | solution.py:49
  142.6 1.0 copy-start.6
  143.6 0.8 copy-start.7
  163.7 29.8 %collective-permute-start.13 = (bf16[2048,352]{0,1:T(8,128)(2,1)S(1)}, bf16[2048,352]{0,1:T(8,128)(2,1)S(1)}, u32[]{:S(2)}, u32[]{:S(2)}) collective-permute-start(bf16[2048,352]{0,1:T(8,128)(2,1)S(1)} %copy.27), channel_id=1, source_target_pairs={{0,16},{1,17},{2,18},{3,19},{4,20},{5,21},{6,22},{7,23},{8,24},{9,... | collective-permute-start | bytes 4325384 | tf_op jit(solution)/shard_map/ppermute | solution.py:49
  189.4 20.1 %collective-permute-start.15 = (bf16[2048,352]{0,1:T(8,128)(2,1)}, bf16[2048,352]{0,1:T(8,128)(2,1)}, u32[]{:S(2)}, u32[]{:S(2)}) collective-permute-start(bf16[2048,352]{0,1:T(8,128)(2,1)} %copy.29), channel_id=1, source_target_pairs={{16,1},{19,2},{20,5},{23,6},{24,9},{27,10},{28,13},{31,14},{17,16}... | collective-permute-start | bytes 4325384 | tf_op jit(solution)/shard_map/ppermute | solution.py:49
  192.2 20.6 %collective-permute-start.14 = (bf16[2048,352]{0,1:T(8,128)(2,1)}, bf16[2048,352]{0,1:T(8,128)(2,1)}, u32[]{:S(2)}, u32[]{:S(2)}) collective-permute-start(bf16[2048,352]{0,1:T(8,128)(2,1)} %copy.29), channel_id=1, source_target_pairs={{0,4},{1,5},{2,6},{3,7},{12,8},{13,9},{14,10},{15,11},{4,16},{5,17... | collective-permute-start | bytes 4325384 | tf_op jit(solution)/shard_map/ppermute | solution.py:49
  212.1 3.3 %copy-start.1 = (bf16[2048,352]{1,0:T(8,128)(2,1)S(1)}, bf16[2048,352]{1,0:T(8,128)(2,1)}, u32[]{:S(2)}) copy-start(bf16[2048,352]{1,0:T(8,128)(2,1)} %shard_map.44) | copy-start | bytes 4325380
  219.3 2.7 %copy-start.2 = (bf16[2048,352]{1,0:T(8,128)(2,1)S(1)}, bf16[2048,352]{1,0:T(8,128)(2,1)}, u32[]{:S(2)}) copy-start(bf16[2048,352]{1,0:T(8,128)(2,1)} %get-tuple-element.11) | copy-start | bytes 4325380

commit v2 on v1

v2 whole, which is shorter than its diff:
```python
import functools

import jax
import jax.numpy as jnp
from jax import lax
from jax.experimental import pallas as pl
from jax.experimental.pallas import tpu as pltpu
from jax.sharding import PartitionSpec as P

COEF_A = 3.4445
COEF_B = -4.775
COEF_C = 2.0315

AXES = ("section", "row", "col")
BLOCK = 128
PAIR = 2 * BLOCK
TILE = 512
VMEM_LIMIT = 28 * 1024 * 1024
ANY = pl.BlockSpec(memory_space=pl.ANY)
SMEM = pl.BlockSpec(memory_space=pltpu.SMEM)
VMEM = pl.BlockSpec(memory_space=pltpu.VMEM)


def device_pairs(route):
    pairs = []
    for x in range(4):
        for core in range(2):
            for y in range(4):
                for z in range(4):
                    target = route(core, y, z)
                    if target is not None:
                        to_core, to_y, to_z = target
                        pairs.append(
                            (((x * 2 + core) * 4 + y) * 4 + z, ((x * 2 + to_core) * 4 + to_y) * 4 + to_z)
                        )
    return pairs


def outer(i):
    return i in (0, 3)


GATE_OUT = device_pairs(lambda c, y, z: (0, y ^ 1, z) if c == (1 if outer(y) else 0) else None)
UP_OUT = device_pairs(lambda c, y, z: (1, y, z ^ 1) if c == (1 if outer(z) else 0) else None)
GATE_OVER = device_pairs(lambda c, y, z: (0, y, z) if c == 1 and not outer(y) else None)
UP_OVER = device_pairs(lambda c, y, z: (1, y, z) if c == 0 and outer(z) else None)


def reverse(pairs):
    return [(b, a) for a, b in pairs]


HOP_1 = device_pairs(lambda c, y, z: (c, y, z ^ 1) if c == 0 else (c, y ^ 1, z))
HOP_2 = device_pairs(lambda c, y, z: (c, y, 3 - z) if c == 0 else (c, 3 - y, z))
HOP_3 = device_pairs(lambda c, y, z: (c, 3 - y, z) if c == 0 else (c, y, 3 - z))


def send(values, pairs):
    return lax.ppermute(values, AXES, pairs)


def params():
    return pltpu.CompilerParams(vmem_limit_bytes=VMEM_LIMIT)


def fetch_wide(choice, sources, wide, sems):
    rows = sources[0].shape[1]
    for k, source in enumerate(sources):

        @pl.when(choice == k)
        def _(source=source):
            whole = pltpu.make_async_copy(source, wide.at[:, 0:rows], sems.at[0])
            head = pltpu.make_async_copy(
                source.at[:, 0 : rows // 2], wide.at[:, rows : rows + rows // 2], sems.at[1]
            )
            whole.start()
            head.start()
            whole.wait()
            head.wait()


def block_pair(wide, index, span):
    first = pl.multiple_of(index * PAIR, PAIR)
    value = lax.dot_general(
        wide[:, pl.ds(first, PAIR)],
        wide[:, pl.ds(first, span + BLOCK)],
        (((0,), (0,)), ((), ())),
        preferred_element_type=jnp.float32,
    )
    return value[0:BLOCK, 0:span], value[BLOCK:PAIR, BLOCK : span + BLOCK]


def own_terms_kernel(scale, order, choice, *rest):
    sources, (corner, others, wide, sems) = rest[:-4], rest[-4:]
    fetch_wide(choice[0], sources, wide, sems)
    span = corner.shape[2]
    for out, start, pairs in ((corner, 0, 2), (others, 2, 6)):

        def one(g, carry, out=out, start=start):
            upper, lower = block_pair(wide, order[start + g], span)
            out[2 * g] = (upper * scale).astype(out.dtype)
            out[2 * g + 1] = (lower * scale).astype(out.dtype)
            return carry

        lax.fori_loop(0, pairs, one, 0)


def own_terms(order, choice, sources, scale):
    dev_cols, rows = sources[0].shape
    span = rows // 2 + BLOCK
    return pl.pallas_call(
        functools.partial(own_terms_kernel, scale),
        out_shape=[jax.ShapeDtypeStruct((n, BLOCK, span), jnp.bfloat16) for n in (4, 12)],
        in_specs=[SMEM, SMEM] + [ANY] * len(sources),
        out_specs=[VMEM, VMEM],
        scratch_shapes=[
            pltpu.VMEM((dev_cols, rows + rows // 2), jnp.bfloat16),
            pltpu.SemaphoreType.DMA((2,)),
        ],
        compiler_params=params(),
        cost_estimate=pl.CostEstimate(
            flops=2 * rows * span * dev_cols, bytes_accessed=20000000, transcendentals=0
        ),
    )(order, choice, *sources)


def add_terms_kernel(scale, start, order, choice, *rest):
    sources, terms, outs, (wide, sems) = rest[:2], rest[2], rest[3:-2], rest[-2:]
    fetch_wide(choice[1], sources, wide, sems)
    span = terms.shape[2]
    done = 0
    for out in outs:

        def one(g, carry, out=out, done=done):
            upper, lower = block_pair(wide, order[start + done + g], span)
            at = 2 * (done + g)
            out[2 * g] = (upper * scale + terms[at].astype(jnp.float32)).astype(out.dtype)
            out[2 * g + 1] = (lower * scale + terms[at + 1].astype(jnp.float32)).astype(out.dtype)
            return carry

        lax.fori_loop(0, out.shape[0] // 2, one, 0)
        done += out.shape[0] // 2


def add_terms(order, choice, sources, terms, start, counts, scale):
    dev_cols, rows = sources[0].shape
    span = rows // 2 + BLOCK
    return pl.pallas_call(
        functools.partial(add_terms_kernel, scale, start),
        out_shape=[jax.ShapeDtypeStruct((n, BLOCK, span), jnp.bfloat16) for n in counts],
        in_specs=[SMEM, SMEM] + [ANY] * len(sources) + [VMEM],
        out_specs=[VMEM] * len(counts),
        scratch_shapes=[
            pltpu.VMEM((dev_cols, rows + rows // 2), jnp.bfloat16),
            pltpu.SemaphoreType.DMA((2,)),
        ],
        compiler_params=params(),
        cost_estimate=pl.CostEstimate(
            flops=2 * sum(counts) * BLOCK * span * dev_cols, bytes_accessed=10000000, transcendentals=0
        ),
    )(order, choice, *sources, terms)


def unpack_kernel(start, order, *rest):
    pieces, gram = rest[:-1], rest[-1]
    count = gram.shape[0] // BLOCK
    place = start
    for piece in pieces:
        span = piece.shape[2]
        for k in range(piece.shape[0]):
            index = 2 * order[place // 2] + place % 2
            place += 1
            top = pl.multiple_of(index * BLOCK, BLOCK)
            for shift in range(span // BLOCK):
                left = pl.multiple_of(((index + shift) % count) * BLOCK, BLOCK)
                block = piece[k, :, shift * BLOCK : (shift + 1) * BLOCK]
                gram[pl.ds(top, BLOCK), pl.ds(left, BLOCK)] = block
                if 0 < shift < span // BLOCK - 1:
                    gram[pl.ds(left, BLOCK), pl.ds(top, BLOCK)] = block.T


def unpack(order, pieces, start, rows):
    return pl.pallas_call(
        functools.partial(unpack_kernel, start),
        out_shape=jax.ShapeDtypeStruct((rows, rows), jnp.bfloat16),
        in_specs=[SMEM] + [VMEM] * len(pieces),
        out_specs=VMEM,
        compiler_params=params(),
        cost_estimate=pl.CostEstimate(flops=0, bytes_accessed=20000000, transcendentals=0),
    )(order, *pieces)


def step_kernel(which, order, choice, *rest):
    sources, (gram_in, last_a, last_b, result, gram, columns, low, linear, sems) = rest[:-9], rest[-9:]
    rows = gram.shape[0]
    load = pltpu.make_async_copy(gram_in, gram, sems.at[0])
    load.start()
    for k, source in enumerate(sources):

        @pl.when(choice[which] == k)
        def _(source=source):
            fetch = pltpu.make_async_copy(source, columns, sems.at[1])
            fetch.start()
            fetch.wait()

    load.wait()
    unpack_kernel(0, order, last_a, last_b, gram)

    def multiply(t, carry):
        at = pl.ds(pl.multiple_of(t * TILE, TILE), TILE)
        value = jnp.dot(columns[...], gram[:, at], preferred_element_type=jnp.float32)
        low[:, at] = value.astype(jnp.bfloat16)
        linear[:, at] = COEF_A * columns[:, at].astype(jnp.float32) + COEF_B * value
        return carry

    lax.fori_loop(0, rows // TILE, multiply, 0)

    def again(t, carry):
        at = pl.ds(pl.multiple_of(t * TILE, TILE), TILE)
        value = jnp.dot(low[...], gram[:, at], preferred_element_type=jnp.float32)
        result[:, at] = (linear[:, at] + COEF_C * value).astype(jnp.bfloat16)
        return carry

    lax.fori_loop(0, rows // TILE, again, 0)


def newton_step(which, order, choice, sources, gram, last_a, last_b):
    dev_cols, rows = sources[0].shape
    return pl.pallas_call(
        functools.partial(step_kernel, which),
        out_shape=jax.ShapeDtypeStruct((dev_cols, rows), jnp.bfloat16),
        in_specs=[SMEM, SMEM] + [ANY] * (len(sources) + 1) + [VMEM, VMEM],
        out_specs=VMEM,
        scratch_shapes=[
            pltpu.VMEM((rows, rows), jnp.bfloat16),
            pltpu.VMEM((dev_cols, rows), jnp.bfloat16),
            pltpu.VMEM((dev_cols, rows), jnp.bfloat16),
            pltpu.VMEM((dev_cols, rows), jnp.float32),
            pltpu.SemaphoreType.DMA((2,)),
        ],
        compiler_params=params(),
        cost_estimate=pl.CostEstimate(
            flops=4 * rows * rows * dev_cols, bytes_accessed=12000000, transcendentals=0
        ),
    )(order, choice, *sources, gram, last_a, last_b)


def add(*terms):
    return sum(t.astype(jnp.float32) for t in terms).astype(jnp.bfloat16)


def per_device(gate_grad, up_grad):
    rows, dev_cols = gate_grad.shape
    scale = 1.0 / (dev_cols * lax.axis_size(("row", "col")))
    gate, up = gate_grad.T, up_grad.T
    on_up = lax.axis_index("section") % 2
    y = lax.axis_index("row")
    z = lax.axis_index("col")
    y_low, y_high = ((y == 1) | (y == 2)).astype(jnp.int32), (y >= 2).astype(jnp.int32)
    z_low, z_high = ((z == 1) | (z == 2)).astype(jnp.int32), (z >= 2).astype(jnp.int32)
    on_gate = on_up == 0
    p = jnp.where(on_gate, z_low, y_low)
    q = jnp.where(on_gate, z_high, y_high)
    gate_part, up_part = y_low, z_low
    order = jnp.stack(
        [
            4 * stream + 2 * (p ^ dp) + (q ^ dq)
            for dp, dq in ((1, 1), (1, 0), (0, 1), (0, 0))
            for stream in (0, 1)
        ]
    )
    own_choice = jnp.where(on_gate, 2 * gate_part, 1 + 2 * (1 - up_part))
    choice = jnp.stack([own_choice, on_up])

    gate_over = send(gate, GATE_OVER)
    up_over = send(up, UP_OVER)
    gate_in = send(gate, GATE_OUT)
    up_in = send(up, UP_OUT)
    own = (gate, up, gate_over, up_over)
    partner = (gate_in, up_in)
    corner_terms, other_terms = own_terms(order, choice, own, scale)

    (corner,) = add_terms(order, choice, partner, corner_terms, 0, (4,), scale)
    got_a = send(corner[0:2], HOP_1)
    got_b = send(corner[2:4], HOP_2)
    side_1, side_2, mine = add_terms(order, choice, partner, other_terms, 2, (4, 4, 4), scale)
    got_1 = send(side_1.at[2:4].set(add(side_1[2:4], got_b)), HOP_1)
    got_2 = send(side_2.at[0:2].set(add(side_2[0:2], got_a)), HOP_2)
    mine = add(mine, got_1, got_2)
    total = add(mine, send(mine, HOP_3))

    all_1 = send(total, HOP_1)
    all_2 = send(total, HOP_2)
    last_a = send(all_2[0:2], HOP_1)
    last_b = send(all_1[2:4], HOP_2)
    gram = unpack(order, (all_1, all_2, total), 4, rows)

    partner_next = newton_step(1, order, choice, partner, gram, last_a, last_b)
    gate_back = send(partner_next, reverse(GATE_OUT))
    up_back = send(partner_next, reverse(UP_OUT))
    last_a, partner_next = lax.optimization_barrier((last_a, partner_next))
    own_next = newton_step(0, order, choice, own, gram, last_a, last_b)
    over_back = send(own_next, reverse(GATE_OVER) + reverse(UP_OVER))

    gate_next = jnp.where(gate_part == on_up, own_next, gate_back)
    up_next = jnp.where(up_part == on_up, own_next, up_back)
    gate_next, up_next = lax.optimization_barrier((gate_next, up_next))
    gate_next = jnp.where((gate_part == on_up) & (on_up == 1), over_back, gate_next)
    up_next = jnp.where((up_part == on_up) & on_gate, over_back, up_next)
    return gate_next.T, up_next.T


def solution(mesh):
    placed = (P("section", ("row", "col")), P("section", ("row", "col")))
    return jax.shard_map(
        per_device,
        mesh=mesh,
        in_specs=placed,
        out_specs=placed,
        check_vma=False,
    )
```

time: 224 us -> 147 us (0.66)
  Pallas kernels: 66.8 us -> 35.7 us
  local copies, waits for them, and re-layouts: 32.7 us -> 3.01 us
  other arithmetic: 15.6 us -> 6.15 us
  waiting for transfers between devices: 74.2 us -> 67.7 us
    pallas_call x5 -> x6, Pallas kernels: 66.8 us -> 35.7 us  [the longest x2 21.1 us: newton_step(): pl.pallas_call(functools.partial(step_kernel, which), out_shape=jax.Shape...]
    ppermute x6 -> x0, local copies, waits for them, and re-layouts: 13.8 us -> none  [send(): return lax.ppermute(values, AXES, pairs)]
    select_n x4 -> x1, other arithmetic: 10.9 us -> 1.6 us  [per_device(): up_next = jnp.where(up_part == on_up, own_next, up_back)]
    unnamed x20 -> x8, local copies, waits for them, and re-layouts: 9.99 us -> 2.74 us
    ppermute x16, waiting for transfers between devices: 74.2 us -> 67.7 us  [send(): return lax.ppermute(values, AXES, pairs)]
    pallas_call x2 -> x0, local copies, waits for them, and re-layouts: 4.23 us -> none  [newton_step(): pl.pallas_call(step_kernel, out_shape=jax.ShapeDtypeStruct(columns.shape,...]
    another operation x2 -> x1, other arithmetic: 3.79 us -> 0.07 us  [per_device(): choice = jnp.stack([own_choice, on_up])]
    transpose x0 -> x1, other arithmetic: none -> 3.18 us  [per_device(): return (gate_next.T, up_next.T)]
  transfers between devices with their start and end apart: 16 -> 16, of which waited for: 10 -> 13; matrix products, arithmetic and copies ran while one was open for 12% -> 2% of each run, Pallas kernels for 13% -> 16%
where the time goes in v2:
time: 147 us
  waiting for transfers between devices  67.7 us (46%)
  Pallas kernels  35.7 us (24%)
  starting transfers between devices  33.1 us (23%)
  other arithmetic  6.15 us (4%)
  local copies, waits for them, and re-layouts  3.01 us (2%)
    ppermute x16, waiting for transfers between devices, send(): return lax.ppermute(values, AXES, pairs)  67.7 us
    ppermute x16, starting transfers between devices, send(): return lax.ppermute(values, AXES, pairs)  33.1 us
    pallas_call x2, Pallas kernels, newton_step(): pl.pallas_call(functools.partial(step_kernel, which), out_shape=jax.Shape...  21.1 us
    pallas_call x1, Pallas kernels, own_terms(): pl.pallas_call(functools.partial(own_terms_kernel, scale), out_shape=[jax...  6.5 us
    pallas_call x2, Pallas kernels, add_terms(): pl.pallas_call(functools.partial(add_terms_kernel, scale, start), out_sha...  5.94 us
    transpose x1, other arithmetic, per_device(): return (gate_next.T, up_next.T)  3.18 us
  transfers between devices with their start and end apart: 16, of which 13 were waited for; matrix products, arithmetic and copies ran while one was open for 2% of the time, Pallas kernels for 16%

profile of v2, /device:TPU:1, one launch (start us, length us, event | category | flops | bytes accessed | tf_op | source)
XLA Modules:
  0.0 146.7 jit_solution(13758750928648139366)
XLA Ops:
  0.6 1.8 %collective-permute-start = (bf16[352,2048]{1,0:T(8,128)(2,1)}, bf16[352,2048]{1,0:T(8,128)(2,1)}, u32[]{:S(2)}, u32[]{:S(2)}) collective-permute-start(bf16[352,2048]{1,0:T(8,128)(2,1)} %bitcast.16), channel_id=1, source_target_pairs={{20,4},{21,5},{22,6},{23,7},{24,8},{25,9},{26,10},{27,11},{52,36},... | collective-permute-start | bytes 4325384 | tf_op jit(solution)/shard_map/ppermute | solution.py:59
  2.4 1.3 collective-permute-start.1
  3.7 8.2 %collective-permute-start.2 = (bf16[352,2048]{1,0:T(8,128)(2,1)}, bf16[352,2048]{1,0:T(8,128)(2,1)S(1)}, u32[]{:S(2)}, u32[]{:S(2)}) collective-permute-start(bf16[352,2048]{1,0:T(8,128)(2,1)} %bitcast.17), channel_id=1, source_target_pairs={{4,0},{5,1},{6,2},{7,3},{8,12},{9,13},{10,14},{11,15},{16,4},{17,5... | collective-permute-start | bytes 4325384 | tf_op jit(solution)/shard_map/ppermute | solution.py:59
  11.9 1.9 %collective-permute-start.3 = (bf16[352,2048]{1,0:T(8,128)(2,1)}, bf16[352,2048]{1,0:T(8,128)(2,1)S(1)}, u32[]{:S(2)}, u32[]{:S(2)}) collective-permute-start(bf16[352,2048]{1,0:T(8,128)(2,1)} %bitcast.21), channel_id=1, source_target_pairs={{1,16},{2,19},{5,20},{6,23},{9,24},{10,27},{13,28},{14,31},{16,17}... | collective-permute-start | bytes 4325384 | tf_op jit(solution)/shard_map/ppermute | solution.py:59
  13.9 0.1 stack.44.order
  14.0 0.1 pad_add_fusion.choice
  14.0 0.0 collective-permute-done.rest_2_
  14.0 1.4 copy-done
  15.4 1.4 copy-done.2
  16.8 6.5 %shard_map.41 = (bf16[4,128,1152]{2,1,0:T(8,128)(2,1)S(1)}, bf16[12,128,1152]{2,1,0:T(8,128)(2,1)S(1)}) custom-call(s32[8]{0:T(128)S(1)} %stack.44.order, s32[2]{0:T(128)S(1)} %pad_add_fusion.choice, bf16[352,2048]{1,0:T(8,128)(2,1)S(1)} %bitcast.18, bf16[352,2048]{1,0:T(8,128)(2,1)S(1)} %bitcast.22, bf16[352,2048]{1,0:T(8,128)(2,1)} %collective-permute-done.rest_2_, ...), custom_call_target="tpu_custom_call" | custom-call | flops 1660944384 | bytes 20000000 | tf_op jit(solution)/shard_map/pallas_call | solution.py:111
  23.3 4.8 %collective-permute-done.2.rest_0_ = bf16[352,2048]{1,0:T(8,128)(2,1)S(1)} collective-permute-done((bf16[352,2048]{1,0:T(8,128)(2,1)}, bf16[352,2048]{1,0:T(8,128)(2,1)S(1)}, u32[]{:S(2)}, u32[]{:S(2)}) %collective-permute-start.2) | collective-permute-done | bytes 1441824 | tf_op jit(solution)/shard_map/ppermute | solution.py:59
  28.0 4.4 %collective-permute-done.3.rest_1_ = bf16[352,2048]{1,0:T(8,128)(2,1)S(1)} collective-permute-done((bf16[352,2048]{1,0:T(8,128)(2,1)}, bf16[352,2048]{1,0:T(8,128)(2,1)S(1)}, u32[]{:S(2)}, u32[]{:S(2)}) %collective-permute-start.3) | collective-permute-done | bytes 1441824 | tf_op jit(solution)/shard_map/ppermute | solution.py:59
  32.4 1.9 %shard_map.43 = bf16[4,128,1152]{2,1,0:T(8,128)(2,1)S(1)} custom-call(s32[8]{0:T(128)S(1)} %stack.44.order, s32[2]{0:T(128)S(1)} %pad_add_fusion.choice, bf16[352,2048]{1,0:T(8,128)(2,1)S(1)} %collective-permute-done.2.rest_0_, bf16[352,2048]{1,0:T(8,128)(2,1)S(1)} %collective-permute-done.3.rest_1_, bf16[4,128,1152]{2,1,0:T(8,128)(2,1)S(1)} %get-tuple-element.37.rest_2_), custom_call_target="tpu_custom_call" | custom-call | flops 415236096 | bytes 10000000 | tf_op jit(solution)/shard_map/pallas_call | solution.py:148
  34.3 0.1 fusion.2
  34.4 2.0 %collective-permute-start.4 = (bf16[2,128,1152]{2,1,0:T(8,128)(2,1)S(1)}, bf16[2,128,1152]{2,1,0:T(8,128)(2,1)S(1)}, u32[]{:S(2)}, u32[]{:S(2)}) collective-permute-start(bf16[2,128,1152]{2,1,0:T(8,128)(2,1)S(1)} %get-tuple-element.46), channel_id=1, source_target_pairs={{0,3},{1,2},{2,1},{3,0},{4,7},{5,6},{6,5},{7,4},{8,11},{9,10},{10,... | collective-permute-start | bytes 1769480 | tf_op jit(solution)/shard_map/ppermute | solution.py:59
  36.4 4.1 %shard_map.42 = (bf16[4,128,1152]{2,1,0:T(8,128)(2,1)S(1)}, bf16[4,128,1152]{2,1,0:T(8,128)(2,1)S(1)}, bf16[4,128,1152]{2,1,0:T(8,128)(2,1)S(1)}) custom-call(s32[8]{0:T(128)S(1)} %stack.44.order, s32[2]{0:T(128)S(1)} %pad_add_fusion.choice, bf16[352,2048]{1,0:T(8,128)(2,1)S(1)} %collective-permute-done.2.rest_0_, ...), custom_call_target="tpu_custom_call" | custom-call | flops 1245708288 | bytes 10000000 | tf_op jit(solution)/shard_map/pallas_call | solution.py:148
  40.5 4.0 %collective-permute-done.4 = bf16[2,128,1152]{2,1,0:T(8,128)(2,1)S(1)} collective-permute-done((bf16[2,128,1152]{2,1,0:T(8,128)(2,1)S(1)}, bf16[2,128,1152]{2,1,0:T(8,128)(2,1)S(1)}, u32[]{:S(2)}, u32[]{:S(2)}) %collective-permute-start.4) | collective-permute-done | bytes 589856 | tf_op jit(solution)/shard_map/ppermute | solution.py:59
  44.4 0.3 fusion
  44.7 0.1 collective-permute-start.5
  44.8 0.6 collective-permute-done.6
  45.4 0.3 fusion.1
  45.7 1.4 collective-permute-start.7
  47.1 13.1 %collective-permute-done.5 = bf16[4,128,1152]{2,1,0:T(8,128)(2,1)S(1)} collective-permute-done((bf16[4,128,1152]{2,1,0:T(8,128)(2,1)S(1)}, bf16[4,128,1152]{2,1,0:T(8,128)(2,1)S(1)}, u32[]{:S(2)}, u32[]{:S(2)}) %collective-permute-start.5) | collective-permute-done | bytes 1179680 | tf_op jit(solution)/shard_map/ppermute | solution.py:59
  60.1 2.2 %collective-permute-done.7 = bf16[4,128,1152]{2,1,0:T(8,128)(2,1)S(1)} collective-permute-done((bf16[4,128,1152]{2,1,0:T(8,128)(2,1)S(1)}, bf16[4,128,1152]{2,1,0:T(8,128)(2,1)S(1)}, u32[]{:S(2)}, u32[]{:S(2)}) %collective-permute-start.7) | collective-permute-done | bytes 1179680 | tf_op jit(solution)/shard_map/ppermute | solution.py:59
  62.3 0.5 add_convert_fusion.1
  62.8 3.5 %collective-permute-start.8 = (bf16[4,128,1152]{2,1,0:T(8,128)(2,1)S(1)}, bf16[4,128,1152]{2,1,0:T(8,128)(2,1)S(1)}, u32[]{:S(2)}, u32[]{:S(2)}) collective-permute-start(bf16[4,128,1152]{2,1,0:T(8,128)(2,1)S(1)} %add_convert_fusion.1), channel_id=1, source_target_pairs={{0,12},{1,13},{2,14},{3,15},{4,8},{5,9},{6,10},{7,11},{8,4},{9,5},... | collective-permute-start | bytes 3538952 | tf_op jit(solution)/shard_map/ppermute | solution.py:59
  66.3 13.9 %collective-permute-done.8 = bf16[4,128,1152]{2,1,0:T(8,128)(2,1)S(1)} collective-permute-done((bf16[4,128,1152]{2,1,0:T(8,128)(2,1)S(1)}, bf16[4,128,1152]{2,1,0:T(8,128)(2,1)S(1)}, u32[]{:S(2)}, u32[]{:S(2)}) %collective-permute-start.8) | collective-permute-done | bytes 1179680 | tf_op jit(solution)/shard_map/ppermute | solution.py:59
  80.2 0.3 add_convert_fusion.rest_2_
  80.5 1.7 %collective-permute-start.10 = (bf16[4,128,1152]{2,1,0:T(8,128)(2,1)S(1)}, bf16[4,128,1152]{2,1,0:T(8,128)(2,1)S(1)}, u32[]{:S(2)}, u32[]{:S(2)}) collective-permute-start(bf16[4,128,1152]{2,1,0:T(8,128)(2,1)S(1)} %add_convert_fusion.rest_2_), channel_id=1, source_target_pairs={{0,3},{1,2},{2,1},{3,0},{4,7},{5,6},{6,5},{7,4},{8,11},{9,10},{10,... | collective-permute-start | bytes 3538952 | tf_op jit(solution)/shard_map/ppermute | solution.py:59
  82.2 0.0 collective-permute-start.9
  82.2 15.0 %collective-permute-done.10.rest_1_ = bf16[4,128,1152]{2,1,0:T(8,128)(2,1)S(1)} collective-permute-done((bf16[4,128,1152]{2,1,0:T(8,128)(2,1)S(1)}, bf16[4,128,1152]{2,1,0:T(8,128)(2,1)S(1)}, u32[]{:S(2)}, u32[]{:S(2)}) %collective-permute-start.10) | collective-permute-done | bytes 1179680 | tf_op jit(solution)/shard_map/ppermute | solution.py:59
  97.2 0.1 collective-permute-start.11
  97.3 0.2 collective-permute-done.9.rest_0_
  97.6 1.4 collective-permute-start.12
  99.0 2.2 %shard_map.44.rest_2_.rest_4_ = bf16[2048,2048]{1,0:T(8,128)(2,1)S(1)} custom-call(s32[8]{0:T(128)S(1)} %stack.44.order, bf16[4,128,1152]{2,1,0:T(8,128)(2,1)S(1)} %collective-permute-done.9.rest_0_, bf16[4,128,1152]{2,1,0:T(8,128)(2,1)S(1)} %collective-permute-done.10.rest_1_, bf16[4,128,1152]{2,1,0:T(8,128)(2,1)S(1)} %add_convert_fusion.rest_2_), custom_call_target="tpu_custom_call" | custom-call | bytes 20000000 | tf_op jit(solution)/shard_map/pallas_call | solution.py:183
  101.3 0.0 copy-start.1
  101.3 0.0 copy-start.3
  101.3 5.0 %collective-permute-done.11.rest_3_.rest_5_ = bf16[2,128,1152]{2,1,0:T(8,128)(2,1)S(1)} collective-permute-done((bf16[2,128,1152]{2,1,0:T(8,128)(2,1)S(1)}, bf16[2,128,1152]{2,1,0:T(8,128)(2,1)S(1)}, u32[]{:S(2)}, u32[]{:S(2)}) %collective-permute-start.11) | collective-permute-done | bytes 589856 | tf_op jit(solution)/shard_map/ppermute | solution.py:59
  106.3 1.6 %collective-permute-done.12.rest_4_.rest_6_ = bf16[2,128,1152]{2,1,0:T(8,128)(2,1)S(1)} collective-permute-done((bf16[2,128,1152]{2,1,0:T(8,128)(2,1)S(1)}, bf16[2,128,1152]{2,1,0:T(8,128)(2,1)S(1)}, u32[]{:S(2)}, u32[]{:S(2)}) %collective-permute-start.12) | collective-permute-done | bytes 589856 | tf_op jit(solution)/shard_map/ppermute | solution.py:59
  107.9 10.5 %shard_map.45 = bf16[352,2048]{1,0:T(8,128)(2,1)} custom-call(s32[8]{0:T(128)S(1)} %stack.44.order, s32[2]{0:T(128)S(1)} %pad_add_fusion.choice, bf16[352,2048]{1,0:T(8,128)(2,1)S(1)} %collective-permute-done.2.rest_0_, bf16[352,2048]{1,0:T(8,128)(2,1)S(1)} %collective-permute-done.3.rest_1_, bf16[2048,2048]{1,0:T(8,128)(2,1)S(1)} %shard_map.44.rest_2_.rest_4_, ...), custom_call_target="tpu_custom_call" | custom-call | flops 5905580032 | bytes 12000000 | tf_op jit(solution)/shard_map/pallas_call | solution.py:229
  118.5 1.3 collective-permute-start.14
  119.8 5.9 %collective-permute-start.15 = (bf16[352,2048]{1,0:T(8,128)(2,1)}, bf16[352,2048]{1,0:T(8,128)(2,1)}, u32[]{:S(2)}, u32[]{:S(2)}) collective-permute-start(bf16[352,2048]{1,0:T(8,128)(2,1)} %shard_map.45), channel_id=1, source_target_pairs={{16,1},{19,2},{20,5},{23,6},{24,9},{27,10},{28,13},{31,14},{17,16}... | collective-permute-start | bytes 4325384 | tf_op jit(solution)/shard_map/ppermute | solution.py:59
  125.6 10.6 %shard_map.46 = bf16[352,2048]{1,0:T(8,128)(2,1)S(1)} custom-call(s32[8]{0:T(128)S(1)} %stack.44.order, s32[2]{0:T(128)S(1)} %pad_add_fusion.choice, bf16[352,2048]{1,0:T(8,128)(2,1)S(1)} %bitcast.19, bf16[352,2048]{1,0:T(8,128)(2,1)S(1)} %bitcast.23, bf16[352,2048]{1,0:T(8,128)(2,1)} %collective-permute-done.rest_2_, ...), custom_call_target="tpu_custom_call" | custom-call | flops 5905580032 | bytes 12000000 | tf_op jit(solution)/shard_map/pallas_call | solution.py:229
  136.2 2.6 %collective-permute-start.13 = (bf16[352,2048]{1,0:T(8,128)(2,1)S(1)}, bf16[352,2048]{1,0:T(8,128)(2,1)}, u32[]{:S(2)}, u32[]{:S(2)}) collective-permute-start(bf16[352,2048]{1,0:T(8,128)(2,1)S(1)} %shard_map.46), channel_id=1, source_target_pairs={{4,20},{5,21},{6,22},{7,23},{8,24},{9,25},{10,26},{11,27},{36,52},... | collective-permute-start | bytes 4325384 | tf_op jit(solution)/shard_map/ppermute | solution.py:59
  138.8 0.8 collective-permute-done.14
  139.7 2.2 %collective-permute-done.15 = bf16[352,2048]{1,0:T(8,128)(2,1)} collective-permute-done((bf16[352,2048]{1,0:T(8,128)(2,1)}, bf16[352,2048]{1,0:T(8,128)(2,1)}, u32[]{:S(2)}, u32[]{:S(2)}) %collective-permute-start.15) | collective-permute-done | bytes 1441824 | tf_op jit(solution)/shard_map/ppermute | solution.py:59
  141.9 1.6 %broadcast_select_fusion = (bf16[352,2048]{1,0:T(8,128)(2,1)S(1)}, bf16[352,2048]{1,0:T(8,128)(2,1)S(1)}) fusion(bf16[352,2048]{1,0:T(8,128)(2,1)S(1)} %shard_map.46, bf16[352,2048]{1,0:T(8,128)(2,1)} %collective-permute-done.15, pred[]{:T(512)S(6)} %eq.35, bf16[352,2048]{1,0:T(8,128)(2,1)S(1)} %collective-permute-done.14, pred[]{:T(512)S(6)} %eq.30), kind=kLoop, calls=%fused_computation.4 | loop fusion | flops 1441792 | bytes 7208962 | tf_op jit(solution)/shard_map/jit(_where)/select_n | solution.py:306
  143.5 3.2 %select_bitcast_fusion = (bf16[2048,352]{0,1:T(8,128)(2,1)}, bf16[2048,352]{0,1:T(8,128)(2,1)}) fusion(bf16[352,2048]{1,0:T(8,128)(2,1)} %collective-permute-done.13, bf16[352,2048]{1,0:T(8,128)(2,1)S(1)} %get-tuple-element.41, pred[]{:T(512)S(6)} %and.22, bf16[352,2048]{1,0:T(8,128)(2,1)S(1)} %get-tuple-element.40, pred[]{:T(512)S(6)} %and.21), kind=kLoop, calls=%fused_computation.2 | loop fusion | flops 1441792 | bytes 7208962 | tf_op jit(solution)/shard_map/transpose | solution.py:310
  (9 shorter events, 0.1 us)
Async XLA Ops:
  0.6 13.4 %collective-permute-start = (bf16[352,2048]{1,0:T(8,128)(2,1)}, bf16[352,2048]{1,0:T(8,128)(2,1)}, u32[]{:S(2)}, u32[]{:S(2)}) collective-permute-start(bf16[352,2048]{1,0:T(8,128)(2,1)} %bitcast.16), channel_id=1, source_target_pairs={{20,4},{21,5},{22,6},{23,7},{24,8},{25,9},{26,10},{27,11},{52,36},... | collective-permute-start | bytes 4325384 | tf_op jit(solution)/shard_map/ppermute | solution.py:59
  2.4 11.6 %collective-permute-start.1 = (bf16[352,2048]{1,0:T(8,128)(2,1)}, bf16[352,2048]{1,0:T(8,128)(2,1)}, u32[]{:S(2)}, u32[]{:S(2)}) collective-permute-start(bf16[352,2048]{1,0:T(8,128)(2,1)} %bitcast.20), channel_id=1, source_target_pairs={{0,16},{3,19},{4,20},{7,23},{8,24},{11,27},{12,28},{15,31},{32,48}... | collective-permute-start | bytes 4325384 | tf_op jit(solution)/shard_map/ppermute | solution.py:59
  3.7 24.3 %collective-permute-start.2 = (bf16[352,2048]{1,0:T(8,128)(2,1)}, bf16[352,2048]{1,0:T(8,128)(2,1)S(1)}, u32[]{:S(2)}, u32[]{:S(2)}) collective-permute-start(bf16[352,2048]{1,0:T(8,128)(2,1)} %bitcast.17), channel_id=1, source_target_pairs={{4,0},{5,1},{6,2},{7,3},{8,12},{9,13},{10,14},{11,15},{16,4},{17,5... | collective-permute-start | bytes 4325384 | tf_op jit(solution)/shard_map/ppermute | solution.py:59
  11.9 20.5 %collective-permute-start.3 = (bf16[352,2048]{1,0:T(8,128)(2,1)}, bf16[352,2048]{1,0:T(8,128)(2,1)S(1)}, u32[]{:S(2)}, u32[]{:S(2)}) collective-permute-start(bf16[352,2048]{1,0:T(8,128)(2,1)} %bitcast.21), channel_id=1, source_target_pairs={{1,16},{2,19},{5,20},{6,23},{9,24},{10,27},{13,28},{14,31},{16,17}... | collective-permute-start | bytes 4325384 | tf_op jit(solution)/shard_map/ppermute | solution.py:59
  14.0 1.4 copy-start
  15.4 1.4 copy-start.2
  34.4 10.0 %collective-permute-start.4 = (bf16[2,128,1152]{2,1,0:T(8,128)(2,1)S(1)}, bf16[2,128,1152]{2,1,0:T(8,128)(2,1)S(1)}, u32[]{:S(2)}, u32[]{:S(2)}) collective-permute-start(bf16[2,128,1152]{2,1,0:T(8,128)(2,1)S(1)} %get-tuple-element.46), channel_id=1, source_target_pairs={{0,3},{1,2},{2,1},{3,0},{4,7},{5,6},{6,5},{7,4},{8,11},{9,10},{10,... | collective-permute-start | bytes 1769480 | tf_op jit(solution)/shard_map/ppermute | solution.py:59
  36.4 9.0 %collective-permute-start.6 = (bf16[2,128,1152]{2,1,0:T(8,128)(2,1)S(1)}, bf16[2,128,1152]{2,1,0:T(8,128)(2,1)S(1)}, u32[]{:S(2)}, u32[]{:S(2)}) collective-permute-start(bf16[2,128,1152]{2,1,0:T(8,128)(2,1)S(1)} %get-tuple-element.47), channel_id=1, source_target_pairs={{0,1},{1,0},{2,3},{3,2},{4,5},{5,4},{6,7},{7,6},{8,9},{9,8},{10,11... | collective-permute-start | bytes 1769480 | tf_op jit(solution)/shard_map/ppermute | solution.py:59
  44.7 15.4 %collective-permute-start.5 = (bf16[4,128,1152]{2,1,0:T(8,128)(2,1)S(1)}, bf16[4,128,1152]{2,1,0:T(8,128)(2,1)S(1)}, u32[]{:S(2)}, u32[]{:S(2)}) collective-permute-start(bf16[4,128,1152]{2,1,0:T(8,128)(2,1)S(1)} %fusion), channel_id=1, source_target_pairs={{0,1},{1,0},{2,3},{3,2},{4,5},{5,4},{6,7},{7,6},{8,9},{9,8},{10,11... | collective-permute-start | bytes 3538952 | tf_op jit(solution)/shard_map/ppermute | solution.py:59
  45.7 16.6 %collective-permute-start.7 = (bf16[4,128,1152]{2,1,0:T(8,128)(2,1)S(1)}, bf16[4,128,1152]{2,1,0:T(8,128)(2,1)S(1)}, u32[]{:S(2)}, u32[]{:S(2)}) collective-permute-start(bf16[4,128,1152]{2,1,0:T(8,128)(2,1)S(1)} %fusion.1), channel_id=1, source_target_pairs={{0,3},{1,2},{2,1},{3,0},{4,7},{5,6},{6,5},{7,4},{8,11},{9,10},{10,... | collective-permute-start | bytes 3538952 | tf_op jit(solution)/shard_map/ppermute | solution.py:59
  62.8 17.4 %collective-permute-start.8 = (bf16[4,128,1152]{2,1,0:T(8,128)(2,1)S(1)}, bf16[4,128,1152]{2,1,0:T(8,128)(2,1)S(1)}, u32[]{:S(2)}, u32[]{:S(2)}) collective-permute-start(bf16[4,128,1152]{2,1,0:T(8,128)(2,1)S(1)} %add_convert_fusion.1), channel_id=1, source_target_pairs={{0,12},{1,13},{2,14},{3,15},{4,8},{5,9},{6,10},{7,11},{8,4},{9,5},... | collective-permute-start | bytes 3538952 | tf_op jit(solution)/shard_map/ppermute | solution.py:59
  80.5 16.6 %collective-permute-start.10 = (bf16[4,128,1152]{2,1,0:T(8,128)(2,1)S(1)}, bf16[4,128,1152]{2,1,0:T(8,128)(2,1)S(1)}, u32[]{:S(2)}, u32[]{:S(2)}) collective-permute-start(bf16[4,128,1152]{2,1,0:T(8,128)(2,1)S(1)} %add_convert_fusion.rest_2_), channel_id=1, source_target_pairs={{0,3},{1,2},{2,1},{3,0},{4,7},{5,6},{6,5},{7,4},{8,11},{9,10},{10,... | collective-permute-start | bytes 3538952 | tf_op jit(solution)/shard_map/ppermute | solution.py:59
  82.2 15.3 %collective-permute-start.9 = (bf16[4,128,1152]{2,1,0:T(8,128)(2,1)S(1)}, bf16[4,128,1152]{2,1,0:T(8,128)(2,1)S(1)}, u32[]{:S(2)}, u32[]{:S(2)}) collective-permute-start(bf16[4,128,1152]{2,1,0:T(8,128)(2,1)S(1)} %add_convert_fusion.rest_2_), channel_id=1, source_target_pairs={{0,1},{1,0},{2,3},{3,2},{4,5},{5,4},{6,7},{7,6},{8,9},{9,8},{10,11... | collective-permute-start | bytes 3538952 | tf_op jit(solution)/shard_map/ppermute | solution.py:59
  97.2 9.1 %collective-permute-start.11 = (bf16[2,128,1152]{2,1,0:T(8,128)(2,1)S(1)}, bf16[2,128,1152]{2,1,0:T(8,128)(2,1)S(1)}, u32[]{:S(2)}, u32[]{:S(2)}) collective-permute-start(bf16[2,128,1152]{2,1,0:T(8,128)(2,1)S(1)} %slice.70), channel_id=1, source_target_pairs={{0,1},{1,0},{2,3},{3,2},{4,5},{5,4},{6,7},{7,6},{8,9},{9,8},{10,11... | collective-permute-start | bytes 1769480 | tf_op jit(solution)/shard_map/ppermute | solution.py:59
  97.6 10.3 %collective-permute-start.12 = (bf16[2,128,1152]{2,1,0:T(8,128)(2,1)S(1)}, bf16[2,128,1152]{2,1,0:T(8,128)(2,1)S(1)}, u32[]{:S(2)}, u32[]{:S(2)}) collective-permute-start(bf16[2,128,1152]{2,1,0:T(8,128)(2,1)S(1)} %slice.71), channel_id=1, source_target_pairs={{0,3},{1,2},{2,1},{3,0},{4,7},{5,6},{6,5},{7,4},{8,11},{9,10},{10,... | collective-permute-start | bytes 1769480 | tf_op jit(solution)/shard_map/ppermute | solution.py:59
  101.3 24.4 %copy-start.1 = (bf16[2048,352]{0,1:T(8,128)(2,1)S(1)}, bf16[2048,352]{0,1:T(8,128)(2,1)}, u32[]{:S(2)}) copy-start(bf16[2048,352]{0,1:T(8,128)(2,1)} %param.6) | copy-start | bytes 4325380
  101.3 24.4 %copy-start.3 = (bf16[2048,352]{0,1:T(8,128)(2,1)S(1)}, bf16[2048,352]{0,1:T(8,128)(2,1)}, u32[]{:S(2)}) copy-start(bf16[2048,352]{0,1:T(8,128)(2,1)} %param.7) | copy-start | bytes 4325380
  118.5 21.2 %collective-permute-start.14 = (bf16[352,2048]{1,0:T(8,128)(2,1)}, bf16[352,2048]{1,0:T(8,128)(2,1)S(1)}, u32[]{:S(2)}, u32[]{:S(2)}) collective-permute-start(bf16[352,2048]{1,0:T(8,128)(2,1)} %shard_map.45), channel_id=1, source_target_pairs={{0,4},{1,5},{2,6},{3,7},{12,8},{13,9},{14,10},{15,11},{4,16},{5,17... | collective-permute-start | bytes 4325384 | tf_op jit(solution)/shard_map/ppermute | solution.py:59
  119.8 22.1 %collective-permute-start.15 = (bf16[352,2048]{1,0:T(8,128)(2,1)}, bf16[352,2048]{1,0:T(8,128)(2,1)}, u32[]{:S(2)}, u32[]{:S(2)}) collective-permute-start(bf16[352,2048]{1,0:T(8,128)(2,1)} %shard_map.45), channel_id=1, source_target_pairs={{16,1},{19,2},{20,5},{23,6},{24,9},{27,10},{28,13},{31,14},{17,16}... | collective-permute-start | bytes 4325384 | tf_op jit(solution)/shard_map/ppermute | solution.py:59
  136.2 7.3 %collective-permute-start.13 = (bf16[352,2048]{1,0:T(8,128)(2,1)S(1)}, bf16[352,2048]{1,0:T(8,128)(2,1)}, u32[]{:S(2)}, u32[]{:S(2)}) collective-permute-start(bf16[352,2048]{1,0:T(8,128)(2,1)S(1)} %shard_map.46), channel_id=1, source_target_pairs={{4,20},{5,21},{6,22},{7,23},{8,24},{9,25},{10,26},{11,27},{36,52},... | collective-permute-start | bytes 4325384 | tf_op jit(solution)/shard_map/ppermute | solution.py:59

commit v3 on v2

--- a/solution.py
+++ b/solution.py
@@ -42,8 +42,7 @@
 
 GATE_OUT = device_pairs(lambda c, y, z: (0, y ^ 1, z) if c == (1 if outer(y) else 0) else None)
 UP_OUT = device_pairs(lambda c, y, z: (1, y, z ^ 1) if c == (1 if outer(z) else 0) else None)
-GATE_OVER = device_pairs(lambda c, y, z: (0, y, z) if c == 1 and not outer(y) else None)
-UP_OVER = device_pairs(lambda c, y, z: (1, y, z) if c == 0 and outer(z) else None)
+OVER = device_pairs(lambda c, y, z: (1 - c, y, z) if (outer(z) if c == 0 else not outer(y)) else None)
 
 
 def reverse(pairs):
@@ -129,47 +128,41 @@
     fetch_wide(choice[1], sources, wide, sems)
     span = terms.shape[2]
     done = 0
-    for out in outs:
-
-        def one(g, carry, out=out, done=done):
-            upper, lower = block_pair(wide, order[start + done + g], span)
-            at = 2 * (done + g)
-            out[2 * g] = (upper * scale + terms[at].astype(jnp.float32)).astype(out.dtype)
-            out[2 * g + 1] = (lower * scale + terms[at + 1].astype(jnp.float32)).astype(out.dtype)
-            return carry
-
-        lax.fori_loop(0, out.shape[0] // 2, one, 0)
-        done += out.shape[0] // 2
+    for upper_out, lower_out in zip(outs[0::2], outs[1::2]):
+        for g in range(upper_out.shape[0]):
+            upper, lower = block_pair(wide, order[start + done], span)
+            at = 2 * done
+            upper_out[g] = (upper * scale + terms[at].astype(jnp.float32)).astype(upper_out.dtype)
+            lower_out[g] = (lower * scale + terms[at + 1].astype(jnp.float32)).astype(lower_out.dtype)
+            done += 1
 
 
 def add_terms(order, choice, sources, terms, start, counts, scale):
     dev_cols, rows = sources[0].shape
     span = rows // 2 + BLOCK
+    shapes = [n for n in counts for half in (0, 1)]
     return pl.pallas_call(
         functools.partial(add_terms_kernel, scale, start),
-        out_shape=[jax.ShapeDtypeStruct((n, BLOCK, span), jnp.bfloat16) for n in counts],
+        out_shape=[jax.ShapeDtypeStruct((n, BLOCK, span), jnp.bfloat16) for n in shapes],
         in_specs=[SMEM, SMEM] + [ANY] * len(sources) + [VMEM],
-        out_specs=[VMEM] * len(counts),
+        out_specs=[VMEM] * len(shapes),
         scratch_shapes=[
             pltpu.VMEM((dev_cols, rows + rows // 2), jnp.bfloat16),
             pltpu.SemaphoreType.DMA((2,)),
         ],
         compiler_params=params(),
         cost_estimate=pl.CostEstimate(
-            flops=2 * sum(counts) * BLOCK * span * dev_cols, bytes_accessed=10000000, transcendentals=0
+            flops=4 * sum(counts) * BLOCK * span * dev_cols, bytes_accessed=10000000, transcendentals=0
         ),
     )(order, choice, *sources, terms)
 
 
-def unpack_kernel(start, order, *rest):
-    pieces, gram = rest[:-1], rest[-1]
+def place_blocks(places, order, pieces, gram):
     count = gram.shape[0] // BLOCK
-    place = start
-    for piece in pieces:
+    for (place, half), piece in zip(places, pieces):
         span = piece.shape[2]
         for k in range(piece.shape[0]):
-            index = 2 * order[place // 2] + place % 2
-            place += 1
+            index = 2 * order[place + k] + half
             top = pl.multiple_of(index * BLOCK, BLOCK)
             for shift in range(span // BLOCK):
                 left = pl.multiple_of(((index + shift) % count) * BLOCK, BLOCK)
@@ -179,9 +172,13 @@
                     gram[pl.ds(left, BLOCK), pl.ds(top, BLOCK)] = block.T
 
 
-def unpack(order, pieces, start, rows):
-    return pl.pallas_call(
-        functools.partial(unpack_kernel, start),
+def unpack_kernel(places, order, *rest):
+    place_blocks(places, order, rest[:-1], rest[-1])
+
+
+def unpack(order, pieces, places, rows):
+    return pl.pallas_call(
+        functools.partial(unpack_kernel, places),
         out_shape=jax.ShapeDtypeStruct((rows, rows), jnp.bfloat16),
         in_specs=[SMEM] + [VMEM] * len(pieces),
         out_specs=VMEM,
@@ -190,8 +187,12 @@
     )(order, *pieces)
 
 
+LAST_PLACES = ((0, 0), (1, 0), (0, 1), (1, 1))
+
+
 def step_kernel(which, order, choice, *rest):
-    sources, (gram_in, last_a, last_b, result, gram, columns, low, linear, sems) = rest[:-9], rest[-9:]
+    sources, lasts = rest[:-11], rest[-10:-6]
+    gram_in, (result, gram, columns, low, linear, sems) = rest[-11], rest[-6:]
     rows = gram.shape[0]
     load = pltpu.make_async_copy(gram_in, gram, sems.at[0])
     load.start()
@@ -204,7 +205,7 @@
             fetch.wait()
 
     load.wait()
-    unpack_kernel(0, order, last_a, last_b, gram)
+    place_blocks(LAST_PLACES, order, lasts, gram)
 
     def multiply(t, carry):
         at = pl.ds(pl.multiple_of(t * TILE, TILE), TILE)
@@ -224,12 +225,12 @@
     lax.fori_loop(0, rows // TILE, again, 0)
 
 
-def newton_step(which, order, choice, sources, gram, last_a, last_b):
+def newton_step(which, order, choice, sources, gram, lasts):
     dev_cols, rows = sources[0].shape
     return pl.pallas_call(
         functools.partial(step_kernel, which),
         out_shape=jax.ShapeDtypeStruct((dev_cols, rows), jnp.bfloat16),
-        in_specs=[SMEM, SMEM] + [ANY] * (len(sources) + 1) + [VMEM, VMEM],
+        in_specs=[SMEM, SMEM] + [ANY] * (len(sources) + 1) + [VMEM] * len(lasts),
         out_specs=VMEM,
         scratch_shapes=[
             pltpu.VMEM((rows, rows), jnp.bfloat16),
@@ -242,7 +243,43 @@
         cost_estimate=pl.CostEstimate(
             flops=4 * rows * rows * dev_cols, bytes_accessed=12000000, transcendentals=0
         ),
-    )(order, choice, *sources, gram, last_a, last_b)
+    )(order, choice, *sources, gram, *lasts)
+
+
+def token_kernel(gate_back, up_back, token):
+    token[...] = jnp.zeros_like(token)
+
+
+def after(*arrays):
+    return pl.pallas_call(
+        token_kernel,
+        out_shape=jax.ShapeDtypeStruct((8, BLOCK), jnp.float32),
+        in_specs=[ANY] * len(arrays),
+        out_specs=VMEM,
+    )(*arrays)
+
+
+def finish_kernel(pick, token, own, over, gate_back, up_back, gate_out, up_out, sems):
+    copies = [
+        (pick[n] == k, pltpu.make_async_copy(source, out, sems.at[n]))
+        for n, (back, out) in enumerate(((gate_back, gate_out), (up_back, up_out)))
+        for k, source in enumerate((own, over, back))
+    ]
+    for wanted, copy in copies:
+        pl.when(wanted)(copy.start)
+    for wanted, copy in copies:
+        pl.when(wanted)(copy.wait)
+
+
+def finish(pick, own, over, gate_back, up_back):
+    shape = jax.ShapeDtypeStruct(own.shape, own.dtype)
+    return pl.pallas_call(
+        finish_kernel,
+        out_shape=[shape, shape],
+        in_specs=[SMEM] + [ANY] * 5,
+        out_specs=[VMEM, VMEM],
+        scratch_shapes=[pltpu.SemaphoreType.DMA((2,))],
+    )(pick, after(gate_back, up_back), own, over, gate_back, up_back)
 
 
 def add(*terms):
@@ -269,44 +306,55 @@
             for stream in (0, 1)
         ]
     )
-    own_choice = jnp.where(on_gate, 2 * gate_part, 1 + 2 * (1 - up_part))
+    own_choice = jnp.where(on_gate, 2 * gate_part, 2 - up_part)
     choice = jnp.stack([own_choice, on_up])
 
-    gate_over = send(gate, GATE_OVER)
-    up_over = send(up, UP_OVER)
     gate_in = send(gate, GATE_OUT)
     up_in = send(up, UP_OUT)
-    own = (gate, up, gate_over, up_over)
+    over = send(jnp.where(on_gate, up, gate), OVER)
+    own = (gate, up, over)
     partner = (gate_in, up_in)
     corner_terms, other_terms = own_terms(order, choice, own, scale)
 
-    (corner,) = add_terms(order, choice, partner, corner_terms, 0, (4,), scale)
-    got_a = send(corner[0:2], HOP_1)
-    got_b = send(corner[2:4], HOP_2)
-    side_1, side_2, mine = add_terms(order, choice, partner, other_terms, 2, (4, 4, 4), scale)
-    got_1 = send(side_1.at[2:4].set(add(side_1[2:4], got_b)), HOP_1)
-    got_2 = send(side_2.at[0:2].set(add(side_2[0:2], got_a)), HOP_2)
-    mine = add(mine, got_1, got_2)
-    total = add(mine, send(mine, HOP_3))
-
-    all_1 = send(total, HOP_1)
-    all_2 = send(total, HOP_2)
-    last_a = send(all_2[0:2], HOP_1)
-    last_b = send(all_1[2:4], HOP_2)
-    gram = unpack(order, (all_1, all_2, total), 4, rows)
-
-    partner_next = newton_step(1, order, choice, partner, gram, last_a, last_b)
+    corner = add_terms(order, choice, partner, corner_terms, 0, (1, 1), scale)
+    got_a = [send(corner[half], HOP_1) for half in (0, 1)]
+    got_b = [send(corner[2 + half], HOP_2) for half in (0, 1)]
+    rest = add_terms(order, choice, partner, other_terms, 2, (2, 2, 2), scale)
+    totals, ones, twos, lasts, places = [], [], [], [], []
+    for half in (0, 1):
+        side_1, side_2, mine = rest[half], rest[2 + half], rest[4 + half]
+        got_1 = send(side_1.at[1:2].set(add(side_1[1:2], got_b[half])), HOP_1)
+        got_2 = send(side_2.at[0:1].set(add(side_2[0:1], got_a[half])), HOP_2)
+        mine = add(mine, got_1, got_2)
+        totals.append(add(mine, send(mine, HOP_3)))
+
+    for half in (0, 1):
+        ones.append(send(totals[half], HOP_1))
+        twos.append(send(totals[half], HOP_2))
+    for half in (0, 1):
+        lasts.append(send(twos[half][0:1], HOP_1))
+        lasts.append(send(ones[half][1:2], HOP_2))
+    gram = unpack(
+        order,
+        ones + twos + totals,
+        ((2, 0), (2, 1), (4, 0), (4, 1), (6, 0), (6, 1)),
+        rows,
+    )
+
+    partner_next = newton_step(1, order, choice, partner, gram, lasts)
     gate_back = send(partner_next, reverse(GATE_OUT))
     up_back = send(partner_next, reverse(UP_OUT))
-    last_a, partner_next = lax.optimization_barrier((last_a, partner_next))
-    own_next = newton_step(0, order, choice, own, gram, last_a, last_b)
-    over_back = send(own_next, reverse(GATE_OVER) + reverse(UP_OVER))
-
-    gate_next = jnp.where(gate_part == on_up, own_next, gate_back)
-    up_next = jnp.where(up_part == on_up, own_next, up_back)
-    gate_next, up_next = lax.optimization_barrier((gate_next, up_next))
-    gate_next = jnp.where((gate_part == on_up) & (on_up == 1), over_back, gate_next)
-    up_next = jnp.where((up_part == on_up) & on_gate, over_back, up_next)
+    lasts[0], partner_next = lax.optimization_barrier((lasts[0], partner_next))
+    own_next = newton_step(0, order, choice, own, gram, lasts)
+    over_back = send(own_next, reverse(OVER))
+
+    pick = jnp.stack(
+        [
+            jnp.where(gate_part == on_up, on_up, 2),
+            jnp.where(up_part == on_up, 1 - on_up, 2),
+        ]
+    )
+    gate_next, up_next = finish(pick, own_next, over_back, gate_back, up_back)
     return gate_next.T, up_next.T
 
 

time: 147 us -> 133 us (0.905)
  waiting for transfers between devices: 67.7 us -> 37.7 us
  starting transfers between devices: 33.1 us -> 48.9 us
  Pallas kernels: 35.7 us -> 39.2 us
  local copies, waits for them, and re-layouts: 3.01 us -> 0.19 us
    ppermute x16 -> x24, waiting for transfers between devices: 67.7 us -> 37.7 us  [send(): return lax.ppermute(values, AXES, pairs)]
    ppermute x16 -> x24, starting transfers between devices: 33.1 us -> 48.9 us  [send(): return lax.ppermute(values, AXES, pairs)]
    pallas_call x1 -> x3, Pallas kernels: 2.21 us -> 6.86 us  [the longest x1 4.05 us: finish(): pl.pallas_call(finish_kernel, out_shape=[shape, shape], in_specs=[SMEM] +...]
    transpose x1 -> x0, other arithmetic: 3.18 us -> none  [per_device(): return (gate_next.T, up_next.T)]
    unnamed x8 -> x4, local copies, waits for them, and re-layouts: 2.74 us -> 0.01 us
  transfers between devices with their start and end apart: 16 -> 24, of which waited for: 13 -> 13; matrix products, arithmetic and copies ran while one was open for 2% -> 2% of each run, Pallas kernels for 16% -> 17%
where the time goes in v3:
time: 133 us; the launch traced here: 132 us
  starting transfers between devices  48.9 us (37%)
  Pallas kernels  39.2 us (29%)
  waiting for transfers between devices  37.7 us (28%)
  other arithmetic  5.05 us (4%)
    ppermute x24, starting transfers between devices, send(): return lax.ppermute(values, AXES, pairs)  48.9 us
    ppermute x24, waiting for transfers between devices, send(): return lax.ppermute(values, AXES, pairs)  37.7 us
    pallas_call x2, Pallas kernels, newton_step(): pl.pallas_call(functools.partial(step_kernel, which), out_shape=jax.Shape...  21.1 us
    pallas_call x1, Pallas kernels, own_terms(): pl.pallas_call(functools.partial(own_terms_kernel, scale), out_shape=[jax...  6.5 us
    pallas_call x2, Pallas kernels, add_terms(): pl.pallas_call(functools.partial(add_terms_kernel, scale, start), out_sha...  4.74 us
    pallas_call x1, Pallas kernels, finish(): pl.pallas_call(finish_kernel, out_shape=[shape, shape], in_specs=[SMEM] +...  4.05 us
    select_n x1, other arithmetic, per_device(): over = send(jnp.where(on_gate, up, gate), OVER)  3.05 us
  transfers between devices with their start and end apart: 24, of which 13 were waited for; matrix products, arithmetic and copies ran while one was open for 2% of the time, Pallas kernels for 17%

profile of v3, /device:TPU:1, one launch (start us, length us, event | category | flops | bytes accessed | tf_op | source)
XLA Modules:
  0.0 132.1 jit_solution(469257924884993768)
XLA Ops:
  0.6 3.0 %broadcast_select_fusion = bf16[352,2048]{1,0:T(8,128)(2,1)} fusion(pred[]{:T(512)S(6)} %eq.29, bf16[2048,352]{0,1:T(8,128)(2,1)} %param.11, bf16[2048,352]{0,1:T(8,128)(2,1)} %param.10), kind=kLoop, calls=%fused_computation | loop fusion | flops 720896 | bytes 4325377 | tf_op jit(solution)/shard_map/jit(_where)/select_n | solution.py:314
  3.7 1.3 collective-permute-start.2
  5.0 5.3 %collective-permute-start = (bf16[352,2048]{1,0:T(8,128)(2,1)}, bf16[352,2048]{1,0:T(8,128)(2,1)S(1)}, u32[]{:S(2)}, u32[]{:S(2)}) collective-permute-start(bf16[352,2048]{1,0:T(8,128)(2,1)} %bitcast.12.rest_0_), channel_id=1, source_target_pairs={{4,0},{5,1},{6,2},{7,3},{8,12},{9,13},{10,14},{11,15},{16,4},{17,5... | collective-permute-start | bytes 4325384 | tf_op jit(solution)/shard_map/ppermute | solution.py:58
  10.3 2.9 %collective-permute-start.1 = (bf16[352,2048]{1,0:T(8,128)(2,1)}, bf16[352,2048]{1,0:T(8,128)(2,1)S(1)}, u32[]{:S(2)}, u32[]{:S(2)}) collective-permute-start(bf16[352,2048]{1,0:T(8,128)(2,1)} %bitcast.13.rest_1_), channel_id=1, source_target_pairs={{1,16},{2,19},{5,20},{6,23},{9,24},{10,27},{13,28},{14,31},{16,17}... | collective-permute-start | bytes 4325384 | tf_op jit(solution)/shard_map/ppermute | solution.py:58
  13.4 6.5 %shard_map.41 = (bf16[4,128,1152]{2,1,0:T(8,128)(2,1)S(1)}, bf16[12,128,1152]{2,1,0:T(8,128)(2,1)S(1)}) custom-call(s32[8]{0:T(128)S(1)} %stack.56.order, s32[2]{0:T(128)S(1)} %pad_add_fusion.1.choice, bf16[352,2048]{1,0:T(8,128)(2,1)} %bitcast.12.rest_0_, bf16[352,2048]{1,0:T(8,128)(2,1)} %bitcast.13.rest_1_, bf16[352,2048]{1,0:T(8,128)(2,1)} %collective-permute-done.2.rest_2_), custom_call_target="tpu_custom_call" | custom-call | flops 1660944384 | bytes 20000000 | tf_op jit(solution)/shard_map/pallas_call | solution.py:110
  19.9 6.5 %collective-permute-done.rest_0_ = bf16[352,2048]{1,0:T(8,128)(2,1)S(1)} collective-permute-done((bf16[352,2048]{1,0:T(8,128)(2,1)}, bf16[352,2048]{1,0:T(8,128)(2,1)S(1)}, u32[]{:S(2)}, u32[]{:S(2)}) %collective-permute-start) | collective-permute-done | bytes 1441824 | tf_op jit(solution)/shard_map/ppermute | solution.py:58
  26.5 4.4 %collective-permute-done.1.rest_1_ = bf16[352,2048]{1,0:T(8,128)(2,1)S(1)} collective-permute-done((bf16[352,2048]{1,0:T(8,128)(2,1)}, bf16[352,2048]{1,0:T(8,128)(2,1)S(1)}, u32[]{:S(2)}, u32[]{:S(2)}) %collective-permute-start.1) | collective-permute-done | bytes 1441824 | tf_op jit(solution)/shard_map/ppermute | solution.py:58
  30.8 1.7 %shard_map.43 = (bf16[1,128,1152]{2,1,0:T(8,128)(2,1)S(1)}, bf16[1,128,1152]{2,1,0:T(8,128)(2,1)S(1)}, bf16[1,128,1152]{2,1,0:T(8,128)(2,1)S(1)}, bf16[1,128,1152]{2,1,0:T(8,128)(2,1)S(1)}) custom-call(s32[8]{0:T(128)S(1)} %stack.56.order, s32[2]{0:T(128)S(1)} %pad_add_fusion.1.choice, bf16[352,2048]{1,0:T(8,128)(2,1)S(1)} %collective-permute-done.rest_0_, ...), custom_call_target="tpu_custom_call" | custom-call | flops 415236096 | bytes 10000000 | tf_op jit(solution)/shard_map/pallas_call | solution.py:144
  32.6 2.2 %collective-permute-start.3 = (bf16[1,128,1152]{2,1,0:T(8,128)(2,1)S(1)}, bf16[1,128,1152]{2,1,0:T(8,128)(2,1)S(1)}, u32[]{:S(2)}, u32[]{:S(2)}) collective-permute-start(bf16[1,128,1152]{2,1,0:T(8,128)(2,1)S(1)} %get-tuple-element.69), channel_id=1, source_target_pairs={{0,3},{1,2},{2,1},{3,0},{4,7},{5,6},{6,5},{7,4},{8,11},{9,10},{10,... | collective-permute-start | bytes 884744 | tf_op jit(solution)/shard_map/ppermute | solution.py:58
  34.8 0.5 collective-permute-start.11
  35.4 0.8 collective-permute-start.9
  36.1 3.1 %shard_map.42 = (bf16[2,128,1152]{2,1,0:T(8,128)(2,1)S(1)}, bf16[2,128,1152]{2,1,0:T(8,128)(2,1)S(1)}, bf16[2,128,1152]{2,1,0:T(8,128)(2,1)S(1)}, bf16[2,128,115...) custom-call(s32[8]{0:T(128)S(1)} %stack.56.order, ...), custom_call_target="tpu_custom_call" | custom-call | flops 1245708288 | bytes 10000000 | tf_op jit(solution)/shard_map/pallas_call | solution.py:144
  39.2 0.1 fusion.1
  39.4 2.0 %collective-permute-start.6 = (bf16[2,128,1152]{2,1,0:T(8,128)(2,1)S(1)}, bf16[2,128,1152]{2,1,0:T(8,128)(2,1)S(1)}, u32[]{:S(2)}, u32[]{:S(2)}) collective-permute-start(bf16[2,128,1152]{2,1,0:T(8,128)(2,1)S(1)} %fusion.1), channel_id=1, source_target_pairs={{0,3},{1,2},{2,1},{3,0},{4,7},{5,6},{6,5},{7,4},{8,11},{9,10},{10,... | collective-permute-start | bytes 1769480 | tf_op jit(solution)/shard_map/ppermute | solution.py:58
  41.4 0.1 fusion
  41.6 0.1 fusion.3
  41.8 2.0 %collective-permute-start.12 = (bf16[2,128,1152]{2,1,0:T(8,128)(2,1)S(1)}, bf16[2,128,1152]{2,1,0:T(8,128)(2,1)S(1)}, u32[]{:S(2)}, u32[]{:S(2)}) collective-permute-start(bf16[2,128,1152]{2,1,0:T(8,128)(2,1)S(1)} %fusion.3), channel_id=1, source_target_pairs={{0,3},{1,2},{2,1},{3,0},{4,7},{5,6},{6,5},{7,4},{8,11},{9,10},{10,... | collective-permute-start | bytes 1769480 | tf_op jit(solution)/shard_map/ppermute | solution.py:58
  43.7 0.1 fusion.2
  44.0 5.7 %collective-permute-done.6 = bf16[2,128,1152]{2,1,0:T(8,128)(2,1)S(1)} collective-permute-done((bf16[2,128,1152]{2,1,0:T(8,128)(2,1)S(1)}, bf16[2,128,1152]{2,1,0:T(8,128)(2,1)S(1)}, u32[]{:S(2)}, u32[]{:S(2)}) %collective-permute-start.6) | collective-permute-done | bytes 589856 | tf_op jit(solution)/shard_map/ppermute | solution.py:58
  49.7 0.9 collective-permute-done.4
  50.6 0.2 add_convert_fusion.3
  50.8 3.8 %collective-permute-start.7 = (bf16[2,128,1152]{2,1,0:T(8,128)(2,1)S(1)}, bf16[2,128,1152]{2,1,0:T(8,128)(2,1)S(1)}, u32[]{:S(2)}, u32[]{:S(2)}) collective-permute-start(bf16[2,128,1152]{2,1,0:T(8,128)(2,1)S(1)} %add_convert_fusion.3), channel_id=1, source_target_pairs={{0,12},{1,13},{2,14},{3,15},{4,8},{5,9},{6,10},{7,11},{8,4},{9,5},... | collective-permute-start | bytes 1769480 | tf_op jit(solution)/shard_map/ppermute | solution.py:58
  54.7 1.3 %collective-permute-done.12 = bf16[2,128,1152]{2,1,0:T(8,128)(2,1)S(1)} collective-permute-done((bf16[2,128,1152]{2,1,0:T(8,128)(2,1)S(1)}, bf16[2,128,1152]{2,1,0:T(8,128)(2,1)S(1)}, u32[]{:S(2)}, u32[]{:S(2)}) %collective-permute-start.12) | collective-permute-done | bytes 589856 | tf_op jit(solution)/shard_map/ppermute | solution.py:58
  56.0 0.9 collective-permute-done.10
  56.9 0.2 add_convert_fusion.1
  57.1 3.8 %collective-permute-start.13 = (bf16[2,128,1152]{2,1,0:T(8,128)(2,1)S(1)}, bf16[2,128,1152]{2,1,0:T(8,128)(2,1)S(1)}, u32[]{:S(2)}, u32[]{:S(2)}) collective-permute-start(bf16[2,128,1152]{2,1,0:T(8,128)(2,1)S(1)} %add_convert_fusion.1), channel_id=1, source_target_pairs={{0,12},{1,13},{2,14},{3,15},{4,8},{5,9},{6,10},{7,11},{8,4},{9,5},... | collective-permute-start | bytes 1769480 | tf_op jit(solution)/shard_map/ppermute | solution.py:58
  61.0 2.8 %collective-permute-done.7 = bf16[2,128,1152]{2,1,0:T(8,128)(2,1)S(1)} collective-permute-done((bf16[2,128,1152]{2,1,0:T(8,128)(2,1)S(1)}, bf16[2,128,1152]{2,1,0:T(8,128)(2,1)S(1)}, u32[]{:S(2)}, u32[]{:S(2)}) %collective-permute-start.7) | collective-permute-done | bytes 589856 | tf_op jit(solution)/shard_map/ppermute | solution.py:58
  63.8 0.1 add_convert_fusion.2.rest_4_
  64.0 2.6 %collective-permute-start.15 = (bf16[2,128,1152]{2,1,0:T(8,128)(2,1)S(1)}, bf16[2,128,1152]{2,1,0:T(8,128)(2,1)S(1)}, u32[]{:S(2)}, u32[]{:S(2)}) collective-permute-start(bf16[2,128,1152]{2,1,0:T(8,128)(2,1)S(1)} %add_convert_fusion.2.rest_4_), channel_id=1, source_target_pairs={{0,3},{1,2},{2,1},{3,0},{4,7},{5,6},{6,5},{7,4},{8,11},{9,10},{10,... | collective-permute-start | bytes 1769480 | tf_op jit(solution)/shard_map/ppermute | solution.py:58
  66.7 3.5 %collective-permute-done.13 = bf16[2,128,1152]{2,1,0:T(8,128)(2,1)S(1)} collective-permute-done((bf16[2,128,1152]{2,1,0:T(8,128)(2,1)S(1)}, bf16[2,128,1152]{2,1,0:T(8,128)(2,1)S(1)}, u32[]{:S(2)}, u32[]{:S(2)}) %collective-permute-start.13) | collective-permute-done | bytes 589856 | tf_op jit(solution)/shard_map/ppermute | solution.py:58
  70.1 0.2 add_convert_fusion.rest_5_
  70.3 3.5 %collective-permute-start.16 = (bf16[2,128,1152]{2,1,0:T(8,128)(2,1)S(1)}, bf16[2,128,1152]{2,1,0:T(8,128)(2,1)S(1)}, u32[]{:S(2)}, u32[]{:S(2)}) collective-permute-start(bf16[2,128,1152]{2,1,0:T(8,128)(2,1)S(1)} %add_convert_fusion.rest_5_), channel_id=1, source_target_pairs={{0,3},{1,2},{2,1},{3,0},{4,7},{5,6},{6,5},{7,4},{8,11},{9,10},{10,... | collective-permute-start | bytes 1769480 | tf_op jit(solution)/shard_map/ppermute | solution.py:58
  73.7 3.8 %collective-permute-done.15.rest_2_ = bf16[2,128,1152]{2,1,0:T(8,128)(2,1)S(1)} collective-permute-done((bf16[2,128,1152]{2,1,0:T(8,128)(2,1)S(1)}, bf16[2,128,1152]{2,1,0:T(8,128)(2,1)S(1)}, u32[]{:S(2)}, u32[]{:S(2)}) %collective-permute-start.15) | collective-permute-done | bytes 589856 | tf_op jit(solution)/shard_map/ppermute | solution.py:58
  77.7 3.0 %collective-permute-start.18 = (bf16[1,128,1152]{2,1,0:T(8,128)(2,1)S(1)}, bf16[1,128,1152]{2,1,0:T(8,128)(2,1)S(1)}, u32[]{:S(2)}, u32[]{:S(2)}) collective-permute-start(bf16[1,128,1152]{2,1,0:T(8,128)(2,1)S(1)} %slice.121), channel_id=1, source_target_pairs={{0,3},{1,2},{2,1},{3,0},{4,7},{5,6},{6,5},{7,4},{8,11},{9,10},{10,... | collective-permute-start | bytes 884744 | tf_op jit(solution)/shard_map/ppermute | solution.py:58
  80.8 3.4 %collective-permute-done.16.rest_3_ = bf16[2,128,1152]{2,1,0:T(8,128)(2,1)S(1)} collective-permute-done((bf16[2,128,1152]{2,1,0:T(8,128)(2,1)S(1)}, bf16[2,128,1152]{2,1,0:T(8,128)(2,1)S(1)}, u32[]{:S(2)}, u32[]{:S(2)}) %collective-permute-start.16) | collective-permute-done | bytes 589856 | tf_op jit(solution)/shard_map/ppermute | solution.py:58
  84.3 3.2 %collective-permute-start.20 = (bf16[1,128,1152]{2,1,0:T(8,128)(2,1)S(1)}, bf16[1,128,1152]{2,1,0:T(8,128)(2,1)S(1)}, u32[]{:S(2)}, u32[]{:S(2)}) collective-permute-start(bf16[1,128,1152]{2,1,0:T(8,128)(2,1)S(1)} %slice.123), channel_id=1, source_target_pairs={{0,3},{1,2},{2,1},{3,0},{4,7},{5,6},{6,5},{7,4},{8,11},{9,10},{10,... | collective-permute-start | bytes 884744 | tf_op jit(solution)/shard_map/ppermute | solution.py:58
  87.6 2.2 %shard_map.44.rest_2_.rest_3_ = bf16[2048,2048]{1,0:T(8,128)(2,1)S(1)} custom-call(s32[8]{0:T(128)S(1)} %stack.56.order, bf16[2,128,1152]{2,1,0:T(8,128)(2,1)S(1)} %collective-permute-done.8.rest_0_, bf16[2,128,1152]{2,1,0:T(8,128)(2,1)S(1)} %collective-permute-done.14.rest_1_, bf16[2,128,1152]{2,1,0:T(8,128)(2,1)S(1)} %collective-permute-done.15.rest_2_, ...), custom_call_target="tpu_custom_call" | custom-call | bytes 20000000 | tf_op jit(solution)/shard_map/pallas_call | solution.py:180
  89.8 0.4 collective-permute-done.19.rest_5_.rest_6_
  90.2 1.5 %collective-permute-done.20.rest_6_.rest_7_ = bf16[1,128,1152]{2,1,0:T(8,128)(2,1)S(1)} collective-permute-done((bf16[1,128,1152]{2,1,0:T(8,128)(2,1)S(1)}, bf16[1,128,1152]{2,1,0:T(8,128)(2,1)S(1)}, u32[]{:S(2)}, u32[]{:S(2)}) %collective-permute-start.20) | collective-permute-done | bytes 294944 | tf_op jit(solution)/shard_map/ppermute | solution.py:58
  91.7 10.5 %shard_map.45 = bf16[352,2048]{1,0:T(8,128)(2,1)} custom-call(s32[8]{0:T(128)S(1)} %stack.56.order, s32[2]{0:T(128)S(1)} %pad_add_fusion.1.choice, bf16[352,2048]{1,0:T(8,128)(2,1)S(1)} %collective-permute-done.rest_0_, bf16[352,2048]{1,0:T(8,128)(2,1)S(1)} %collective-permute-done.1.rest_1_, bf16[2048,2048]{1,0:T(8,128)(2,1)S(1)} %shard_map.44.rest_2_.rest_3_, ...), custom_call_target="tpu_custom_call" | custom-call | flops 5905580032 | bytes 12000000 | tf_op jit(solution)/shard_map/pallas_call | solution.py:230
  102.2 1.3 collective-permute-start.21
  103.5 7.5 %collective-permute-start.22 = (bf16[352,2048]{1,0:T(8,128)(2,1)}, bf16[352,2048]{1,0:T(8,128)(2,1)}, u32[]{:S(2)}, u32[]{:S(2)}) collective-permute-start(bf16[352,2048]{1,0:T(8,128)(2,1)} %shard_map.45), channel_id=1, source_target_pairs={{16,1},{19,2},{20,5},{23,6},{24,9},{27,10},{28,13},{31,14},{17,16}... | collective-permute-start | bytes 4325384 | tf_op jit(solution)/shard_map/ppermute | solution.py:58
  111.1 10.5 %shard_map.47.own = bf16[352,2048]{1,0:T(8,128)(2,1)S(1)} custom-call(s32[8]{0:T(128)S(1)} %stack.56.order, s32[2]{0:T(128)S(1)} %pad_add_fusion.1.choice, bf16[352,2048]{1,0:T(8,128)(2,1)} %bitcast.12.rest_0_, bf16[352,2048]{1,0:T(8,128)(2,1)} %bitcast.13.rest_1_, bf16[352,2048]{1,0:T(8,128)(2,1)} %collective-permute-done.2.rest_2_, ...), custom_call_target="tpu_custom_call" | custom-call | flops 5905580032 | bytes 12000000 | tf_op jit(solution)/shard_map/pallas_call | solution.py:230
  121.6 2.6 %collective-permute-start.23 = (bf16[352,2048]{1,0:T(8,128)(2,1)S(1)}, bf16[352,2048]{1,0:T(8,128)(2,1)}, u32[]{:S(2)}, u32[]{:S(2)}) collective-permute-start(bf16[352,2048]{1,0:T(8,128)(2,1)S(1)} %shard_map.47.own), channel_id=1, source_target_pairs={{16,0},{19,3},{20,4},{23,7},{24,8},{27,11},{28,12},{31,15},{4,20},... | collective-permute-start | bytes 4325384 | tf_op jit(solution)/shard_map/ppermute | solution.py:58
  124.2 0.6 pad_add_fusion.pick
  124.8 2.5 %collective-permute-done.22.up_back = bf16[352,2048]{1,0:T(8,128)(2,1)} collective-permute-done((bf16[352,2048]{1,0:T(8,128)(2,1)}, bf16[352,2048]{1,0:T(8,128)(2,1)}, u32[]{:S(2)}, u32[]{:S(2)}) %collective-permute-start.22) | collective-permute-done | bytes 1441824 | tf_op jit(solution)/shard_map/ppermute | solution.py:58
  127.3 0.6 shard_map.46.token
  127.9 4.1 %shard_map.48 = (bf16[352,2048]{1,0:T(8,128)(2,1)}, bf16[352,2048]{1,0:T(8,128)(2,1)}) custom-call(s32[2]{0:T(128)} %pad_add_fusion.pick, f32[8,128]{1,0:T(8,128)} %shard_map.46.token, bf16[352,2048]{1,0:T(8,128)(2,1)} %copy-done, bf16[352,2048]{1,0:T(8,128)(2,1)} %collective-permute-done.23.over, bf16[352,2048]{1,0:T(8,128)(2,1)} %copy-done.1, ...), custom_call_target="tpu_custom_call" | custom-call | tf_op jit(solution)/shard_map/pallas_call | solution.py:276
  (28 shorter events, 0.8 us)
Async XLA Ops:
  3.7 9.7 %collective-permute-start.2 = (bf16[352,2048]{1,0:T(8,128)(2,1)}, bf16[352,2048]{1,0:T(8,128)(2,1)}, u32[]{:S(2)}, u32[]{:S(2)}) collective-permute-start(bf16[352,2048]{1,0:T(8,128)(2,1)} %broadcast_select_fusion), channel_id=1, source_target_pairs={{0,16},{3,19},{4,20},{7,23},{8,24},{11,27},{12,28},{15,31},{20,4},... | collective-permute-start | bytes 4325384 | tf_op jit(solution)/shard_map/ppermute | solution.py:58
  5.0 21.5 %collective-permute-start = (bf16[352,2048]{1,0:T(8,128)(2,1)}, bf16[352,2048]{1,0:T(8,128)(2,1)S(1)}, u32[]{:S(2)}, u32[]{:S(2)}) collective-permute-start(bf16[352,2048]{1,0:T(8,128)(2,1)} %bitcast.12.rest_0_), channel_id=1, source_target_pairs={{4,0},{5,1},{6,2},{7,3},{8,12},{9,13},{10,14},{11,15},{16,4},{17,5... | collective-permute-start | bytes 4325384 | tf_op jit(solution)/shard_map/ppermute | solution.py:58
  10.3 20.5 %collective-permute-start.1 = (bf16[352,2048]{1,0:T(8,128)(2,1)}, bf16[352,2048]{1,0:T(8,128)(2,1)S(1)}, u32[]{:S(2)}, u32[]{:S(2)}) collective-permute-start(bf16[352,2048]{1,0:T(8,128)(2,1)} %bitcast.13.rest_1_), channel_id=1, source_target_pairs={{1,16},{2,19},{5,20},{6,23},{9,24},{10,27},{13,28},{14,31},{16,17}... | collective-permute-start | bytes 4325384 | tf_op jit(solution)/shard_map/ppermute | solution.py:58
  32.5 6.7 %collective-permute-start.5 = (bf16[1,128,1152]{2,1,0:T(8,128)(2,1)S(1)}, bf16[1,128,1152]{2,1,0:T(8,128)(2,1)S(1)}, u32[]{:S(2)}, u32[]{:S(2)}) collective-permute-start(bf16[1,128,1152]{2,1,0:T(8,128)(2,1)S(1)} %get-tuple-element.71), channel_id=1, source_target_pairs={{0,1},{1,0},{2,3},{3,2},{4,5},{5,4},{6,7},{7,6},{8,9},{9,8},{10,11... | collective-permute-start | bytes 884744 | tf_op jit(solution)/shard_map/ppermute | solution.py:58
  32.6 8.7 %collective-permute-start.3 = (bf16[1,128,1152]{2,1,0:T(8,128)(2,1)S(1)}, bf16[1,128,1152]{2,1,0:T(8,128)(2,1)S(1)}, u32[]{:S(2)}, u32[]{:S(2)}) collective-permute-start(bf16[1,128,1152]{2,1,0:T(8,128)(2,1)S(1)} %get-tuple-element.69), channel_id=1, source_target_pairs={{0,3},{1,2},{2,1},{3,0},{4,7},{5,6},{6,5},{7,4},{8,11},{9,10},{10,... | collective-permute-start | bytes 884744 | tf_op jit(solution)/shard_map/ppermute | solution.py:58
  34.8 6.8 %collective-permute-start.11 = (bf16[1,128,1152]{2,1,0:T(8,128)(2,1)S(1)}, bf16[1,128,1152]{2,1,0:T(8,128)(2,1)S(1)}, u32[]{:S(2)}, u32[]{:S(2)}) collective-permute-start(bf16[1,128,1152]{2,1,0:T(8,128)(2,1)S(1)} %get-tuple-element.76), channel_id=1, source_target_pairs={{0,1},{1,0},{2,3},{3,2},{4,5},{5,4},{6,7},{7,6},{8,9},{9,8},{10,11... | collective-permute-start | bytes 884744 | tf_op jit(solution)/shard_map/ppermute | solution.py:58
  35.4 8.4 %collective-permute-start.9 = (bf16[1,128,1152]{2,1,0:T(8,128)(2,1)S(1)}, bf16[1,128,1152]{2,1,0:T(8,128)(2,1)S(1)}, u32[]{:S(2)}, u32[]{:S(2)}) collective-permute-start(bf16[1,128,1152]{2,1,0:T(8,128)(2,1)S(1)} %get-tuple-element.74), channel_id=1, source_target_pairs={{0,3},{1,2},{2,1},{3,0},{4,7},{5,6},{6,5},{7,4},{8,11},{9,10},{10,... | collective-permute-start | bytes 884744 | tf_op jit(solution)/shard_map/ppermute | solution.py:58
  39.4 10.3 %collective-permute-start.6 = (bf16[2,128,1152]{2,1,0:T(8,128)(2,1)S(1)}, bf16[2,128,1152]{2,1,0:T(8,128)(2,1)S(1)}, u32[]{:S(2)}, u32[]{:S(2)}) collective-permute-start(bf16[2,128,1152]{2,1,0:T(8,128)(2,1)S(1)} %fusion.1), channel_id=1, source_target_pairs={{0,3},{1,2},{2,1},{3,0},{4,7},{5,6},{6,5},{7,4},{8,11},{9,10},{10,... | collective-permute-start | bytes 1769480 | tf_op jit(solution)/shard_map/ppermute | solution.py:58
  41.5 9.1 %collective-permute-start.4 = (bf16[2,128,1152]{2,1,0:T(8,128)(2,1)S(1)}, bf16[2,128,1152]{2,1,0:T(8,128)(2,1)S(1)}, u32[]{:S(2)}, u32[]{:S(2)}) collective-permute-start(bf16[2,128,1152]{2,1,0:T(8,128)(2,1)S(1)} %fusion), channel_id=1, source_target_pairs={{0,1},{1,0},{2,3},{3,2},{4,5},{5,4},{6,7},{7,6},{8,9},{9,8},{10,11... | collective-permute-start | bytes 1769480 | tf_op jit(solution)/shard_map/ppermute | solution.py:58
  41.8 14.2 %collective-permute-start.12 = (bf16[2,128,1152]{2,1,0:T(8,128)(2,1)S(1)}, bf16[2,128,1152]{2,1,0:T(8,128)(2,1)S(1)}, u32[]{:S(2)}, u32[]{:S(2)}) collective-permute-start(bf16[2,128,1152]{2,1,0:T(8,128)(2,1)S(1)} %fusion.3), channel_id=1, source_target_pairs={{0,3},{1,2},{2,1},{3,0},{4,7},{5,6},{6,5},{7,4},{8,11},{9,10},{10,... | collective-permute-start | bytes 1769480 | tf_op jit(solution)/shard_map/ppermute | solution.py:58
  43.9 13.0 %collective-permute-start.10 = (bf16[2,128,1152]{2,1,0:T(8,128)(2,1)S(1)}, bf16[2,128,1152]{2,1,0:T(8,128)(2,1)S(1)}, u32[]{:S(2)}, u32[]{:S(2)}) collective-permute-start(bf16[2,128,1152]{2,1,0:T(8,128)(2,1)S(1)} %fusion.2), channel_id=1, source_target_pairs={{0,1},{1,0},{2,3},{3,2},{4,5},{5,4},{6,7},{7,6},{8,9},{9,8},{10,11... | collective-permute-start | bytes 1769480 | tf_op jit(solution)/shard_map/ppermute | solution.py:58
  50.8 13.0 %collective-permute-start.7 = (bf16[2,128,1152]{2,1,0:T(8,128)(2,1)S(1)}, bf16[2,128,1152]{2,1,0:T(8,128)(2,1)S(1)}, u32[]{:S(2)}, u32[]{:S(2)}) collective-permute-start(bf16[2,128,1152]{2,1,0:T(8,128)(2,1)S(1)} %add_convert_fusion.3), channel_id=1, source_target_pairs={{0,12},{1,13},{2,14},{3,15},{4,8},{5,9},{6,10},{7,11},{8,4},{9,5},... | collective-permute-start | bytes 1769480 | tf_op jit(solution)/shard_map/ppermute | solution.py:58
  57.1 13.0 %collective-permute-start.13 = (bf16[2,128,1152]{2,1,0:T(8,128)(2,1)S(1)}, bf16[2,128,1152]{2,1,0:T(8,128)(2,1)S(1)}, u32[]{:S(2)}, u32[]{:S(2)}) collective-permute-start(bf16[2,128,1152]{2,1,0:T(8,128)(2,1)S(1)} %add_convert_fusion.1), channel_id=1, source_target_pairs={{0,12},{1,13},{2,14},{3,15},{4,8},{5,9},{6,10},{7,11},{8,4},{9,5},... | collective-permute-start | bytes 1769480 | tf_op jit(solution)/shard_map/ppermute | solution.py:58
  64.0 13.7 %collective-permute-start.8 = (bf16[2,128,1152]{2,1,0:T(8,128)(2,1)S(1)}, bf16[2,128,1152]{2,1,0:T(8,128)(2,1)S(1)}, u32[]{:S(2)}, u32[]{:S(2)}) collective-permute-start(bf16[2,128,1152]{2,1,0:T(8,128)(2,1)S(1)} %add_convert_fusion.2.rest_4_), channel_id=1, source_target_pairs={{0,1},{1,0},{2,3},{3,2},{4,5},{5,4},{6,7},{7,6},{8,9},{9,8},{10,11... | collective-permute-start | bytes 1769480 | tf_op jit(solution)/shard_map/ppermute | solution.py:58
  64.0 13.5 %collective-permute-start.15 = (bf16[2,128,1152]{2,1,0:T(8,128)(2,1)S(1)}, bf16[2,128,1152]{2,1,0:T(8,128)(2,1)S(1)}, u32[]{:S(2)}, u32[]{:S(2)}) collective-permute-start(bf16[2,128,1152]{2,1,0:T(8,128)(2,1)S(1)} %add_convert_fusion.2.rest_4_), channel_id=1, source_target_pairs={{0,3},{1,2},{2,1},{3,0},{4,7},{5,6},{6,5},{7,4},{8,11},{9,10},{10,... | collective-permute-start | bytes 1769480 | tf_op jit(solution)/shard_map/ppermute | solution.py:58
  70.3 13.9 %collective-permute-start.16 = (bf16[2,128,1152]{2,1,0:T(8,128)(2,1)S(1)}, bf16[2,128,1152]{2,1,0:T(8,128)(2,1)S(1)}, u32[]{:S(2)}, u32[]{:S(2)}) collective-permute-start(bf16[2,128,1152]{2,1,0:T(8,128)(2,1)S(1)} %add_convert_fusion.rest_5_), channel_id=1, source_target_pairs={{0,3},{1,2},{2,1},{3,0},{4,7},{5,6},{6,5},{7,4},{8,11},{9,10},{10,... | collective-permute-start | bytes 1769480 | tf_op jit(solution)/shard_map/ppermute | solution.py:58
  73.7 10.6 %collective-permute-start.14 = (bf16[2,128,1152]{2,1,0:T(8,128)(2,1)S(1)}, bf16[2,128,1152]{2,1,0:T(8,128)(2,1)S(1)}, u32[]{:S(2)}, u32[]{:S(2)}) collective-permute-start(bf16[2,128,1152]{2,1,0:T(8,128)(2,1)S(1)} %add_convert_fusion.rest_5_), channel_id=1, source_target_pairs={{0,1},{1,0},{2,3},{3,2},{4,5},{5,4},{6,7},{7,6},{8,9},{9,8},{10,11... | collective-permute-start | bytes 1769480 | tf_op jit(solution)/shard_map/ppermute | solution.py:58
  77.6 12.2 %collective-permute-start.17 = (bf16[1,128,1152]{2,1,0:T(8,128)(2,1)S(1)}, bf16[1,128,1152]{2,1,0:T(8,128)(2,1)S(1)}, u32[]{:S(2)}, u32[]{:S(2)}) collective-permute-start(bf16[1,128,1152]{2,1,0:T(8,128)(2,1)S(1)} %slice.120), channel_id=1, source_target_pairs={{0,1},{1,0},{2,3},{3,2},{4,5},{5,4},{6,7},{7,6},{8,9},{9,8},{10,11... | collective-permute-start | bytes 884744 | tf_op jit(solution)/shard_map/ppermute | solution.py:58
  77.7 12.1 %collective-permute-start.18 = (bf16[1,128,1152]{2,1,0:T(8,128)(2,1)S(1)}, bf16[1,128,1152]{2,1,0:T(8,128)(2,1)S(1)}, u32[]{:S(2)}, u32[]{:S(2)}) collective-permute-start(bf16[1,128,1152]{2,1,0:T(8,128)(2,1)S(1)} %slice.121), channel_id=1, source_target_pairs={{0,3},{1,2},{2,1},{3,0},{4,7},{5,6},{6,5},{7,4},{8,11},{9,10},{10,... | collective-permute-start | bytes 884744 | tf_op jit(solution)/shard_map/ppermute | solution.py:58
  84.2 5.9 %collective-permute-start.19 = (bf16[1,128,1152]{2,1,0:T(8,128)(2,1)S(1)}, bf16[1,128,1152]{2,1,0:T(8,128)(2,1)S(1)}, u32[]{:S(2)}, u32[]{:S(2)}) collective-permute-start(bf16[1,128,1152]{2,1,0:T(8,128)(2,1)S(1)} %slice.122), channel_id=1, source_target_pairs={{0,1},{1,0},{2,3},{3,2},{4,5},{5,4},{6,7},{7,6},{8,9},{9,8},{10,11... | collective-permute-start | bytes 884744 | tf_op jit(solution)/shard_map/ppermute | solution.py:58
  84.3 7.3 %collective-permute-start.20 = (bf16[1,128,1152]{2,1,0:T(8,128)(2,1)S(1)}, bf16[1,128,1152]{2,1,0:T(8,128)(2,1)S(1)}, u32[]{:S(2)}, u32[]{:S(2)}) collective-permute-start(bf16[1,128,1152]{2,1,0:T(8,128)(2,1)S(1)} %slice.123), channel_id=1, source_target_pairs={{0,3},{1,2},{2,1},{3,0},{4,7},{5,6},{6,5},{7,4},{8,11},{9,10},{10,... | collective-permute-start | bytes 884744 | tf_op jit(solution)/shard_map/ppermute | solution.py:58
  102.2 22.6 %collective-permute-start.21 = (bf16[352,2048]{1,0:T(8,128)(2,1)}, bf16[352,2048]{1,0:T(8,128)(2,1)S(1)}, u32[]{:S(2)}, u32[]{:S(2)}) collective-permute-start(bf16[352,2048]{1,0:T(8,128)(2,1)} %shard_map.45), channel_id=1, source_target_pairs={{0,4},{1,5},{2,6},{3,7},{12,8},{13,9},{14,10},{15,11},{4,16},{5,17... | collective-permute-start | bytes 4325384 | tf_op jit(solution)/shard_map/ppermute | solution.py:58
  103.5 23.8 %collective-permute-start.22 = (bf16[352,2048]{1,0:T(8,128)(2,1)}, bf16[352,2048]{1,0:T(8,128)(2,1)}, u32[]{:S(2)}, u32[]{:S(2)}) collective-permute-start(bf16[352,2048]{1,0:T(8,128)(2,1)} %shard_map.45), channel_id=1, source_target_pairs={{16,1},{19,2},{20,5},{23,6},{24,9},{27,10},{28,13},{31,14},{17,16}... | collective-permute-start | bytes 4325384 | tf_op jit(solution)/shard_map/ppermute | solution.py:58
  121.6 6.3 %copy-start = (bf16[352,2048]{1,0:T(8,128)(2,1)}, bf16[352,2048]{1,0:T(8,128)(2,1)S(1)}, u32[]{:S(2)}) copy-start(bf16[352,2048]{1,0:T(8,128)(2,1)S(1)} %shard_map.47.own) | copy-start | bytes 4325380
  121.6 6.3 %collective-permute-start.23 = (bf16[352,2048]{1,0:T(8,128)(2,1)S(1)}, bf16[352,2048]{1,0:T(8,128)(2,1)}, u32[]{:S(2)}, u32[]{:S(2)}) collective-permute-start(bf16[352,2048]{1,0:T(8,128)(2,1)S(1)} %shard_map.47.own), channel_id=1, source_target_pairs={{16,0},{19,3},{20,4},{23,7},{24,8},{27,11},{28,12},{31,15},{4,20},... | collective-permute-start | bytes 4325384 | tf_op jit(solution)/shard_map/ppermute | solution.py:58
  124.8 2.5 %copy-start.1 = (bf16[352,2048]{1,0:T(8,128)(2,1)}, bf16[352,2048]{1,0:T(8,128)(2,1)S(1)}, u32[]{:S(2)}) copy-start(bf16[352,2048]{1,0:T(8,128)(2,1)S(1)} %collective-permute-done.21.gate_back) | copy-start | bytes 4325380

commit v4 on v3

--- a/solution.py
+++ b/solution.py
@@ -14,7 +14,8 @@
 AXES = ("section", "row", "col")
 BLOCK = 128
 PAIR = 2 * BLOCK
-TILE = 512
+TILE = 1024
+OUT_TILES = ((0, 1024), (1024, 512), (1536, 512))
 VMEM_LIMIT = 28 * 1024 * 1024
 ANY = pl.BlockSpec(memory_space=pl.ANY)
 SMEM = pl.BlockSpec(memory_space=pltpu.SMEM)
@@ -62,20 +63,28 @@
     return pltpu.CompilerParams(vmem_limit_bytes=VMEM_LIMIT)
 
 
-def fetch_wide(choice, sources, wide, sems):
+def fetches(chosen, sources, columns, sems):
+    copies = []
+    for k, parts in enumerate((sources[0:1], sources[1:2], sources[2:])):
+        first = 0
+        for n, part in enumerate(parts):
+            at = slice(first, first + part.shape[0])
+            first += part.shape[0]
+            copies.append((chosen == k, pltpu.make_async_copy(part, columns.at[at, :], sems.at[n])))
+    for wanted, copy in copies:
+        pl.when(wanted)(copy.start)
+    return copies
+
+
+def finish_fetches(copies):
+    for wanted, copy in copies:
+        pl.when(wanted)(copy.wait)
+
+
+def fetch_wide(chosen, sources, wide, sems):
     rows = sources[0].shape[1]
-    for k, source in enumerate(sources):
-
-        @pl.when(choice == k)
-        def _(source=source):
-            whole = pltpu.make_async_copy(source, wide.at[:, 0:rows], sems.at[0])
-            head = pltpu.make_async_copy(
-                source.at[:, 0 : rows // 2], wide.at[:, rows : rows + rows // 2], sems.at[1]
-            )
-            whole.start()
-            head.start()
-            whole.wait()
-            head.wait()
+    finish_fetches(fetches(chosen, sources, wide.at[:, 0:rows], sems))
+    wide[:, rows : rows + rows // 2] = wide[:, 0 : rows // 2]
 
 
 def block_pair(wide, index, span):
@@ -191,21 +200,15 @@
 
 
 def step_kernel(which, order, choice, *rest):
-    sources, lasts = rest[:-11], rest[-10:-6]
-    gram_in, (result, gram, columns, low, linear, sems) = rest[-11], rest[-6:]
+    sources, gram_in, lasts = rest[:-13], rest[-13], rest[-12:-8]
+    result, gram, columns, low, linear, ready, sems, out_sems = rest[-8:]
     rows = gram.shape[0]
     load = pltpu.make_async_copy(gram_in, gram, sems.at[0])
     load.start()
-    for k, source in enumerate(sources):
-
-        @pl.when(choice[which] == k)
-        def _(source=source):
-            fetch = pltpu.make_async_copy(source, columns, sems.at[1])
-            fetch.start()
-            fetch.wait()
-
+    fetching = fetches(choice[which], sources, columns, sems.at[pl.ds(1, 2)])
     load.wait()
     place_blocks(LAST_PLACES, order, lasts, gram)
+    finish_fetches(fetching)
 
     def multiply(t, carry):
         at = pl.ds(pl.multiple_of(t * TILE, TILE), TILE)
@@ -215,14 +218,15 @@
         return carry
 
     lax.fori_loop(0, rows // TILE, multiply, 0)
-
-    def again(t, carry):
-        at = pl.ds(pl.multiple_of(t * TILE, TILE), TILE)
+    leaving = []
+    for n, (first, width) in enumerate(OUT_TILES):
+        at = slice(first, first + width)
         value = jnp.dot(low[...], gram[:, at], preferred_element_type=jnp.float32)
-        result[:, at] = (linear[:, at] + COEF_C * value).astype(jnp.bfloat16)
-        return carry
-
-    lax.fori_loop(0, rows // TILE, again, 0)
+        ready[:, at] = (linear[:, at] + COEF_C * value).astype(jnp.bfloat16)
+        leaving.append(pltpu.make_async_copy(ready.at[:, at], result.at[:, at], out_sems.at[n]))
+        leaving[-1].start()
+    for copy in leaving:
+        copy.wait()
 
 
 def newton_step(which, order, choice, sources, gram, lasts):
@@ -231,13 +235,15 @@
         functools.partial(step_kernel, which),
         out_shape=jax.ShapeDtypeStruct((dev_cols, rows), jnp.bfloat16),
         in_specs=[SMEM, SMEM] + [ANY] * (len(sources) + 1) + [VMEM] * len(lasts),
-        out_specs=VMEM,
+        out_specs=ANY,
         scratch_shapes=[
             pltpu.VMEM((rows, rows), jnp.bfloat16),
             pltpu.VMEM((dev_cols, rows), jnp.bfloat16),
             pltpu.VMEM((dev_cols, rows), jnp.bfloat16),
             pltpu.VMEM((dev_cols, rows), jnp.float32),
-            pltpu.SemaphoreType.DMA((2,)),
+            pltpu.VMEM((dev_cols, rows), jnp.bfloat16),
+            pltpu.SemaphoreType.DMA((3,)),
+            pltpu.SemaphoreType.DMA((len(OUT_TILES),)),
         ],
         compiler_params=params(),
         cost_estimate=pl.CostEstimate(
@@ -247,28 +253,37 @@
 
 
 def token_kernel(gate_back, up_back, token):
-    token[...] = jnp.zeros_like(token)
+    token[0] = 0
 
 
 def after(*arrays):
     return pl.pallas_call(
         token_kernel,
-        out_shape=jax.ShapeDtypeStruct((8, BLOCK), jnp.float32),
+        out_shape=jax.ShapeDtypeStruct((1,), jnp.int32),
         in_specs=[ANY] * len(arrays),
-        out_specs=VMEM,
+        out_specs=SMEM,
+        compiler_params=pltpu.CompilerParams(vmem_limit_bytes=1024 * 1024),
     )(*arrays)
 
 
-def finish_kernel(pick, token, own, over, gate_back, up_back, gate_out, up_out, sems):
-    copies = [
-        (pick[n] == k, pltpu.make_async_copy(source, out, sems.at[n]))
-        for n, (back, out) in enumerate(((gate_back, gate_out), (up_back, up_out)))
-        for k, source in enumerate((own, over, back))
-    ]
-    for wanted, copy in copies:
-        pl.when(wanted)(copy.start)
-    for wanted, copy in copies:
-        pl.when(wanted)(copy.wait)
+def finish_kernel(pick, token, own, over, gate_back, up_back, gate_out, up_out, staged, sems):
+    kept = []
+    for n, (back, out) in enumerate(((gate_back, gate_out), (up_back, up_out))):
+        came = pltpu.make_async_copy(back, out, sems.at[n])
+        pl.when(pick[n] == 2)(came.start)
+        for k, source in enumerate((own, over)):
+            stage = pltpu.make_async_copy(source, staged.at[n], sems.at[2 + n])
+            pl.when(pick[n] == k)(stage.start)
+            kept.append((pick[n] == k, stage, pltpu.make_async_copy(staged.at[n], out, sems.at[n])))
+    for wanted, stage, leave in kept:
+
+        @pl.when(wanted)
+        def _(stage=stage, leave=leave):
+            stage.wait()
+            leave.start()
+
+    for n, (back, out) in enumerate(((gate_back, gate_out), (up_back, up_out))):
+        pltpu.make_async_copy(back, out, sems.at[n]).wait()
 
 
 def finish(pick, own, over, gate_back, up_back):
@@ -276,9 +291,10 @@
     return pl.pallas_call(
         finish_kernel,
         out_shape=[shape, shape],
-        in_specs=[SMEM] + [ANY] * 5,
-        out_specs=[VMEM, VMEM],
-        scratch_shapes=[pltpu.SemaphoreType.DMA((2,))],
+        in_specs=[SMEM, SMEM, ANY, ANY, VMEM, VMEM],
+        out_specs=[ANY, ANY],
+        scratch_shapes=[pltpu.VMEM((2,) + own.shape, own.dtype), pltpu.SemaphoreType.DMA((4,))],
+        compiler_params=pltpu.CompilerParams(vmem_limit_bytes=8 * 1024 * 1024),
     )(pick, after(gate_back, up_back), own, over, gate_back, up_back)
 
 

time: 133 us -> 131 us (0.985)
  Pallas kernels: 39.2 us -> 35.7 us
  waiting for transfers between devices: 37.7 us -> 39.2 us
    pallas_call x2, Pallas kernels: 21.1 us -> 19.2 us  [newton_step(): pl.pallas_call(functools.partial(step_kernel, which), out_shape=jax.Shape...]
    ppermute x24, waiting for transfers between devices: 37.7 us -> 39.2 us  [send(): return lax.ppermute(values, AXES, pairs)]
    pallas_call x2, Pallas kernels: 4.65 us -> 3.3 us  [the longest x1 2.78 us: finish(): pl.pallas_call(finish_kernel, out_shape=[shape, shape], in_specs=[SMEM, S...]
  transfers between devices with their start and end apart: 24 -> 24, of which waited for: 13 -> 14; matrix products, arithmetic and copies ran while one was open for 2% -> 1% of each run, Pallas kernels for 17% -> 17%
where the time goes in v4:
time: 131 us; the launch traced here: 130 us
  starting transfers between devices  48.8 us (37%)
  waiting for transfers between devices  39.2 us (30%)
  Pallas kernels  35.7 us (27%)
  other arithmetic  4.48 us (3%)
    ppermute x24, starting transfers between devices, send(): return lax.ppermute(values, AXES, pairs)  48.8 us
    ppermute x24, waiting for transfers between devices, send(): return lax.ppermute(values, AXES, pairs)  39.2 us
    pallas_call x2, Pallas kernels, newton_step(): pl.pallas_call(functools.partial(step_kernel, which), out_shape=jax.Shape...  19.2 us
    pallas_call x1, Pallas kernels, own_terms(): pl.pallas_call(functools.partial(own_terms_kernel, scale), out_shape=[jax...  6.36 us
    pallas_call x2, Pallas kernels, add_terms(): pl.pallas_call(functools.partial(add_terms_kernel, scale, start), out_sha...  4.7 us
    select_n x1, other arithmetic, per_device(): over = send(jnp.where(on_gate, up, gate), OVER)  3.05 us
    pallas_call x1, Pallas kernels, finish(): pl.pallas_call(finish_kernel, out_shape=[shape, shape], in_specs=[SMEM, S...  2.78 us
  transfers between devices with their start and end apart: 24, of which 14 were waited for; matrix products, arithmetic and copies ran while one was open for 1% of the time, Pallas kernels for 17%

profile of v4, /device:TPU:1, one launch (start us, length us, event | category | flops | bytes accessed | tf_op | source)
XLA Modules:
  0.0 129.5 jit_solution(15772069102374548430)
XLA Ops:
  0.6 3.0 %broadcast_select_fusion = bf16[352,2048]{1,0:T(8,128)(2,1)} fusion(pred[]{:T(512)S(6)} %eq.29, bf16[2048,352]{0,1:T(8,128)(2,1)} %param.11, bf16[2048,352]{0,1:T(8,128)(2,1)} %param.10), kind=kLoop, calls=%fused_computation | loop fusion | flops 720896 | bytes 4325377 | tf_op jit(solution)/shard_map/jit(_where)/select_n | solution.py:330
  3.7 1.3 collective-permute-start.2
  5.0 5.3 %collective-permute-start = (bf16[352,2048]{1,0:T(8,128)(2,1)}, bf16[352,2048]{1,0:T(8,128)(2,1)S(1)}, u32[]{:S(2)}, u32[]{:S(2)}) collective-permute-start(bf16[352,2048]{1,0:T(8,128)(2,1)} %bitcast.12.rest_0_), channel_id=1, source_target_pairs={{4,0},{5,1},{6,2},{7,3},{8,12},{9,13},{10,14},{11,15},{16,4},{17,5... | collective-permute-start | bytes 4325384 | tf_op jit(solution)/shard_map/ppermute | solution.py:59
  10.3 2.9 %collective-permute-start.1 = (bf16[352,2048]{1,0:T(8,128)(2,1)}, bf16[352,2048]{1,0:T(8,128)(2,1)S(1)}, u32[]{:S(2)}, u32[]{:S(2)}) collective-permute-start(bf16[352,2048]{1,0:T(8,128)(2,1)} %bitcast.13.rest_1_), channel_id=1, source_target_pairs={{1,16},{2,19},{5,20},{6,23},{9,24},{10,27},{13,28},{14,31},{16,17}... | collective-permute-start | bytes 4325384 | tf_op jit(solution)/shard_map/ppermute | solution.py:59
  13.4 6.4 %shard_map.41 = (bf16[4,128,1152]{2,1,0:T(8,128)(2,1)S(1)}, bf16[12,128,1152]{2,1,0:T(8,128)(2,1)S(1)}) custom-call(s32[8]{0:T(128)S(1)} %stack.56.order, s32[2]{0:T(128)S(1)} %pad_add_fusion.1.choice, bf16[352,2048]{1,0:T(8,128)(2,1)} %bitcast.12.rest_0_, bf16[352,2048]{1,0:T(8,128)(2,1)} %bitcast.13.rest_1_, bf16[352,2048]{1,0:T(8,128)(2,1)} %collective-permute-done.2.rest_2_), custom_call_target="tpu_custom_call" | custom-call | flops 1660944384 | bytes 20000000 | tf_op jit(solution)/shard_map/pallas_call | solution.py:119
  19.8 6.7 %collective-permute-done.rest_0_ = bf16[352,2048]{1,0:T(8,128)(2,1)S(1)} collective-permute-done((bf16[352,2048]{1,0:T(8,128)(2,1)}, bf16[352,2048]{1,0:T(8,128)(2,1)S(1)}, u32[]{:S(2)}, u32[]{:S(2)}) %collective-permute-start) | collective-permute-done | bytes 1441824 | tf_op jit(solution)/shard_map/ppermute | solution.py:59
  26.5 4.4 %collective-permute-done.1.rest_1_ = bf16[352,2048]{1,0:T(8,128)(2,1)S(1)} collective-permute-done((bf16[352,2048]{1,0:T(8,128)(2,1)}, bf16[352,2048]{1,0:T(8,128)(2,1)S(1)}, u32[]{:S(2)}, u32[]{:S(2)}) %collective-permute-start.1) | collective-permute-done | bytes 1441824 | tf_op jit(solution)/shard_map/ppermute | solution.py:59
  30.8 1.6 %shard_map.43 = (bf16[1,128,1152]{2,1,0:T(8,128)(2,1)S(1)}, bf16[1,128,1152]{2,1,0:T(8,128)(2,1)S(1)}, bf16[1,128,1152]{2,1,0:T(8,128)(2,1)S(1)}, bf16[1,128,1152]{2,1,0:T(8,128)(2,1)S(1)}) custom-call(s32[8]{0:T(128)S(1)} %stack.56.order, s32[2]{0:T(128)S(1)} %pad_add_fusion.1.choice, bf16[352,2048]{1,0:T(8,128)(2,1)S(1)} %collective-permute-done.rest_0_, ...), custom_call_target="tpu_custom_call" | custom-call | flops 415236096 | bytes 10000000 | tf_op jit(solution)/shard_map/pallas_call | solution.py:153
  32.5 0.1 collective-permute-start.5
  32.6 2.2 %collective-permute-start.3 = (bf16[1,128,1152]{2,1,0:T(8,128)(2,1)S(1)}, bf16[1,128,1152]{2,1,0:T(8,128)(2,1)S(1)}, u32[]{:S(2)}, u32[]{:S(2)}) collective-permute-start(bf16[1,128,1152]{2,1,0:T(8,128)(2,1)S(1)} %get-tuple-element.69), channel_id=1, source_target_pairs={{0,3},{1,2},{2,1},{3,0},{4,7},{5,6},{6,5},{7,4},{8,11},{9,10},{10,... | collective-permute-start | bytes 884744 | tf_op jit(solution)/shard_map/ppermute | solution.py:59
  34.8 0.5 collective-permute-start.11
  35.3 0.8 collective-permute-start.9
  36.1 3.1 %shard_map.42 = (bf16[2,128,1152]{2,1,0:T(8,128)(2,1)S(1)}, bf16[2,128,1152]{2,1,0:T(8,128)(2,1)S(1)}, bf16[2,128,1152]{2,1,0:T(8,128)(2,1)S(1)}, bf16[2,128,115...) custom-call(s32[8]{0:T(128)S(1)} %stack.56.order, ...), custom_call_target="tpu_custom_call" | custom-call | flops 1245708288 | bytes 10000000 | tf_op jit(solution)/shard_map/pallas_call | solution.py:153
  39.2 0.1 fusion.1
  39.3 2.0 %collective-permute-start.6 = (bf16[2,128,1152]{2,1,0:T(8,128)(2,1)S(1)}, bf16[2,128,1152]{2,1,0:T(8,128)(2,1)S(1)}, u32[]{:S(2)}, u32[]{:S(2)}) collective-permute-start(bf16[2,128,1152]{2,1,0:T(8,128)(2,1)S(1)} %fusion.1), channel_id=1, source_target_pairs={{0,3},{1,2},{2,1},{3,0},{4,7},{5,6},{6,5},{7,4},{8,11},{9,10},{10,... | collective-permute-start | bytes 1769480 | tf_op jit(solution)/shard_map/ppermute | solution.py:59
  41.3 0.1 fusion
  41.6 0.1 fusion.3
  41.7 2.0 %collective-permute-start.12 = (bf16[2,128,1152]{2,1,0:T(8,128)(2,1)S(1)}, bf16[2,128,1152]{2,1,0:T(8,128)(2,1)S(1)}, u32[]{:S(2)}, u32[]{:S(2)}) collective-permute-start(bf16[2,128,1152]{2,1,0:T(8,128)(2,1)S(1)} %fusion.3), channel_id=1, source_target_pairs={{0,3},{1,2},{2,1},{3,0},{4,7},{5,6},{6,5},{7,4},{8,11},{9,10},{10,... | collective-permute-start | bytes 1769480 | tf_op jit(solution)/shard_map/ppermute | solution.py:59
  43.7 0.1 fusion.2
  44.0 5.7 %collective-permute-done.6 = bf16[2,128,1152]{2,1,0:T(8,128)(2,1)S(1)} collective-permute-done((bf16[2,128,1152]{2,1,0:T(8,128)(2,1)S(1)}, bf16[2,128,1152]{2,1,0:T(8,128)(2,1)S(1)}, u32[]{:S(2)}, u32[]{:S(2)}) %collective-permute-start.6) | collective-permute-done | bytes 589856 | tf_op jit(solution)/shard_map/ppermute | solution.py:59
  49.6 0.9 collective-permute-done.4
  50.6 0.2 add_convert_fusion.3
  50.8 3.8 %collective-permute-start.7 = (bf16[2,128,1152]{2,1,0:T(8,128)(2,1)S(1)}, bf16[2,128,1152]{2,1,0:T(8,128)(2,1)S(1)}, u32[]{:S(2)}, u32[]{:S(2)}) collective-permute-start(bf16[2,128,1152]{2,1,0:T(8,128)(2,1)S(1)} %add_convert_fusion.3), channel_id=1, source_target_pairs={{0,12},{1,13},{2,14},{3,15},{4,8},{5,9},{6,10},{7,11},{8,4},{9,5},... | collective-permute-start | bytes 1769480 | tf_op jit(solution)/shard_map/ppermute | solution.py:59
  54.6 1.3 %collective-permute-done.12 = bf16[2,128,1152]{2,1,0:T(8,128)(2,1)S(1)} collective-permute-done((bf16[2,128,1152]{2,1,0:T(8,128)(2,1)S(1)}, bf16[2,128,1152]{2,1,0:T(8,128)(2,1)S(1)}, u32[]{:S(2)}, u32[]{:S(2)}) %collective-permute-start.12) | collective-permute-done | bytes 589856 | tf_op jit(solution)/shard_map/ppermute | solution.py:59
  56.0 0.9 collective-permute-done.10
  56.9 0.2 add_convert_fusion.1
  57.1 3.8 %collective-permute-start.13 = (bf16[2,128,1152]{2,1,0:T(8,128)(2,1)S(1)}, bf16[2,128,1152]{2,1,0:T(8,128)(2,1)S(1)}, u32[]{:S(2)}, u32[]{:S(2)}) collective-permute-start(bf16[2,128,1152]{2,1,0:T(8,128)(2,1)S(1)} %add_convert_fusion.1), channel_id=1, source_target_pairs={{0,12},{1,13},{2,14},{3,15},{4,8},{5,9},{6,10},{7,11},{8,4},{9,5},... | collective-permute-start | bytes 1769480 | tf_op jit(solution)/shard_map/ppermute | solution.py:59
  60.9 2.8 %collective-permute-done.7 = bf16[2,128,1152]{2,1,0:T(8,128)(2,1)S(1)} collective-permute-done((bf16[2,128,1152]{2,1,0:T(8,128)(2,1)S(1)}, bf16[2,128,1152]{2,1,0:T(8,128)(2,1)S(1)}, u32[]{:S(2)}, u32[]{:S(2)}) %collective-permute-start.7) | collective-permute-done | bytes 589856 | tf_op jit(solution)/shard_map/ppermute | solution.py:59
  63.8 0.1 add_convert_fusion.2.rest_4_
  64.0 2.6 %collective-permute-start.15 = (bf16[2,128,1152]{2,1,0:T(8,128)(2,1)S(1)}, bf16[2,128,1152]{2,1,0:T(8,128)(2,1)S(1)}, u32[]{:S(2)}, u32[]{:S(2)}) collective-permute-start(bf16[2,128,1152]{2,1,0:T(8,128)(2,1)S(1)} %add_convert_fusion.2.rest_4_), channel_id=1, source_target_pairs={{0,3},{1,2},{2,1},{3,0},{4,7},{5,6},{6,5},{7,4},{8,11},{9,10},{10,... | collective-permute-start | bytes 1769480 | tf_op jit(solution)/shard_map/ppermute | solution.py:59
  66.7 3.4 %collective-permute-done.13 = bf16[2,128,1152]{2,1,0:T(8,128)(2,1)S(1)} collective-permute-done((bf16[2,128,1152]{2,1,0:T(8,128)(2,1)S(1)}, bf16[2,128,1152]{2,1,0:T(8,128)(2,1)S(1)}, u32[]{:S(2)}, u32[]{:S(2)}) %collective-permute-start.13) | collective-permute-done | bytes 589856 | tf_op jit(solution)/shard_map/ppermute | solution.py:59
  70.1 0.2 add_convert_fusion.rest_5_
  70.2 3.5 %collective-permute-start.16 = (bf16[2,128,1152]{2,1,0:T(8,128)(2,1)S(1)}, bf16[2,128,1152]{2,1,0:T(8,128)(2,1)S(1)}, u32[]{:S(2)}, u32[]{:S(2)}) collective-permute-start(bf16[2,128,1152]{2,1,0:T(8,128)(2,1)S(1)} %add_convert_fusion.rest_5_), channel_id=1, source_target_pairs={{0,3},{1,2},{2,1},{3,0},{4,7},{5,6},{6,5},{7,4},{8,11},{9,10},{10,... | collective-permute-start | bytes 1769480 | tf_op jit(solution)/shard_map/ppermute | solution.py:59
  73.7 3.8 %collective-permute-done.15.rest_2_ = bf16[2,128,1152]{2,1,0:T(8,128)(2,1)S(1)} collective-permute-done((bf16[2,128,1152]{2,1,0:T(8,128)(2,1)S(1)}, bf16[2,128,1152]{2,1,0:T(8,128)(2,1)S(1)}, u32[]{:S(2)}, u32[]{:S(2)}) %collective-permute-start.15) | collective-permute-done | bytes 589856 | tf_op jit(solution)/shard_map/ppermute | solution.py:59
  77.7 3.0 %collective-permute-start.18 = (bf16[1,128,1152]{2,1,0:T(8,128)(2,1)S(1)}, bf16[1,128,1152]{2,1,0:T(8,128)(2,1)S(1)}, u32[]{:S(2)}, u32[]{:S(2)}) collective-permute-start(bf16[1,128,1152]{2,1,0:T(8,128)(2,1)S(1)} %slice.121), channel_id=1, source_target_pairs={{0,3},{1,2},{2,1},{3,0},{4,7},{5,6},{6,5},{7,4},{8,11},{9,10},{10,... | collective-permute-start | bytes 884744 | tf_op jit(solution)/shard_map/ppermute | solution.py:59
  80.8 3.4 %collective-permute-done.16.rest_3_ = bf16[2,128,1152]{2,1,0:T(8,128)(2,1)S(1)} collective-permute-done((bf16[2,128,1152]{2,1,0:T(8,128)(2,1)S(1)}, bf16[2,128,1152]{2,1,0:T(8,128)(2,1)S(1)}, u32[]{:S(2)}, u32[]{:S(2)}) %collective-permute-start.16) | collective-permute-done | bytes 589856 | tf_op jit(solution)/shard_map/ppermute | solution.py:59
  84.3 3.2 %collective-permute-start.20 = (bf16[1,128,1152]{2,1,0:T(8,128)(2,1)S(1)}, bf16[1,128,1152]{2,1,0:T(8,128)(2,1)S(1)}, u32[]{:S(2)}, u32[]{:S(2)}) collective-permute-start(bf16[1,128,1152]{2,1,0:T(8,128)(2,1)S(1)} %slice.123), channel_id=1, source_target_pairs={{0,3},{1,2},{2,1},{3,0},{4,7},{5,6},{6,5},{7,4},{8,11},{9,10},{10,... | collective-permute-start | bytes 884744 | tf_op jit(solution)/shard_map/ppermute | solution.py:59
  87.6 2.2 %shard_map.44.rest_2_.rest_3_ = bf16[2048,2048]{1,0:T(8,128)(2,1)S(1)} custom-call(s32[8]{0:T(128)S(1)} %stack.56.order, bf16[2,128,1152]{2,1,0:T(8,128)(2,1)S(1)} %collective-permute-done.8.rest_0_, bf16[2,128,1152]{2,1,0:T(8,128)(2,1)S(1)} %collective-permute-done.14.rest_1_, bf16[2,128,1152]{2,1,0:T(8,128)(2,1)S(1)} %collective-permute-done.15.rest_2_, ...), custom_call_target="tpu_custom_call" | custom-call | bytes 20000000 | tf_op jit(solution)/shard_map/pallas_call | solution.py:189
  89.8 0.4 collective-permute-done.19.rest_5_.rest_6_
  90.2 1.5 %collective-permute-done.20.rest_6_.rest_7_ = bf16[1,128,1152]{2,1,0:T(8,128)(2,1)S(1)} collective-permute-done((bf16[1,128,1152]{2,1,0:T(8,128)(2,1)S(1)}, bf16[1,128,1152]{2,1,0:T(8,128)(2,1)S(1)}, u32[]{:S(2)}, u32[]{:S(2)}) %collective-permute-start.20) | collective-permute-done | bytes 294944 | tf_op jit(solution)/shard_map/ppermute | solution.py:59
  91.7 9.3 %shard_map.45 = bf16[352,2048]{1,0:T(8,128)(2,1)} custom-call(s32[8]{0:T(128)S(1)} %stack.56.order, s32[2]{0:T(128)S(1)} %pad_add_fusion.1.choice, bf16[352,2048]{1,0:T(8,128)(2,1)S(1)} %collective-permute-done.rest_0_, bf16[352,2048]{1,0:T(8,128)(2,1)S(1)} %collective-permute-done.1.rest_1_, bf16[2048,2048]{1,0:T(8,128)(2,1)S(1)} %shard_map.44.rest_2_.rest_3_, ...), custom_call_target="tpu_custom_call" | custom-call | flops 5905580032 | bytes 12000000 | tf_op jit(solution)/shard_map/pallas_call | solution.py:234
  101.0 1.3 collective-permute-start.21
  102.3 7.5 %collective-permute-start.22 = (bf16[352,2048]{1,0:T(8,128)(2,1)}, bf16[352,2048]{1,0:T(8,128)(2,1)S(1)}, u32[]{:S(2)}, u32[]{:S(2)}) collective-permute-start(bf16[352,2048]{1,0:T(8,128)(2,1)} %shard_map.45), channel_id=1, source_target_pairs={{16,1},{19,2},{20,5},{23,6},{24,9},{27,10},{28,13},{31,14},{17,16}... | collective-permute-start | bytes 4325384 | tf_op jit(solution)/shard_map/ppermute | solution.py:59
  109.8 9.9 %shard_map.47.own = bf16[352,2048]{1,0:T(8,128)(2,1)} custom-call(s32[8]{0:T(128)S(1)} %stack.56.order, s32[2]{0:T(128)S(1)} %pad_add_fusion.1.choice, bf16[352,2048]{1,0:T(8,128)(2,1)} %bitcast.12.rest_0_, bf16[352,2048]{1,0:T(8,128)(2,1)} %bitcast.13.rest_1_, bf16[352,2048]{1,0:T(8,128)(2,1)} %collective-permute-done.2.rest_2_, ...), custom_call_target="tpu_custom_call" | custom-call | flops 5905580032 | bytes 12000000 | tf_op jit(solution)/shard_map/pallas_call | solution.py:234
  119.6 2.4 %collective-permute-start.23 = (bf16[352,2048]{1,0:T(8,128)(2,1)}, bf16[352,2048]{1,0:T(8,128)(2,1)}, u32[]{:S(2)}, u32[]{:S(2)}) collective-permute-start(bf16[352,2048]{1,0:T(8,128)(2,1)} %shard_map.47.own), channel_id=1, source_target_pairs={{16,0},{19,3},{20,4},{23,7},{24,8},{27,11},{28,12},{31,15},{4,20},... | collective-permute-start | bytes 4325384 | tf_op jit(solution)/shard_map/ppermute | solution.py:59
  122.2 3.9 %collective-permute-done.22.up_back = bf16[352,2048]{1,0:T(8,128)(2,1)S(1)} collective-permute-done((bf16[352,2048]{1,0:T(8,128)(2,1)}, bf16[352,2048]{1,0:T(8,128)(2,1)S(1)}, u32[]{:S(2)}, u32[]{:S(2)}) %collective-permute-start.22) | collective-permute-done | bytes 1441824 | tf_op jit(solution)/shard_map/ppermute | solution.py:59
  126.0 0.5 shard_map.46.token
  126.6 2.8 %shard_map.48 = (bf16[352,2048]{1,0:T(8,128)(2,1)}, bf16[352,2048]{1,0:T(8,128)(2,1)}) custom-call(s32[2]{0:T(128)S(1)} %pad_add_fusion.pick, s32[1]{0:T(128)} %shard_map.46.token, bf16[352,2048]{1,0:T(8,128)(2,1)} %shard_map.47.own, bf16[352,2048]{1,0:T(8,128)(2,1)} %collective-permute-done.23.over, ...), custom_call_target="tpu_custom_call" | custom-call | tf_op jit(solution)/shard_map/pallas_call | solution.py:291
  (24 shorter events, 0.8 us)
Async XLA Ops:
  3.7 9.7 %collective-permute-start.2 = (bf16[352,2048]{1,0:T(8,128)(2,1)}, bf16[352,2048]{1,0:T(8,128)(2,1)}, u32[]{:S(2)}, u32[]{:S(2)}) collective-permute-start(bf16[352,2048]{1,0:T(8,128)(2,1)} %broadcast_select_fusion), channel_id=1, source_target_pairs={{0,16},{3,19},{4,20},{7,23},{8,24},{11,27},{12,28},{15,31},{20,4},... | collective-permute-start | bytes 4325384 | tf_op jit(solution)/shard_map/ppermute | solution.py:59
  5.0 21.5 %collective-permute-start = (bf16[352,2048]{1,0:T(8,128)(2,1)}, bf16[352,2048]{1,0:T(8,128)(2,1)S(1)}, u32[]{:S(2)}, u32[]{:S(2)}) collective-permute-start(bf16[352,2048]{1,0:T(8,128)(2,1)} %bitcast.12.rest_0_), channel_id=1, source_target_pairs={{4,0},{5,1},{6,2},{7,3},{8,12},{9,13},{10,14},{11,15},{16,4},{17,5... | collective-permute-start | bytes 4325384 | tf_op jit(solution)/shard_map/ppermute | solution.py:59
  10.3 20.5 %collective-permute-start.1 = (bf16[352,2048]{1,0:T(8,128)(2,1)}, bf16[352,2048]{1,0:T(8,128)(2,1)S(1)}, u32[]{:S(2)}, u32[]{:S(2)}) collective-permute-start(bf16[352,2048]{1,0:T(8,128)(2,1)} %bitcast.13.rest_1_), channel_id=1, source_target_pairs={{1,16},{2,19},{5,20},{6,23},{9,24},{10,27},{13,28},{14,31},{16,17}... | collective-permute-start | bytes 4325384 | tf_op jit(solution)/shard_map/ppermute | solution.py:59
  32.5 6.7 %collective-permute-start.5 = (bf16[1,128,1152]{2,1,0:T(8,128)(2,1)S(1)}, bf16[1,128,1152]{2,1,0:T(8,128)(2,1)S(1)}, u32[]{:S(2)}, u32[]{:S(2)}) collective-permute-start(bf16[1,128,1152]{2,1,0:T(8,128)(2,1)S(1)} %get-tuple-element.71), channel_id=1, source_target_pairs={{0,1},{1,0},{2,3},{3,2},{4,5},{5,4},{6,7},{7,6},{8,9},{9,8},{10,11... | collective-permute-start | bytes 884744 | tf_op jit(solution)/shard_map/ppermute | solution.py:59
  32.6 8.7 %collective-permute-start.3 = (bf16[1,128,1152]{2,1,0:T(8,128)(2,1)S(1)}, bf16[1,128,1152]{2,1,0:T(8,128)(2,1)S(1)}, u32[]{:S(2)}, u32[]{:S(2)}) collective-permute-start(bf16[1,128,1152]{2,1,0:T(8,128)(2,1)S(1)} %get-tuple-element.69), channel_id=1, source_target_pairs={{0,3},{1,2},{2,1},{3,0},{4,7},{5,6},{6,5},{7,4},{8,11},{9,10},{10,... | collective-permute-start | bytes 884744 | tf_op jit(solution)/shard_map/ppermute | solution.py:59
  34.8 6.8 %collective-permute-start.11 = (bf16[1,128,1152]{2,1,0:T(8,128)(2,1)S(1)}, bf16[1,128,1152]{2,1,0:T(8,128)(2,1)S(1)}, u32[]{:S(2)}, u32[]{:S(2)}) collective-permute-start(bf16[1,128,1152]{2,1,0:T(8,128)(2,1)S(1)} %get-tuple-element.76), channel_id=1, source_target_pairs={{0,1},{1,0},{2,3},{3,2},{4,5},{5,4},{6,7},{7,6},{8,9},{9,8},{10,11... | collective-permute-start | bytes 884744 | tf_op jit(solution)/shard_map/ppermute | solution.py:59
  35.3 8.4 %collective-permute-start.9 = (bf16[1,128,1152]{2,1,0:T(8,128)(2,1)S(1)}, bf16[1,128,1152]{2,1,0:T(8,128)(2,1)S(1)}, u32[]{:S(2)}, u32[]{:S(2)}) collective-permute-start(bf16[1,128,1152]{2,1,0:T(8,128)(2,1)S(1)} %get-tuple-element.74), channel_id=1, source_target_pairs={{0,3},{1,2},{2,1},{3,0},{4,7},{5,6},{6,5},{7,4},{8,11},{9,10},{10,... | collective-permute-start | bytes 884744 | tf_op jit(solution)/shard_map/ppermute | solution.py:59
  39.3 10.3 %collective-permute-start.6 = (bf16[2,128,1152]{2,1,0:T(8,128)(2,1)S(1)}, bf16[2,128,1152]{2,1,0:T(8,128)(2,1)S(1)}, u32[]{:S(2)}, u32[]{:S(2)}) collective-permute-start(bf16[2,128,1152]{2,1,0:T(8,128)(2,1)S(1)} %fusion.1), channel_id=1, source_target_pairs={{0,3},{1,2},{2,1},{3,0},{4,7},{5,6},{6,5},{7,4},{8,11},{9,10},{10,... | collective-permute-start | bytes 1769480 | tf_op jit(solution)/shard_map/ppermute | solution.py:59
  41.5 9.1 %collective-permute-start.4 = (bf16[2,128,1152]{2,1,0:T(8,128)(2,1)S(1)}, bf16[2,128,1152]{2,1,0:T(8,128)(2,1)S(1)}, u32[]{:S(2)}, u32[]{:S(2)}) collective-permute-start(bf16[2,128,1152]{2,1,0:T(8,128)(2,1)S(1)} %fusion), channel_id=1, source_target_pairs={{0,1},{1,0},{2,3},{3,2},{4,5},{5,4},{6,7},{7,6},{8,9},{9,8},{10,11... | collective-permute-start | bytes 1769480 | tf_op jit(solution)/shard_map/ppermute | solution.py:59
  41.7 14.2 %collective-permute-start.12 = (bf16[2,128,1152]{2,1,0:T(8,128)(2,1)S(1)}, bf16[2,128,1152]{2,1,0:T(8,128)(2,1)S(1)}, u32[]{:S(2)}, u32[]{:S(2)}) collective-permute-start(bf16[2,128,1152]{2,1,0:T(8,128)(2,1)S(1)} %fusion.3), channel_id=1, source_target_pairs={{0,3},{1,2},{2,1},{3,0},{4,7},{5,6},{6,5},{7,4},{8,11},{9,10},{10,... | collective-permute-start | bytes 1769480 | tf_op jit(solution)/shard_map/ppermute | solution.py:59
  43.9 13.0 %collective-permute-start.10 = (bf16[2,128,1152]{2,1,0:T(8,128)(2,1)S(1)}, bf16[2,128,1152]{2,1,0:T(8,128)(2,1)S(1)}, u32[]{:S(2)}, u32[]{:S(2)}) collective-permute-start(bf16[2,128,1152]{2,1,0:T(8,128)(2,1)S(1)} %fusion.2), channel_id=1, source_target_pairs={{0,1},{1,0},{2,3},{3,2},{4,5},{5,4},{6,7},{7,6},{8,9},{9,8},{10,11... | collective-permute-start | bytes 1769480 | tf_op jit(solution)/shard_map/ppermute | solution.py:59
  50.8 13.0 %collective-permute-start.7 = (bf16[2,128,1152]{2,1,0:T(8,128)(2,1)S(1)}, bf16[2,128,1152]{2,1,0:T(8,128)(2,1)S(1)}, u32[]{:S(2)}, u32[]{:S(2)}) collective-permute-start(bf16[2,128,1152]{2,1,0:T(8,128)(2,1)S(1)} %add_convert_fusion.3), channel_id=1, source_target_pairs={{0,12},{1,13},{2,14},{3,15},{4,8},{5,9},{6,10},{7,11},{8,4},{9,5},... | collective-permute-start | bytes 1769480 | tf_op jit(solution)/shard_map/ppermute | solution.py:59
  57.1 13.0 %collective-permute-start.13 = (bf16[2,128,1152]{2,1,0:T(8,128)(2,1)S(1)}, bf16[2,128,1152]{2,1,0:T(8,128)(2,1)S(1)}, u32[]{:S(2)}, u32[]{:S(2)}) collective-permute-start(bf16[2,128,1152]{2,1,0:T(8,128)(2,1)S(1)} %add_convert_fusion.1), channel_id=1, source_target_pairs={{0,12},{1,13},{2,14},{3,15},{4,8},{5,9},{6,10},{7,11},{8,4},{9,5},... | collective-permute-start | bytes 1769480 | tf_op jit(solution)/shard_map/ppermute | solution.py:59
  63.9 13.8 %collective-permute-start.8 = (bf16[2,128,1152]{2,1,0:T(8,128)(2,1)S(1)}, bf16[2,128,1152]{2,1,0:T(8,128)(2,1)S(1)}, u32[]{:S(2)}, u32[]{:S(2)}) collective-permute-start(bf16[2,128,1152]{2,1,0:T(8,128)(2,1)S(1)} %add_convert_fusion.2.rest_4_), channel_id=1, source_target_pairs={{0,1},{1,0},{2,3},{3,2},{4,5},{5,4},{6,7},{7,6},{8,9},{9,8},{10,11... | collective-permute-start | bytes 1769480 | tf_op jit(solution)/shard_map/ppermute | solution.py:59
  64.0 13.6 %collective-permute-start.15 = (bf16[2,128,1152]{2,1,0:T(8,128)(2,1)S(1)}, bf16[2,128,1152]{2,1,0:T(8,128)(2,1)S(1)}, u32[]{:S(2)}, u32[]{:S(2)}) collective-permute-start(bf16[2,128,1152]{2,1,0:T(8,128)(2,1)S(1)} %add_convert_fusion.2.rest_4_), channel_id=1, source_target_pairs={{0,3},{1,2},{2,1},{3,0},{4,7},{5,6},{6,5},{7,4},{8,11},{9,10},{10,... | collective-permute-start | bytes 1769480 | tf_op jit(solution)/shard_map/ppermute | solution.py:59
  70.2 13.9 %collective-permute-start.16 = (bf16[2,128,1152]{2,1,0:T(8,128)(2,1)S(1)}, bf16[2,128,1152]{2,1,0:T(8,128)(2,1)S(1)}, u32[]{:S(2)}, u32[]{:S(2)}) collective-permute-start(bf16[2,128,1152]{2,1,0:T(8,128)(2,1)S(1)} %add_convert_fusion.rest_5_), channel_id=1, source_target_pairs={{0,3},{1,2},{2,1},{3,0},{4,7},{5,6},{6,5},{7,4},{8,11},{9,10},{10,... | collective-permute-start | bytes 1769480 | tf_op jit(solution)/shard_map/ppermute | solution.py:59
  73.7 10.6 %collective-permute-start.14 = (bf16[2,128,1152]{2,1,0:T(8,128)(2,1)S(1)}, bf16[2,128,1152]{2,1,0:T(8,128)(2,1)S(1)}, u32[]{:S(2)}, u32[]{:S(2)}) collective-permute-start(bf16[2,128,1152]{2,1,0:T(8,128)(2,1)S(1)} %add_convert_fusion.rest_5_), channel_id=1, source_target_pairs={{0,1},{1,0},{2,3},{3,2},{4,5},{5,4},{6,7},{7,6},{8,9},{9,8},{10,11... | collective-permute-start | bytes 1769480 | tf_op jit(solution)/shard_map/ppermute | solution.py:59
  77.6 12.2 %collective-permute-start.17 = (bf16[1,128,1152]{2,1,0:T(8,128)(2,1)S(1)}, bf16[1,128,1152]{2,1,0:T(8,128)(2,1)S(1)}, u32[]{:S(2)}, u32[]{:S(2)}) collective-permute-start(bf16[1,128,1152]{2,1,0:T(8,128)(2,1)S(1)} %slice.120), channel_id=1, source_target_pairs={{0,1},{1,0},{2,3},{3,2},{4,5},{5,4},{6,7},{7,6},{8,9},{9,8},{10,11... | collective-permute-start | bytes 884744 | tf_op jit(solution)/shard_map/ppermute | solution.py:59
  77.7 12.1 %collective-permute-start.18 = (bf16[1,128,1152]{2,1,0:T(8,128)(2,1)S(1)}, bf16[1,128,1152]{2,1,0:T(8,128)(2,1)S(1)}, u32[]{:S(2)}, u32[]{:S(2)}) collective-permute-start(bf16[1,128,1152]{2,1,0:T(8,128)(2,1)S(1)} %slice.121), channel_id=1, source_target_pairs={{0,3},{1,2},{2,1},{3,0},{4,7},{5,6},{6,5},{7,4},{8,11},{9,10},{10,... | collective-permute-start | bytes 884744 | tf_op jit(solution)/shard_map/ppermute | solution.py:59
  84.2 5.9 %collective-permute-start.19 = (bf16[1,128,1152]{2,1,0:T(8,128)(2,1)S(1)}, bf16[1,128,1152]{2,1,0:T(8,128)(2,1)S(1)}, u32[]{:S(2)}, u32[]{:S(2)}) collective-permute-start(bf16[1,128,1152]{2,1,0:T(8,128)(2,1)S(1)} %slice.122), channel_id=1, source_target_pairs={{0,1},{1,0},{2,3},{3,2},{4,5},{5,4},{6,7},{7,6},{8,9},{9,8},{10,11... | collective-permute-start | bytes 884744 | tf_op jit(solution)/shard_map/ppermute | solution.py:59
  84.3 7.3 %collective-permute-start.20 = (bf16[1,128,1152]{2,1,0:T(8,128)(2,1)S(1)}, bf16[1,128,1152]{2,1,0:T(8,128)(2,1)S(1)}, u32[]{:S(2)}, u32[]{:S(2)}) collective-permute-start(bf16[1,128,1152]{2,1,0:T(8,128)(2,1)S(1)} %slice.123), channel_id=1, source_target_pairs={{0,3},{1,2},{2,1},{3,0},{4,7},{5,6},{6,5},{7,4},{8,11},{9,10},{10,... | collective-permute-start | bytes 884744 | tf_op jit(solution)/shard_map/ppermute | solution.py:59
  101.0 21.2 %collective-permute-start.21 = (bf16[352,2048]{1,0:T(8,128)(2,1)}, bf16[352,2048]{1,0:T(8,128)(2,1)S(1)}, u32[]{:S(2)}, u32[]{:S(2)}) collective-permute-start(bf16[352,2048]{1,0:T(8,128)(2,1)} %shard_map.45), channel_id=1, source_target_pairs={{0,4},{1,5},{2,6},{3,7},{12,8},{13,9},{14,10},{15,11},{4,16},{5,17... | collective-permute-start | bytes 4325384 | tf_op jit(solution)/shard_map/ppermute | solution.py:59
  102.3 23.8 %collective-permute-start.22 = (bf16[352,2048]{1,0:T(8,128)(2,1)}, bf16[352,2048]{1,0:T(8,128)(2,1)S(1)}, u32[]{:S(2)}, u32[]{:S(2)}) collective-permute-start(bf16[352,2048]{1,0:T(8,128)(2,1)} %shard_map.45), channel_id=1, source_target_pairs={{16,1},{19,2},{20,5},{23,6},{24,9},{27,10},{28,13},{31,14},{17,16}... | collective-permute-start | bytes 4325384 | tf_op jit(solution)/shard_map/ppermute | solution.py:59
  119.6 6.9 %collective-permute-start.23 = (bf16[352,2048]{1,0:T(8,128)(2,1)}, bf16[352,2048]{1,0:T(8,128)(2,1)}, u32[]{:S(2)}, u32[]{:S(2)}) collective-permute-start(bf16[352,2048]{1,0:T(8,128)(2,1)} %shard_map.47.own), channel_id=1, source_target_pairs={{16,0},{19,3},{20,4},{23,7},{24,8},{27,11},{28,12},{31,15},{4,20},... | collective-permute-start | bytes 4325384 | tf_op jit(solution)/shard_map/ppermute | solution.py:59

commit v5 on v4

--- a/solution.py
+++ b/solution.py
@@ -16,6 +16,7 @@
 PAIR = 2 * BLOCK
 TILE = 1024
 OUT_TILES = ((0, 1024), (1024, 512), (1536, 512))
+ROW_CHUNKS = ((0, 96), (96, 96), (192, 80), (272, 80))
 VMEM_LIMIT = 28 * 1024 * 1024
 ANY = pl.BlockSpec(memory_space=pl.ANY)
 SMEM = pl.BlockSpec(memory_space=pltpu.SMEM)
@@ -127,7 +128,7 @@
         ],
         compiler_params=params(),
         cost_estimate=pl.CostEstimate(
-            flops=2 * rows * span * dev_cols, bytes_accessed=20000000, transcendentals=0
+            flops=0, bytes_accessed=1000, transcendentals=0
         ),
     )(order, choice, *sources)
 
@@ -266,24 +267,27 @@
     )(*arrays)
 
 
-def finish_kernel(pick, token, own, over, gate_back, up_back, gate_out, up_out, staged, sems):
-    kept = []
-    for n, (back, out) in enumerate(((gate_back, gate_out), (up_back, up_out))):
-        came = pltpu.make_async_copy(back, out, sems.at[n])
-        pl.when(pick[n] == 2)(came.start)
-        for k, source in enumerate((own, over)):
-            stage = pltpu.make_async_copy(source, staged.at[n], sems.at[2 + n])
-            pl.when(pick[n] == k)(stage.start)
-            kept.append((pick[n] == k, stage, pltpu.make_async_copy(staged.at[n], out, sems.at[n])))
-    for wanted, stage, leave in kept:
-
-        @pl.when(wanted)
-        def _(stage=stage, leave=leave):
-            stage.wait()
-            leave.start()
-
-    for n, (back, out) in enumerate(((gate_back, gate_out), (up_back, up_out))):
-        pltpu.make_async_copy(back, out, sems.at[n]).wait()
+def finish_kernel(pick, token, own, over, gate_back, up_back, gate_out, up_out, staged, in_sems, out_sems):
+    arrivals, departures = [], []
+    for c, (first, count) in enumerate(ROW_CHUNKS):
+        at = slice(first, first + count)
+        for n, (back, out) in enumerate(((gate_back, gate_out), (up_back, up_out))):
+            for k, source in enumerate((own, over, back)):
+                arrivals.append(
+                    (
+                        pick[n] == k,
+                        pltpu.make_async_copy(source.at[at, :], staged.at[n, at, :], in_sems.at[n, c]),
+                    )
+                )
+            departures.append(pltpu.make_async_copy(staged.at[n, at, :], out.at[at, :], out_sems.at[n, c]))
+    for wanted, copy in arrivals:
+        pl.when(wanted)(copy.start)
+    for d, copy in enumerate(departures):
+        for wanted, arrival in arrivals[3 * d : 3 * d + 3]:
+            pl.when(wanted)(arrival.wait)
+        copy.start()
+    for copy in departures:
+        copy.wait()
 
 
 def finish(pick, own, over, gate_back, up_back):
@@ -291,9 +295,13 @@
     return pl.pallas_call(
         finish_kernel,
         out_shape=[shape, shape],
-        in_specs=[SMEM, SMEM, ANY, ANY, VMEM, VMEM],
+        in_specs=[SMEM, SMEM] + [ANY] * 4,
         out_specs=[ANY, ANY],
-        scratch_shapes=[pltpu.VMEM((2,) + own.shape, own.dtype), pltpu.SemaphoreType.DMA((4,))],
+        scratch_shapes=[
+            pltpu.VMEM((2,) + own.shape, own.dtype),
+            pltpu.SemaphoreType.DMA((2, len(ROW_CHUNKS))),
+            pltpu.SemaphoreType.DMA((2, len(ROW_CHUNKS))),
+        ],
         compiler_params=pltpu.CompilerParams(vmem_limit_bytes=8 * 1024 * 1024),
     )(pick, after(gate_back, up_back), own, over, gate_back, up_back)
 
@@ -327,8 +335,8 @@
 
     gate_in = send(gate, GATE_OUT)
     up_in = send(up, UP_OUT)
-    over = send(jnp.where(on_gate, up, gate), OVER)
-    own = (gate, up, over)
+    over = jnp.where(on_gate, up, gate)
+    own = (gate, up, send(over[: dev_cols // 2], OVER), send(over[dev_cols // 2 :], OVER))
     partner = (gate_in, up_in)
     corner_terms, other_terms = own_terms(order, choice, own, scale)
 

time: 131 us -> 131 us (level)
  Pallas kernels: 35.7 us -> 39.7 us
  waiting for transfers between devices: 39.2 us -> 36.1 us
    ppermute x24 -> x25, waiting for transfers between devices: 39.2 us -> 36.1 us  [send(): return lax.ppermute(values, AXES, pairs)]
    pallas_call x2, Pallas kernels: 4.7 us -> 7.14 us  [add_terms(): pl.pallas_call(functools.partial(add_terms_kernel, scale, start), out_sha...]
    ppermute x24 -> x25, starting transfers between devices: 48.8 us -> 48.5 us  [send(): return lax.ppermute(values, AXES, pairs)]
  transfers between devices with their start and end apart: 24 -> 25, of which waited for: 14 -> 14; matrix products, arithmetic and copies ran while one was open for 1% -> 4% of each run, Pallas kernels for 17% -> 18%
where the time goes in v5:
time: 131 us; the launch traced here: 130 us
  starting transfers between devices  48.5 us (37%)
  Pallas kernels  39.7 us (30%)
  waiting for transfers between devices  36.1 us (28%)
  other arithmetic  3.39 us (3%)
  local copies, waits for them, and re-layouts  1.38 us (1%)
    ppermute x25, starting transfers between devices, send(): return lax.ppermute(values, AXES, pairs)  48.5 us
    ppermute x25, waiting for transfers between devices, send(): return lax.ppermute(values, AXES, pairs)  36.1 us
    pallas_call x2, Pallas kernels, newton_step(): pl.pallas_call(functools.partial(step_kernel, which), out_shape=jax.Shape...  19.6 us
    pallas_call x2, Pallas kernels, add_terms(): pl.pallas_call(functools.partial(add_terms_kernel, scale, start), out_sha...  7.14 us
    pallas_call x1, Pallas kernels, own_terms(): pl.pallas_call(functools.partial(own_terms_kernel, scale), out_shape=[jax...  6.33 us
    pallas_call x1, Pallas kernels, finish(): pl.pallas_call(finish_kernel, out_shape=[shape, shape], in_specs=[SMEM, S...  3.93 us
  transfers between devices with their start and end apart: 25, of which 14 were waited for; matrix products, arithmetic and copies ran while one was open for 4% of the time, Pallas kernels for 18%

profile of v5, /device:TPU:1, one launch (start us, length us, event | category | flops | bytes accessed | tf_op | source)
XLA Modules:
  0.0 130.2 jit_solution(8585023602340935752)
XLA Ops:
  0.6 5.7 %collective-permute-start = (bf16[352,2048]{1,0:T(8,128)(2,1)}, bf16[352,2048]{1,0:T(8,128)(2,1)}, u32[]{:S(2)}, u32[]{:S(2)}) collective-permute-start(bf16[352,2048]{1,0:T(8,128)(2,1)} %bitcast.18), channel_id=1, source_target_pairs={{4,0},{5,1},{6,2},{7,3},{8,12},{9,13},{10,14},{11,15},{16,4},{17,5... | collective-permute-start | bytes 4325384 | tf_op jit(solution)/shard_map/ppermute | solution.py:60
  6.4 3.5 %collective-permute-start.1 = (bf16[352,2048]{1,0:T(8,128)(2,1)}, bf16[352,2048]{1,0:T(8,128)(2,1)}, u32[]{:S(2)}, u32[]{:S(2)}) collective-permute-start(bf16[352,2048]{1,0:T(8,128)(2,1)} %bitcast.21), channel_id=1, source_target_pairs={{1,16},{2,19},{5,20},{6,23},{9,24},{10,27},{13,28},{14,31},{16,17}... | collective-permute-start | bytes 4325384 | tf_op jit(solution)/shard_map/ppermute | solution.py:60
  9.9 1.9 %broadcast_select_fusion = bf16[352,2048]{1,0:T(8,128)(2,1)S(1)} fusion(pred[]{:T(512)S(6)} %eq.29, bf16[2048,352]{0,1:T(8,128)(2,1)} %param.11, bf16[2048,352]{0,1:T(8,128)(2,1)} %param.10), kind=kLoop, calls=%fused_computation | loop fusion | flops 720896 | bytes 4325377 | tf_op jit(solution)/shard_map/jit(_where)/select_n | solution.py:338
  11.9 1.2 fusion.4
  13.1 1.4 %collective-permute-start.2 = (bf16[176,2048]{1,0:T(8,128)(2,1)}, bf16[176,2048]{1,0:T(8,128)(2,1)}, u32[]{:S(2)}, u32[]{:S(2)}) collective-permute-start(bf16[176,2048]{1,0:T(8,128)(2,1)} %get-tuple-element.81), channel_id=1, source_target_pairs={{0,16},{3,19},{4,20},{7,23},{8,24},{11,27},{12,28},{15,31},{20,4},... | collective-permute-start | bytes 2162696 | tf_op jit(solution)/shard_map/ppermute | solution.py:60
  14.5 1.3 collective-permute-start.3
  16.0 1.6 %collective-permute-done.2.rest_2_ = bf16[176,2048]{1,0:T(8,128)(2,1)} collective-permute-done((bf16[176,2048]{1,0:T(8,128)(2,1)}, bf16[176,2048]{1,0:T(8,128)(2,1)}, u32[]{:S(2)}, u32[]{:S(2)}) %collective-permute-start.2) | collective-permute-done | bytes 720928 | tf_op jit(solution)/shard_map/ppermute | solution.py:60
  17.6 2.2 %collective-permute-done.3.rest_3_ = bf16[176,2048]{1,0:T(8,128)(2,1)} collective-permute-done((bf16[176,2048]{1,0:T(8,128)(2,1)}, bf16[176,2048]{1,0:T(8,128)(2,1)}, u32[]{:S(2)}, u32[]{:S(2)}) %collective-permute-start.3) | collective-permute-done | bytes 720928 | tf_op jit(solution)/shard_map/ppermute | solution.py:60
  19.8 6.3 %shard_map.41 = (bf16[4,128,1152]{2,1,0:T(8,128)(2,1)S(1)}, bf16[12,128,1152]{2,1,0:T(8,128)(2,1)S(1)}) custom-call(s32[8]{0:T(128)S(1)} %stack.56.order, s32[2]{0:T(128)S(1)} %pad_add_fusion.1.choice, bf16[352,2048]{1,0:T(8,128)(2,1)S(1)} %bitcast.19, bf16[352,2048]{1,0:T(8,128)(2,1)S(1)} %bitcast.22, bf16[176,2048]{1,0:T(8,128)(2,1)} %collective-permute-done.2.rest_2_, ...), custom_call_target="tpu_custom_call" | custom-call | bytes 1000 | tf_op jit(solution)/shard_map/pallas_call | solution.py:120
  26.1 0.9 collective-permute-done.1.rest_1_
  27.0 2.9 %shard_map.43 = (bf16[1,128,1152]{2,1,0:T(8,128)(2,1)S(1)}, bf16[1,128,1152]{2,1,0:T(8,128)(2,1)S(1)}, bf16[1,128,1152]{2,1,0:T(8,128)(2,1)S(1)}, bf16[1,128,1152]{2,1,0:T(8,128)(2,1)S(1)}) custom-call(s32[8]{0:T(128)S(1)} %stack.56.order, s32[2]{0:T(128)S(1)} %pad_add_fusion.1.choice, bf16[352,2048]{1,0:T(8,128)(2,1)} %collective-permute-done.rest_0_, ...), custom_call_target="tpu_custom_call" | custom-call | flops 415236096 | bytes 10000000 | tf_op jit(solution)/shard_map/pallas_call | solution.py:154
  30.0 2.0 %collective-permute-start.4 = (bf16[1,128,1152]{2,1,0:T(8,128)(2,1)S(1)}, bf16[1,128,1152]{2,1,0:T(8,128)(2,1)S(1)}, u32[]{:S(2)}, u32[]{:S(2)}) collective-permute-start(bf16[1,128,1152]{2,1,0:T(8,128)(2,1)S(1)} %get-tuple-element.69), channel_id=1, source_target_pairs={{0,3},{1,2},{2,1},{3,0},{4,7},{5,6},{6,5},{7,4},{8,11},{9,10},{10,... | collective-permute-start | bytes 884744 | tf_op jit(solution)/shard_map/ppermute | solution.py:60
  31.9 0.8 collective-permute-start.12
  32.7 0.8 collective-permute-start.10
  33.5 4.3 %shard_map.42 = (bf16[2,128,1152]{2,1,0:T(8,128)(2,1)S(1)}, bf16[2,128,1152]{2,1,0:T(8,128)(2,1)S(1)}, bf16[2,128,1152]{2,1,0:T(8,128)(2,1)S(1)}, bf16[2,128,115...) custom-call(s32[8]{0:T(128)S(1)} %stack.56.order, ...), custom_call_target="tpu_custom_call" | custom-call | flops 1245708288 | bytes 10000000 | tf_op jit(solution)/shard_map/pallas_call | solution.py:154
  37.9 2.0 %collective-permute-start.7 = (bf16[2,128,1152]{2,1,0:T(8,128)(2,1)S(1)}, bf16[2,128,1152]{2,1,0:T(8,128)(2,1)S(1)}, u32[]{:S(2)}, u32[]{:S(2)}) collective-permute-start(bf16[2,128,1152]{2,1,0:T(8,128)(2,1)S(1)} %fusion.1), channel_id=1, source_target_pairs={{0,3},{1,2},{2,1},{3,0},{4,7},{5,6},{6,5},{7,4},{8,11},{9,10},{10,... | collective-permute-start | bytes 1769480 | tf_op jit(solution)/shard_map/ppermute | solution.py:60
  40.2 0.1 fusion.3
  40.3 0.8 collective-permute-start.13
  41.3 0.9 collective-permute-start.11
  42.2 6.0 %collective-permute-done.7 = bf16[2,128,1152]{2,1,0:T(8,128)(2,1)S(1)} collective-permute-done((bf16[2,128,1152]{2,1,0:T(8,128)(2,1)S(1)}, bf16[2,128,1152]{2,1,0:T(8,128)(2,1)S(1)}, u32[]{:S(2)}, u32[]{:S(2)}) %collective-permute-start.7) | collective-permute-done | bytes 589856 | tf_op jit(solution)/shard_map/ppermute | solution.py:60
  48.2 0.9 collective-permute-done.5
  49.2 0.2 add_convert_fusion.3
  49.4 3.8 %collective-permute-start.8 = (bf16[2,128,1152]{2,1,0:T(8,128)(2,1)S(1)}, bf16[2,128,1152]{2,1,0:T(8,128)(2,1)S(1)}, u32[]{:S(2)}, u32[]{:S(2)}) collective-permute-start(bf16[2,128,1152]{2,1,0:T(8,128)(2,1)S(1)} %add_convert_fusion.3), channel_id=1, source_target_pairs={{0,12},{1,13},{2,14},{3,15},{4,8},{5,9},{6,10},{7,11},{8,4},{9,5},... | collective-permute-start | bytes 1769480 | tf_op jit(solution)/shard_map/ppermute | solution.py:60
  53.2 1.3 %collective-permute-done.13 = bf16[2,128,1152]{2,1,0:T(8,128)(2,1)S(1)} collective-permute-done((bf16[2,128,1152]{2,1,0:T(8,128)(2,1)S(1)}, bf16[2,128,1152]{2,1,0:T(8,128)(2,1)S(1)}, u32[]{:S(2)}, u32[]{:S(2)}) %collective-permute-start.13) | collective-permute-done | bytes 589856 | tf_op jit(solution)/shard_map/ppermute | solution.py:60
  54.6 0.9 collective-permute-done.11
  55.5 0.2 add_convert_fusion.1
  55.7 3.8 %collective-permute-start.14 = (bf16[2,128,1152]{2,1,0:T(8,128)(2,1)S(1)}, bf16[2,128,1152]{2,1,0:T(8,128)(2,1)S(1)}, u32[]{:S(2)}, u32[]{:S(2)}) collective-permute-start(bf16[2,128,1152]{2,1,0:T(8,128)(2,1)S(1)} %add_convert_fusion.1), channel_id=1, source_target_pairs={{0,12},{1,13},{2,14},{3,15},{4,8},{5,9},{6,10},{7,11},{8,4},{9,5},... | collective-permute-start | bytes 1769480 | tf_op jit(solution)/shard_map/ppermute | solution.py:60
  59.5 2.7 %collective-permute-done.8 = bf16[2,128,1152]{2,1,0:T(8,128)(2,1)S(1)} collective-permute-done((bf16[2,128,1152]{2,1,0:T(8,128)(2,1)S(1)}, bf16[2,128,1152]{2,1,0:T(8,128)(2,1)S(1)}, u32[]{:S(2)}, u32[]{:S(2)}) %collective-permute-start.8) | collective-permute-done | bytes 589856 | tf_op jit(solution)/shard_map/ppermute | solution.py:60
  62.3 0.1 add_convert_fusion.2.rest_4_
  62.5 2.0 %collective-permute-start.16 = (bf16[2,128,1152]{2,1,0:T(8,128)(2,1)S(1)}, bf16[2,128,1152]{2,1,0:T(8,128)(2,1)S(1)}, u32[]{:S(2)}, u32[]{:S(2)}) collective-permute-start(bf16[2,128,1152]{2,1,0:T(8,128)(2,1)S(1)} %add_convert_fusion.2.rest_4_), channel_id=1, source_target_pairs={{0,3},{1,2},{2,1},{3,0},{4,7},{5,6},{6,5},{7,4},{8,11},{9,10},{10,... | collective-permute-start | bytes 1769480 | tf_op jit(solution)/shard_map/ppermute | solution.py:60
  64.5 4.1 %collective-permute-done.14 = bf16[2,128,1152]{2,1,0:T(8,128)(2,1)S(1)} collective-permute-done((bf16[2,128,1152]{2,1,0:T(8,128)(2,1)S(1)}, bf16[2,128,1152]{2,1,0:T(8,128)(2,1)S(1)}, u32[]{:S(2)}, u32[]{:S(2)}) %collective-permute-start.14) | collective-permute-done | bytes 589856 | tf_op jit(solution)/shard_map/ppermute | solution.py:60
  68.6 0.2 add_convert_fusion.rest_5_
  68.7 2.9 %collective-permute-start.17 = (bf16[2,128,1152]{2,1,0:T(8,128)(2,1)S(1)}, bf16[2,128,1152]{2,1,0:T(8,128)(2,1)S(1)}, u32[]{:S(2)}, u32[]{:S(2)}) collective-permute-start(bf16[2,128,1152]{2,1,0:T(8,128)(2,1)S(1)} %add_convert_fusion.rest_5_), channel_id=1, source_target_pairs={{0,3},{1,2},{2,1},{3,0},{4,7},{5,6},{6,5},{7,4},{8,11},{9,10},{10,... | collective-permute-start | bytes 1769480 | tf_op jit(solution)/shard_map/ppermute | solution.py:60
  71.6 3.8 %collective-permute-done.16.rest_2_ = bf16[2,128,1152]{2,1,0:T(8,128)(2,1)S(1)} collective-permute-done((bf16[2,128,1152]{2,1,0:T(8,128)(2,1)S(1)}, bf16[2,128,1152]{2,1,0:T(8,128)(2,1)S(1)}, u32[]{:S(2)}, u32[]{:S(2)}) %collective-permute-start.16) | collective-permute-done | bytes 589856 | tf_op jit(solution)/shard_map/ppermute | solution.py:60
  75.6 2.2 %collective-permute-start.19 = (bf16[1,128,1152]{2,1,0:T(8,128)(2,1)S(1)}, bf16[1,128,1152]{2,1,0:T(8,128)(2,1)S(1)}, u32[]{:S(2)}, u32[]{:S(2)}) collective-permute-start(bf16[1,128,1152]{2,1,0:T(8,128)(2,1)S(1)} %slice.131), channel_id=1, source_target_pairs={{0,3},{1,2},{2,1},{3,0},{4,7},{5,6},{6,5},{7,4},{8,11},{9,10},{10,... | collective-permute-start | bytes 884744 | tf_op jit(solution)/shard_map/ppermute | solution.py:60
  77.8 4.2 %collective-permute-done.17.rest_3_ = bf16[2,128,1152]{2,1,0:T(8,128)(2,1)S(1)} collective-permute-done((bf16[2,128,1152]{2,1,0:T(8,128)(2,1)S(1)}, bf16[2,128,1152]{2,1,0:T(8,128)(2,1)S(1)}, u32[]{:S(2)}, u32[]{:S(2)}) %collective-permute-start.17) | collective-permute-done | bytes 589856 | tf_op jit(solution)/shard_map/ppermute | solution.py:60
  82.2 2.4 %collective-permute-start.21 = (bf16[1,128,1152]{2,1,0:T(8,128)(2,1)S(1)}, bf16[1,128,1152]{2,1,0:T(8,128)(2,1)S(1)}, u32[]{:S(2)}, u32[]{:S(2)}) collective-permute-start(bf16[1,128,1152]{2,1,0:T(8,128)(2,1)S(1)} %slice.133), channel_id=1, source_target_pairs={{0,3},{1,2},{2,1},{3,0},{4,7},{5,6},{6,5},{7,4},{8,11},{9,10},{10,... | collective-permute-start | bytes 884744 | tf_op jit(solution)/shard_map/ppermute | solution.py:60
  84.6 2.2 %shard_map.44.rest_2_.rest_4_ = bf16[2048,2048]{1,0:T(8,128)(2,1)S(1)} custom-call(s32[8]{0:T(128)S(1)} %stack.56.order, bf16[2,128,1152]{2,1,0:T(8,128)(2,1)S(1)} %collective-permute-done.9.rest_0_, bf16[2,128,1152]{2,1,0:T(8,128)(2,1)S(1)} %collective-permute-done.15.rest_1_, bf16[2,128,1152]{2,1,0:T(8,128)(2,1)S(1)} %collective-permute-done.16.rest_2_, ...), custom_call_target="tpu_custom_call" | custom-call | bytes 20000000 | tf_op jit(solution)/shard_map/pallas_call | solution.py:190
  86.9 1.2 collective-permute-done.20.rest_5_.rest_7_
  88.0 1.2 collective-permute-done.21.rest_6_.rest_8_
  89.3 9.8 %shard_map.45 = bf16[352,2048]{1,0:T(8,128)(2,1)} custom-call(s32[8]{0:T(128)S(1)} %stack.56.order, s32[2]{0:T(128)S(1)} %pad_add_fusion.1.choice, bf16[352,2048]{1,0:T(8,128)(2,1)} %collective-permute-done.rest_0_, bf16[352,2048]{1,0:T(8,128)(2,1)} %collective-permute-done.1.rest_1_, bf16[2048,2048]{1,0:T(8,128)(2,1)S(1)} %shard_map.44.rest_2_.rest_4_, ...), custom_call_target="tpu_custom_call" | custom-call | flops 5905580032 | bytes 12000000 | tf_op jit(solution)/shard_map/pallas_call | solution.py:235
  99.1 1.3 collective-permute-start.22
  100.4 9.0 %collective-permute-start.23 = (bf16[352,2048]{1,0:T(8,128)(2,1)}, bf16[352,2048]{1,0:T(8,128)(2,1)}, u32[]{:S(2)}, u32[]{:S(2)}) collective-permute-start(bf16[352,2048]{1,0:T(8,128)(2,1)} %shard_map.45), channel_id=1, source_target_pairs={{16,1},{19,2},{20,5},{23,6},{24,9},{27,10},{28,13},{31,14},{17,16}... | collective-permute-start | bytes 4325384 | tf_op jit(solution)/shard_map/ppermute | solution.py:60
  109.4 9.8 %shard_map.47.own = bf16[352,2048]{1,0:T(8,128)(2,1)} custom-call(s32[8]{0:T(128)S(1)} %stack.56.order, s32[2]{0:T(128)S(1)} %pad_add_fusion.1.choice, bf16[352,2048]{1,0:T(8,128)(2,1)S(1)} %bitcast.20, bf16[352,2048]{1,0:T(8,128)(2,1)S(1)} %bitcast.23, bf16[176,2048]{1,0:T(8,128)(2,1)} %collective-permute-done.2.rest_2_, ...), custom_call_target="tpu_custom_call" | custom-call | flops 5905580032 | bytes 12000000 | tf_op jit(solution)/shard_map/pallas_call | solution.py:235
  119.2 1.4 %collective-permute-start.24 = (bf16[352,2048]{1,0:T(8,128)(2,1)}, bf16[352,2048]{1,0:T(8,128)(2,1)S(1)}, u32[]{:S(2)}, u32[]{:S(2)}) collective-permute-start(bf16[352,2048]{1,0:T(8,128)(2,1)} %shard_map.47.own), channel_id=1, source_target_pairs={{16,0},{19,3},{20,4},{23,7},{24,8},{27,11},{28,12},{31,15},{4,20},... | collective-permute-start | bytes 4325384 | tf_op jit(solution)/shard_map/ppermute | solution.py:60
  120.7 5.0 %collective-permute-done.23.up_back = bf16[352,2048]{1,0:T(8,128)(2,1)} collective-permute-done((bf16[352,2048]{1,0:T(8,128)(2,1)}, bf16[352,2048]{1,0:T(8,128)(2,1)}, u32[]{:S(2)}, u32[]{:S(2)}) %collective-permute-start.23) | collective-permute-done | bytes 1441824 | tf_op jit(solution)/shard_map/ppermute | solution.py:60
  125.6 0.5 shard_map.46.token
  126.1 3.9 %shard_map.48 = (bf16[352,2048]{1,0:T(8,128)(2,1)}, bf16[352,2048]{1,0:T(8,128)(2,1)}) custom-call(s32[2]{0:T(128)S(1)} %pad_add_fusion.pick, s32[1]{0:T(128)} %shard_map.46.token, bf16[352,2048]{1,0:T(8,128)(2,1)} %shard_map.47.own, bf16[352,2048]{1,0:T(8,128)(2,1)S(1)} %collective-permute-done.24.over, ...), custom_call_target="tpu_custom_call" | custom-call | tf_op jit(solution)/shard_map/pallas_call | solution.py:295
  (31 shorter events, 1.2 us)
Async XLA Ops:
  0.6 25.5 %collective-permute-start = (bf16[352,2048]{1,0:T(8,128)(2,1)}, bf16[352,2048]{1,0:T(8,128)(2,1)}, u32[]{:S(2)}, u32[]{:S(2)}) collective-permute-start(bf16[352,2048]{1,0:T(8,128)(2,1)} %bitcast.18), channel_id=1, source_target_pairs={{4,0},{5,1},{6,2},{7,3},{8,12},{9,13},{10,14},{11,15},{16,4},{17,5... | collective-permute-start | bytes 4325384 | tf_op jit(solution)/shard_map/ppermute | solution.py:60
  6.4 20.6 %collective-permute-start.1 = (bf16[352,2048]{1,0:T(8,128)(2,1)}, bf16[352,2048]{1,0:T(8,128)(2,1)}, u32[]{:S(2)}, u32[]{:S(2)}) collective-permute-start(bf16[352,2048]{1,0:T(8,128)(2,1)} %bitcast.21), channel_id=1, source_target_pairs={{1,16},{2,19},{5,20},{6,23},{9,24},{10,27},{13,28},{14,31},{16,17}... | collective-permute-start | bytes 4325384 | tf_op jit(solution)/shard_map/ppermute | solution.py:60
  11.9 7.9 %copy-start = (bf16[2048,352]{0,1:T(8,128)(2,1)S(1)}, bf16[2048,352]{0,1:T(8,128)(2,1)}, u32[]{:S(2)}) copy-start(bf16[2048,352]{0,1:T(8,128)(2,1)} %param.10) | copy-start | bytes 4325380
  11.9 7.9 %copy-start.1 = (bf16[2048,352]{0,1:T(8,128)(2,1)S(1)}, bf16[2048,352]{0,1:T(8,128)(2,1)}, u32[]{:S(2)}) copy-start(bf16[2048,352]{0,1:T(8,128)(2,1)} %param.11) | copy-start | bytes 4325380
  13.1 4.5 %collective-permute-start.2 = (bf16[176,2048]{1,0:T(8,128)(2,1)}, bf16[176,2048]{1,0:T(8,128)(2,1)}, u32[]{:S(2)}, u32[]{:S(2)}) collective-permute-start(bf16[176,2048]{1,0:T(8,128)(2,1)} %get-tuple-element.81), channel_id=1, source_target_pairs={{0,16},{3,19},{4,20},{7,23},{8,24},{11,27},{12,28},{15,31},{20,4},... | collective-permute-start | bytes 2162696 | tf_op jit(solution)/shard_map/ppermute | solution.py:60
  14.5 5.3 %collective-permute-start.3 = (bf16[176,2048]{1,0:T(8,128)(2,1)}, bf16[176,2048]{1,0:T(8,128)(2,1)}, u32[]{:S(2)}, u32[]{:S(2)}) collective-permute-start(bf16[176,2048]{1,0:T(8,128)(2,1)} %get-tuple-element.80), channel_id=1, source_target_pairs={{0,16},{3,19},{4,20},{7,23},{8,24},{11,27},{12,28},{15,31},{20,4},... | collective-permute-start | bytes 2162696 | tf_op jit(solution)/shard_map/ppermute | solution.py:60
  29.9 7.9 %collective-permute-start.6 = (bf16[1,128,1152]{2,1,0:T(8,128)(2,1)S(1)}, bf16[1,128,1152]{2,1,0:T(8,128)(2,1)S(1)}, u32[]{:S(2)}, u32[]{:S(2)}) collective-permute-start(bf16[1,128,1152]{2,1,0:T(8,128)(2,1)S(1)} %get-tuple-element.71), channel_id=1, source_target_pairs={{0,1},{1,0},{2,3},{3,2},{4,5},{5,4},{6,7},{7,6},{8,9},{9,8},{10,11... | collective-permute-start | bytes 884744 | tf_op jit(solution)/shard_map/ppermute | solution.py:60
  30.0 10.0 %collective-permute-start.4 = (bf16[1,128,1152]{2,1,0:T(8,128)(2,1)S(1)}, bf16[1,128,1152]{2,1,0:T(8,128)(2,1)S(1)}, u32[]{:S(2)}, u32[]{:S(2)}) collective-permute-start(bf16[1,128,1152]{2,1,0:T(8,128)(2,1)S(1)} %get-tuple-element.69), channel_id=1, source_target_pairs={{0,3},{1,2},{2,1},{3,0},{4,7},{5,6},{6,5},{7,4},{8,11},{9,10},{10,... | collective-permute-start | bytes 884744 | tf_op jit(solution)/shard_map/ppermute | solution.py:60
  31.9 8.2 %collective-permute-start.12 = (bf16[1,128,1152]{2,1,0:T(8,128)(2,1)S(1)}, bf16[1,128,1152]{2,1,0:T(8,128)(2,1)S(1)}, u32[]{:S(2)}, u32[]{:S(2)}) collective-permute-start(bf16[1,128,1152]{2,1,0:T(8,128)(2,1)S(1)} %get-tuple-element.76), channel_id=1, source_target_pairs={{0,1},{1,0},{2,3},{3,2},{4,5},{5,4},{6,7},{7,6},{8,9},{9,8},{10,11... | collective-permute-start | bytes 884744 | tf_op jit(solution)/shard_map/ppermute | solution.py:60
  32.7 8.4 %collective-permute-start.10 = (bf16[1,128,1152]{2,1,0:T(8,128)(2,1)S(1)}, bf16[1,128,1152]{2,1,0:T(8,128)(2,1)S(1)}, u32[]{:S(2)}, u32[]{:S(2)}) collective-permute-start(bf16[1,128,1152]{2,1,0:T(8,128)(2,1)S(1)} %get-tuple-element.74), channel_id=1, source_target_pairs={{0,3},{1,2},{2,1},{3,0},{4,7},{5,6},{6,5},{7,4},{8,11},{9,10},{10,... | collective-permute-start | bytes 884744 | tf_op jit(solution)/shard_map/ppermute | solution.py:60
  37.9 10.3 %collective-permute-start.7 = (bf16[2,128,1152]{2,1,0:T(8,128)(2,1)S(1)}, bf16[2,128,1152]{2,1,0:T(8,128)(2,1)S(1)}, u32[]{:S(2)}, u32[]{:S(2)}) collective-permute-start(bf16[2,128,1152]{2,1,0:T(8,128)(2,1)S(1)} %fusion.1), channel_id=1, source_target_pairs={{0,3},{1,2},{2,1},{3,0},{4,7},{5,6},{6,5},{7,4},{8,11},{9,10},{10,... | collective-permute-start | bytes 1769480 | tf_op jit(solution)/shard_map/ppermute | solution.py:60
  40.0 9.1 %collective-permute-start.5 = (bf16[2,128,1152]{2,1,0:T(8,128)(2,1)S(1)}, bf16[2,128,1152]{2,1,0:T(8,128)(2,1)S(1)}, u32[]{:S(2)}, u32[]{:S(2)}) collective-permute-start(bf16[2,128,1152]{2,1,0:T(8,128)(2,1)S(1)} %fusion), channel_id=1, source_target_pairs={{0,1},{1,0},{2,3},{3,2},{4,5},{5,4},{6,7},{7,6},{8,9},{9,8},{10,11... | collective-permute-start | bytes 1769480 | tf_op jit(solution)/shard_map/ppermute | solution.py:60
  40.3 14.3 %collective-permute-start.13 = (bf16[2,128,1152]{2,1,0:T(8,128)(2,1)S(1)}, bf16[2,128,1152]{2,1,0:T(8,128)(2,1)S(1)}, u32[]{:S(2)}, u32[]{:S(2)}) collective-permute-start(bf16[2,128,1152]{2,1,0:T(8,128)(2,1)S(1)} %fusion.3), channel_id=1, source_target_pairs={{0,3},{1,2},{2,1},{3,0},{4,7},{5,6},{6,5},{7,4},{8,11},{9,10},{10,... | collective-permute-start | bytes 1769480 | tf_op jit(solution)/shard_map/ppermute | solution.py:60
  41.3 14.2 %collective-permute-start.11 = (bf16[2,128,1152]{2,1,0:T(8,128)(2,1)S(1)}, bf16[2,128,1152]{2,1,0:T(8,128)(2,1)S(1)}, u32[]{:S(2)}, u32[]{:S(2)}) collective-permute-start(bf16[2,128,1152]{2,1,0:T(8,128)(2,1)S(1)} %fusion.2), channel_id=1, source_target_pairs={{0,1},{1,0},{2,3},{3,2},{4,5},{5,4},{6,7},{7,6},{8,9},{9,8},{10,11... | collective-permute-start | bytes 1769480 | tf_op jit(solution)/shard_map/ppermute | solution.py:60
  49.4 12.9 %collective-permute-start.8 = (bf16[2,128,1152]{2,1,0:T(8,128)(2,1)S(1)}, bf16[2,128,1152]{2,1,0:T(8,128)(2,1)S(1)}, u32[]{:S(2)}, u32[]{:S(2)}) collective-permute-start(bf16[2,128,1152]{2,1,0:T(8,128)(2,1)S(1)} %add_convert_fusion.3), channel_id=1, source_target_pairs={{0,12},{1,13},{2,14},{3,15},{4,8},{5,9},{6,10},{7,11},{8,4},{9,5},... | collective-permute-start | bytes 1769480 | tf_op jit(solution)/shard_map/ppermute | solution.py:60
  55.7 12.9 %collective-permute-start.14 = (bf16[2,128,1152]{2,1,0:T(8,128)(2,1)S(1)}, bf16[2,128,1152]{2,1,0:T(8,128)(2,1)S(1)}, u32[]{:S(2)}, u32[]{:S(2)}) collective-permute-start(bf16[2,128,1152]{2,1,0:T(8,128)(2,1)S(1)} %add_convert_fusion.1), channel_id=1, source_target_pairs={{0,12},{1,13},{2,14},{3,15},{4,8},{5,9},{6,10},{7,11},{8,4},{9,5},... | collective-permute-start | bytes 1769480 | tf_op jit(solution)/shard_map/ppermute | solution.py:60
  62.4 13.2 %collective-permute-start.9 = (bf16[2,128,1152]{2,1,0:T(8,128)(2,1)S(1)}, bf16[2,128,1152]{2,1,0:T(8,128)(2,1)S(1)}, u32[]{:S(2)}, u32[]{:S(2)}) collective-permute-start(bf16[2,128,1152]{2,1,0:T(8,128)(2,1)S(1)} %add_convert_fusion.2.rest_4_), channel_id=1, source_target_pairs={{0,1},{1,0},{2,3},{3,2},{4,5},{5,4},{6,7},{7,6},{8,9},{9,8},{10,11... | collective-permute-start | bytes 1769480 | tf_op jit(solution)/shard_map/ppermute | solution.py:60
  62.5 12.9 %collective-permute-start.16 = (bf16[2,128,1152]{2,1,0:T(8,128)(2,1)S(1)}, bf16[2,128,1152]{2,1,0:T(8,128)(2,1)S(1)}, u32[]{:S(2)}, u32[]{:S(2)}) collective-permute-start(bf16[2,128,1152]{2,1,0:T(8,128)(2,1)S(1)} %add_convert_fusion.2.rest_4_), channel_id=1, source_target_pairs={{0,3},{1,2},{2,1},{3,0},{4,7},{5,6},{6,5},{7,4},{8,11},{9,10},{10,... | collective-permute-start | bytes 1769480 | tf_op jit(solution)/shard_map/ppermute | solution.py:60
  68.7 13.3 %collective-permute-start.17 = (bf16[2,128,1152]{2,1,0:T(8,128)(2,1)S(1)}, bf16[2,128,1152]{2,1,0:T(8,128)(2,1)S(1)}, u32[]{:S(2)}, u32[]{:S(2)}) collective-permute-start(bf16[2,128,1152]{2,1,0:T(8,128)(2,1)S(1)} %add_convert_fusion.rest_5_), channel_id=1, source_target_pairs={{0,3},{1,2},{2,1},{3,0},{4,7},{5,6},{6,5},{7,4},{8,11},{9,10},{10,... | collective-permute-start | bytes 1769480 | tf_op jit(solution)/shard_map/ppermute | solution.py:60
  71.6 10.5 %collective-permute-start.15 = (bf16[2,128,1152]{2,1,0:T(8,128)(2,1)S(1)}, bf16[2,128,1152]{2,1,0:T(8,128)(2,1)S(1)}, u32[]{:S(2)}, u32[]{:S(2)}) collective-permute-start(bf16[2,128,1152]{2,1,0:T(8,128)(2,1)S(1)} %add_convert_fusion.rest_5_), channel_id=1, source_target_pairs={{0,1},{1,0},{2,3},{3,2},{4,5},{5,4},{6,7},{7,6},{8,9},{9,8},{10,11... | collective-permute-start | bytes 1769480 | tf_op jit(solution)/shard_map/ppermute | solution.py:60
  75.5 11.4 %collective-permute-start.18 = (bf16[1,128,1152]{2,1,0:T(8,128)(2,1)S(1)}, bf16[1,128,1152]{2,1,0:T(8,128)(2,1)S(1)}, u32[]{:S(2)}, u32[]{:S(2)}) collective-permute-start(bf16[1,128,1152]{2,1,0:T(8,128)(2,1)S(1)} %slice.130), channel_id=1, source_target_pairs={{0,1},{1,0},{2,3},{3,2},{4,5},{5,4},{6,7},{7,6},{8,9},{9,8},{10,11... | collective-permute-start | bytes 884744 | tf_op jit(solution)/shard_map/ppermute | solution.py:60
  75.6 11.3 %collective-permute-start.19 = (bf16[1,128,1152]{2,1,0:T(8,128)(2,1)S(1)}, bf16[1,128,1152]{2,1,0:T(8,128)(2,1)S(1)}, u32[]{:S(2)}, u32[]{:S(2)}) collective-permute-start(bf16[1,128,1152]{2,1,0:T(8,128)(2,1)S(1)} %slice.131), channel_id=1, source_target_pairs={{0,3},{1,2},{2,1},{3,0},{4,7},{5,6},{6,5},{7,4},{8,11},{9,10},{10,... | collective-permute-start | bytes 884744 | tf_op jit(solution)/shard_map/ppermute | solution.py:60
  82.1 5.9 %collective-permute-start.20 = (bf16[1,128,1152]{2,1,0:T(8,128)(2,1)S(1)}, bf16[1,128,1152]{2,1,0:T(8,128)(2,1)S(1)}, u32[]{:S(2)}, u32[]{:S(2)}) collective-permute-start(bf16[1,128,1152]{2,1,0:T(8,128)(2,1)S(1)} %slice.132), channel_id=1, source_target_pairs={{0,1},{1,0},{2,3},{3,2},{4,5},{5,4},{6,7},{7,6},{8,9},{9,8},{10,11... | collective-permute-start | bytes 884744 | tf_op jit(solution)/shard_map/ppermute | solution.py:60
  82.2 7.0 %collective-permute-start.21 = (bf16[1,128,1152]{2,1,0:T(8,128)(2,1)S(1)}, bf16[1,128,1152]{2,1,0:T(8,128)(2,1)S(1)}, u32[]{:S(2)}, u32[]{:S(2)}) collective-permute-start(bf16[1,128,1152]{2,1,0:T(8,128)(2,1)S(1)} %slice.133), channel_id=1, source_target_pairs={{0,3},{1,2},{2,1},{3,0},{4,7},{5,6},{6,5},{7,4},{8,11},{9,10},{10,... | collective-permute-start | bytes 884744 | tf_op jit(solution)/shard_map/ppermute | solution.py:60
  99.1 21.6 %collective-permute-start.22 = (bf16[352,2048]{1,0:T(8,128)(2,1)}, bf16[352,2048]{1,0:T(8,128)(2,1)}, u32[]{:S(2)}, u32[]{:S(2)}) collective-permute-start(bf16[352,2048]{1,0:T(8,128)(2,1)} %shard_map.45), channel_id=1, source_target_pairs={{0,4},{1,5},{2,6},{3,7},{12,8},{13,9},{14,10},{15,11},{4,16},{5,17... | collective-permute-start | bytes 4325384 | tf_op jit(solution)/shard_map/ppermute | solution.py:60
  100.4 25.3 %collective-permute-start.23 = (bf16[352,2048]{1,0:T(8,128)(2,1)}, bf16[352,2048]{1,0:T(8,128)(2,1)}, u32[]{:S(2)}, u32[]{:S(2)}) collective-permute-start(bf16[352,2048]{1,0:T(8,128)(2,1)} %shard_map.45), channel_id=1, source_target_pairs={{16,1},{19,2},{20,5},{23,6},{24,9},{27,10},{28,13},{31,14},{17,16}... | collective-permute-start | bytes 4325384 | tf_op jit(solution)/shard_map/ppermute | solution.py:60
  119.2 7.0 %collective-permute-start.24 = (bf16[352,2048]{1,0:T(8,128)(2,1)}, bf16[352,2048]{1,0:T(8,128)(2,1)S(1)}, u32[]{:S(2)}, u32[]{:S(2)}) collective-permute-start(bf16[352,2048]{1,0:T(8,128)(2,1)} %shard_map.47.own), channel_id=1, source_target_pairs={{16,0},{19,3},{20,4},{23,7},{24,8},{27,11},{28,12},{31,15},{4,20},... | collective-permute-start | bytes 4325384 | tf_op jit(solution)/shard_map/ppermute | solution.py:60

commit v6 on v5

--- a/solution.py
+++ b/solution.py
@@ -14,8 +14,8 @@
 AXES = ("section", "row", "col")
 BLOCK = 128
 PAIR = 2 * BLOCK
-TILE = 1024
-OUT_TILES = ((0, 1024), (1024, 512), (1536, 512))
+TILE = 2048
+OUT_TILES = ((0, 1024), (1024, 768), (1792, 256))
 ROW_CHUNKS = ((0, 96), (96, 96), (192, 80), (272, 80))
 VMEM_LIMIT = 28 * 1024 * 1024
 ANY = pl.BlockSpec(memory_space=pl.ANY)

time: 131 us -> 131 us (level)
  no operation moved by 1% of the time
where the time goes in v6:
time: 131 us; the launch traced here: 130 us
  starting transfers between devices  48.5 us (37%)
  Pallas kernels  39.5 us (30%)
  waiting for transfers between devices  36.1 us (28%)
  other arithmetic  3.39 us (3%)
  local copies, waits for them, and re-layouts  1.38 us (1%)
    ppermute x25, starting transfers between devices, send(): return lax.ppermute(values, AXES, pairs)  48.5 us
    ppermute x25, waiting for transfers between devices, send(): return lax.ppermute(values, AXES, pairs)  36.1 us
    pallas_call x2, Pallas kernels, newton_step(): pl.pallas_call(functools.partial(step_kernel, which), out_shape=jax.Shape...  19.4 us
    pallas_call x2, Pallas kernels, add_terms(): pl.pallas_call(functools.partial(add_terms_kernel, scale, start), out_sha...  7.14 us
    pallas_call x1, Pallas kernels, own_terms(): pl.pallas_call(functools.partial(own_terms_kernel, scale), out_shape=[jax...  6.33 us
    pallas_call x1, Pallas kernels, finish(): pl.pallas_call(finish_kernel, out_shape=[shape, shape], in_specs=[SMEM, S...  3.93 us
  transfers between devices with their start and end apart: 25, of which 14 were waited for; matrix products, arithmetic and copies ran while one was open for 4% of the time, Pallas kernels for 18%

profile of v6, /device:TPU:1, one launch (start us, length us, event | category | flops | bytes accessed | tf_op | source)
XLA Modules:
  0.0 130.1 jit_solution(15868140397475839181)
XLA Ops:
  0.6 5.7 %collective-permute-start = (bf16[352,2048]{1,0:T(8,128)(2,1)}, bf16[352,2048]{1,0:T(8,128)(2,1)}, u32[]{:S(2)}, u32[]{:S(2)}) collective-permute-start(bf16[352,2048]{1,0:T(8,128)(2,1)} %bitcast.18), channel_id=1, source_target_pairs={{4,0},{5,1},{6,2},{7,3},{8,12},{9,13},{10,14},{11,15},{16,4},{17,5... | collective-permute-start | bytes 4325384 | tf_op jit(solution)/shard_map/ppermute | solution.py:60
  6.4 3.5 %collective-permute-start.1 = (bf16[352,2048]{1,0:T(8,128)(2,1)}, bf16[352,2048]{1,0:T(8,128)(2,1)}, u32[]{:S(2)}, u32[]{:S(2)}) collective-permute-start(bf16[352,2048]{1,0:T(8,128)(2,1)} %bitcast.21), channel_id=1, source_target_pairs={{1,16},{2,19},{5,20},{6,23},{9,24},{10,27},{13,28},{14,31},{16,17}... | collective-permute-start | bytes 4325384 | tf_op jit(solution)/shard_map/ppermute | solution.py:60
  9.9 1.9 %broadcast_select_fusion = bf16[352,2048]{1,0:T(8,128)(2,1)S(1)} fusion(pred[]{:T(512)S(6)} %eq.29, bf16[2048,352]{0,1:T(8,128)(2,1)} %param.11, bf16[2048,352]{0,1:T(8,128)(2,1)} %param.10), kind=kLoop, calls=%fused_computation | loop fusion | flops 720896 | bytes 4325377 | tf_op jit(solution)/shard_map/jit(_where)/select_n | solution.py:338
  11.9 1.2 fusion.4
  13.1 1.4 %collective-permute-start.2 = (bf16[176,2048]{1,0:T(8,128)(2,1)}, bf16[176,2048]{1,0:T(8,128)(2,1)}, u32[]{:S(2)}, u32[]{:S(2)}) collective-permute-start(bf16[176,2048]{1,0:T(8,128)(2,1)} %get-tuple-element.81), channel_id=1, source_target_pairs={{0,16},{3,19},{4,20},{7,23},{8,24},{11,27},{12,28},{15,31},{20,4},... | collective-permute-start | bytes 2162696 | tf_op jit(solution)/shard_map/ppermute | solution.py:60
  14.5 1.3 collective-permute-start.3
  16.0 1.6 %collective-permute-done.2.rest_2_ = bf16[176,2048]{1,0:T(8,128)(2,1)} collective-permute-done((bf16[176,2048]{1,0:T(8,128)(2,1)}, bf16[176,2048]{1,0:T(8,128)(2,1)}, u32[]{:S(2)}, u32[]{:S(2)}) %collective-permute-start.2) | collective-permute-done | bytes 720928 | tf_op jit(solution)/shard_map/ppermute | solution.py:60
  17.6 2.2 %collective-permute-done.3.rest_3_ = bf16[176,2048]{1,0:T(8,128)(2,1)} collective-permute-done((bf16[176,2048]{1,0:T(8,128)(2,1)}, bf16[176,2048]{1,0:T(8,128)(2,1)}, u32[]{:S(2)}, u32[]{:S(2)}) %collective-permute-start.3) | collective-permute-done | bytes 720928 | tf_op jit(solution)/shard_map/ppermute | solution.py:60
  19.8 6.3 %shard_map.41 = (bf16[4,128,1152]{2,1,0:T(8,128)(2,1)S(1)}, bf16[12,128,1152]{2,1,0:T(8,128)(2,1)S(1)}) custom-call(s32[8]{0:T(128)S(1)} %stack.56.order, s32[2]{0:T(128)S(1)} %pad_add_fusion.1.choice, bf16[352,2048]{1,0:T(8,128)(2,1)S(1)} %bitcast.19, bf16[352,2048]{1,0:T(8,128)(2,1)S(1)} %bitcast.22, bf16[176,2048]{1,0:T(8,128)(2,1)} %collective-permute-done.2.rest_2_, ...), custom_call_target="tpu_custom_call" | custom-call | bytes 1000 | tf_op jit(solution)/shard_map/pallas_call | solution.py:120
  26.1 0.9 collective-permute-done.1.rest_1_
  27.0 2.9 %shard_map.43 = (bf16[1,128,1152]{2,1,0:T(8,128)(2,1)S(1)}, bf16[1,128,1152]{2,1,0:T(8,128)(2,1)S(1)}, bf16[1,128,1152]{2,1,0:T(8,128)(2,1)S(1)}, bf16[1,128,1152]{2,1,0:T(8,128)(2,1)S(1)}) custom-call(s32[8]{0:T(128)S(1)} %stack.56.order, s32[2]{0:T(128)S(1)} %pad_add_fusion.1.choice, bf16[352,2048]{1,0:T(8,128)(2,1)} %collective-permute-done.rest_0_, ...), custom_call_target="tpu_custom_call" | custom-call | flops 415236096 | bytes 10000000 | tf_op jit(solution)/shard_map/pallas_call | solution.py:154
  30.0 2.0 %collective-permute-start.4 = (bf16[1,128,1152]{2,1,0:T(8,128)(2,1)S(1)}, bf16[1,128,1152]{2,1,0:T(8,128)(2,1)S(1)}, u32[]{:S(2)}, u32[]{:S(2)}) collective-permute-start(bf16[1,128,1152]{2,1,0:T(8,128)(2,1)S(1)} %get-tuple-element.69), channel_id=1, source_target_pairs={{0,3},{1,2},{2,1},{3,0},{4,7},{5,6},{6,5},{7,4},{8,11},{9,10},{10,... | collective-permute-start | bytes 884744 | tf_op jit(solution)/shard_map/ppermute | solution.py:60
  31.9 0.8 collective-permute-start.12
  32.7 0.8 collective-permute-start.10
  33.5 4.3 %shard_map.42 = (bf16[2,128,1152]{2,1,0:T(8,128)(2,1)S(1)}, bf16[2,128,1152]{2,1,0:T(8,128)(2,1)S(1)}, bf16[2,128,1152]{2,1,0:T(8,128)(2,1)S(1)}, bf16[2,128,115...) custom-call(s32[8]{0:T(128)S(1)} %stack.56.order, ...), custom_call_target="tpu_custom_call" | custom-call | flops 1245708288 | bytes 10000000 | tf_op jit(solution)/shard_map/pallas_call | solution.py:154
  37.9 2.0 %collective-permute-start.7 = (bf16[2,128,1152]{2,1,0:T(8,128)(2,1)S(1)}, bf16[2,128,1152]{2,1,0:T(8,128)(2,1)S(1)}, u32[]{:S(2)}, u32[]{:S(2)}) collective-permute-start(bf16[2,128,1152]{2,1,0:T(8,128)(2,1)S(1)} %fusion.1), channel_id=1, source_target_pairs={{0,3},{1,2},{2,1},{3,0},{4,7},{5,6},{6,5},{7,4},{8,11},{9,10},{10,... | collective-permute-start | bytes 1769480 | tf_op jit(solution)/shard_map/ppermute | solution.py:60
  40.2 0.1 fusion.3
  40.3 0.8 collective-permute-start.13
  41.3 0.9 collective-permute-start.11
  42.2 6.0 %collective-permute-done.7 = bf16[2,128,1152]{2,1,0:T(8,128)(2,1)S(1)} collective-permute-done((bf16[2,128,1152]{2,1,0:T(8,128)(2,1)S(1)}, bf16[2,128,1152]{2,1,0:T(8,128)(2,1)S(1)}, u32[]{:S(2)}, u32[]{:S(2)}) %collective-permute-start.7) | collective-permute-done | bytes 589856 | tf_op jit(solution)/shard_map/ppermute | solution.py:60
  48.2 0.9 collective-permute-done.5
  49.2 0.2 add_convert_fusion.3
  49.4 3.8 %collective-permute-start.8 = (bf16[2,128,1152]{2,1,0:T(8,128)(2,1)S(1)}, bf16[2,128,1152]{2,1,0:T(8,128)(2,1)S(1)}, u32[]{:S(2)}, u32[]{:S(2)}) collective-permute-start(bf16[2,128,1152]{2,1,0:T(8,128)(2,1)S(1)} %add_convert_fusion.3), channel_id=1, source_target_pairs={{0,12},{1,13},{2,14},{3,15},{4,8},{5,9},{6,10},{7,11},{8,4},{9,5},... | collective-permute-start | bytes 1769480 | tf_op jit(solution)/shard_map/ppermute | solution.py:60
  53.2 1.3 %collective-permute-done.13 = bf16[2,128,1152]{2,1,0:T(8,128)(2,1)S(1)} collective-permute-done((bf16[2,128,1152]{2,1,0:T(8,128)(2,1)S(1)}, bf16[2,128,1152]{2,1,0:T(8,128)(2,1)S(1)}, u32[]{:S(2)}, u32[]{:S(2)}) %collective-permute-start.13) | collective-permute-done | bytes 589856 | tf_op jit(solution)/shard_map/ppermute | solution.py:60
  54.6 0.9 collective-permute-done.11
  55.5 0.2 add_convert_fusion.1
  55.7 3.8 %collective-permute-start.14 = (bf16[2,128,1152]{2,1,0:T(8,128)(2,1)S(1)}, bf16[2,128,1152]{2,1,0:T(8,128)(2,1)S(1)}, u32[]{:S(2)}, u32[]{:S(2)}) collective-permute-start(bf16[2,128,1152]{2,1,0:T(8,128)(2,1)S(1)} %add_convert_fusion.1), channel_id=1, source_target_pairs={{0,12},{1,13},{2,14},{3,15},{4,8},{5,9},{6,10},{7,11},{8,4},{9,5},... | collective-permute-start | bytes 1769480 | tf_op jit(solution)/shard_map/ppermute | solution.py:60
  59.5 2.7 %collective-permute-done.8 = bf16[2,128,1152]{2,1,0:T(8,128)(2,1)S(1)} collective-permute-done((bf16[2,128,1152]{2,1,0:T(8,128)(2,1)S(1)}, bf16[2,128,1152]{2,1,0:T(8,128)(2,1)S(1)}, u32[]{:S(2)}, u32[]{:S(2)}) %collective-permute-start.8) | collective-permute-done | bytes 589856 | tf_op jit(solution)/shard_map/ppermute | solution.py:60
  62.3 0.1 add_convert_fusion.2.rest_4_
  62.5 2.0 %collective-permute-start.16 = (bf16[2,128,1152]{2,1,0:T(8,128)(2,1)S(1)}, bf16[2,128,1152]{2,1,0:T(8,128)(2,1)S(1)}, u32[]{:S(2)}, u32[]{:S(2)}) collective-permute-start(bf16[2,128,1152]{2,1,0:T(8,128)(2,1)S(1)} %add_convert_fusion.2.rest_4_), channel_id=1, source_target_pairs={{0,3},{1,2},{2,1},{3,0},{4,7},{5,6},{6,5},{7,4},{8,11},{9,10},{10,... | collective-permute-start | bytes 1769480 | tf_op jit(solution)/shard_map/ppermute | solution.py:60
  64.5 4.1 %collective-permute-done.14 = bf16[2,128,1152]{2,1,0:T(8,128)(2,1)S(1)} collective-permute-done((bf16[2,128,1152]{2,1,0:T(8,128)(2,1)S(1)}, bf16[2,128,1152]{2,1,0:T(8,128)(2,1)S(1)}, u32[]{:S(2)}, u32[]{:S(2)}) %collective-permute-start.14) | collective-permute-done | bytes 589856 | tf_op jit(solution)/shard_map/ppermute | solution.py:60
  68.6 0.2 add_convert_fusion.rest_5_
  68.7 2.9 %collective-permute-start.17 = (bf16[2,128,1152]{2,1,0:T(8,128)(2,1)S(1)}, bf16[2,128,1152]{2,1,0:T(8,128)(2,1)S(1)}, u32[]{:S(2)}, u32[]{:S(2)}) collective-permute-start(bf16[2,128,1152]{2,1,0:T(8,128)(2,1)S(1)} %add_convert_fusion.rest_5_), channel_id=1, source_target_pairs={{0,3},{1,2},{2,1},{3,0},{4,7},{5,6},{6,5},{7,4},{8,11},{9,10},{10,... | collective-permute-start | bytes 1769480 | tf_op jit(solution)/shard_map/ppermute | solution.py:60
  71.6 3.8 %collective-permute-done.16.rest_2_ = bf16[2,128,1152]{2,1,0:T(8,128)(2,1)S(1)} collective-permute-done((bf16[2,128,1152]{2,1,0:T(8,128)(2,1)S(1)}, bf16[2,128,1152]{2,1,0:T(8,128)(2,1)S(1)}, u32[]{:S(2)}, u32[]{:S(2)}) %collective-permute-start.16) | collective-permute-done | bytes 589856 | tf_op jit(solution)/shard_map/ppermute | solution.py:60
  75.6 2.2 %collective-permute-start.19 = (bf16[1,128,1152]{2,1,0:T(8,128)(2,1)S(1)}, bf16[1,128,1152]{2,1,0:T(8,128)(2,1)S(1)}, u32[]{:S(2)}, u32[]{:S(2)}) collective-permute-start(bf16[1,128,1152]{2,1,0:T(8,128)(2,1)S(1)} %slice.131), channel_id=1, source_target_pairs={{0,3},{1,2},{2,1},{3,0},{4,7},{5,6},{6,5},{7,4},{8,11},{9,10},{10,... | collective-permute-start | bytes 884744 | tf_op jit(solution)/shard_map/ppermute | solution.py:60
  77.8 4.2 %collective-permute-done.17.rest_3_ = bf16[2,128,1152]{2,1,0:T(8,128)(2,1)S(1)} collective-permute-done((bf16[2,128,1152]{2,1,0:T(8,128)(2,1)S(1)}, bf16[2,128,1152]{2,1,0:T(8,128)(2,1)S(1)}, u32[]{:S(2)}, u32[]{:S(2)}) %collective-permute-start.17) | collective-permute-done | bytes 589856 | tf_op jit(solution)/shard_map/ppermute | solution.py:60
  82.2 2.4 %collective-permute-start.21 = (bf16[1,128,1152]{2,1,0:T(8,128)(2,1)S(1)}, bf16[1,128,1152]{2,1,0:T(8,128)(2,1)S(1)}, u32[]{:S(2)}, u32[]{:S(2)}) collective-permute-start(bf16[1,128,1152]{2,1,0:T(8,128)(2,1)S(1)} %slice.133), channel_id=1, source_target_pairs={{0,3},{1,2},{2,1},{3,0},{4,7},{5,6},{6,5},{7,4},{8,11},{9,10},{10,... | collective-permute-start | bytes 884744 | tf_op jit(solution)/shard_map/ppermute | solution.py:60
  84.6 2.2 %shard_map.44.rest_2_.rest_4_ = bf16[2048,2048]{1,0:T(8,128)(2,1)S(1)} custom-call(s32[8]{0:T(128)S(1)} %stack.56.order, bf16[2,128,1152]{2,1,0:T(8,128)(2,1)S(1)} %collective-permute-done.9.rest_0_, bf16[2,128,1152]{2,1,0:T(8,128)(2,1)S(1)} %collective-permute-done.15.rest_1_, bf16[2,128,1152]{2,1,0:T(8,128)(2,1)S(1)} %collective-permute-done.16.rest_2_, ...), custom_call_target="tpu_custom_call" | custom-call | bytes 20000000 | tf_op jit(solution)/shard_map/pallas_call | solution.py:190
  86.9 1.2 collective-permute-done.20.rest_5_.rest_7_
  88.0 1.2 collective-permute-done.21.rest_6_.rest_8_
  89.3 9.7 %shard_map.45 = bf16[352,2048]{1,0:T(8,128)(2,1)} custom-call(s32[8]{0:T(128)S(1)} %stack.56.order, s32[2]{0:T(128)S(1)} %pad_add_fusion.1.choice, bf16[352,2048]{1,0:T(8,128)(2,1)} %collective-permute-done.rest_0_, bf16[352,2048]{1,0:T(8,128)(2,1)} %collective-permute-done.1.rest_1_, bf16[2048,2048]{1,0:T(8,128)(2,1)S(1)} %shard_map.44.rest_2_.rest_4_, ...), custom_call_target="tpu_custom_call" | custom-call | flops 5905580032 | bytes 12000000 | tf_op jit(solution)/shard_map/pallas_call | solution.py:235
  98.9 1.3 collective-permute-start.22
  100.2 9.0 %collective-permute-start.23 = (bf16[352,2048]{1,0:T(8,128)(2,1)}, bf16[352,2048]{1,0:T(8,128)(2,1)}, u32[]{:S(2)}, u32[]{:S(2)}) collective-permute-start(bf16[352,2048]{1,0:T(8,128)(2,1)} %shard_map.45), channel_id=1, source_target_pairs={{16,1},{19,2},{20,5},{23,6},{24,9},{27,10},{28,13},{31,14},{17,16}... | collective-permute-start | bytes 4325384 | tf_op jit(solution)/shard_map/ppermute | solution.py:60
  109.2 9.7 %shard_map.47.own = bf16[352,2048]{1,0:T(8,128)(2,1)} custom-call(s32[8]{0:T(128)S(1)} %stack.56.order, s32[2]{0:T(128)S(1)} %pad_add_fusion.1.choice, bf16[352,2048]{1,0:T(8,128)(2,1)S(1)} %bitcast.20, bf16[352,2048]{1,0:T(8,128)(2,1)S(1)} %bitcast.23, bf16[176,2048]{1,0:T(8,128)(2,1)} %collective-permute-done.2.rest_2_, ...), custom_call_target="tpu_custom_call" | custom-call | flops 5905580032 | bytes 12000000 | tf_op jit(solution)/shard_map/pallas_call | solution.py:235
  119.0 1.4 %collective-permute-start.24 = (bf16[352,2048]{1,0:T(8,128)(2,1)}, bf16[352,2048]{1,0:T(8,128)(2,1)S(1)}, u32[]{:S(2)}, u32[]{:S(2)}) collective-permute-start(bf16[352,2048]{1,0:T(8,128)(2,1)} %shard_map.47.own), channel_id=1, source_target_pairs={{16,0},{19,3},{20,4},{23,7},{24,8},{27,11},{28,12},{31,15},{4,20},... | collective-permute-start | bytes 4325384 | tf_op jit(solution)/shard_map/ppermute | solution.py:60
  120.5 5.0 %collective-permute-done.23.up_back = bf16[352,2048]{1,0:T(8,128)(2,1)} collective-permute-done((bf16[352,2048]{1,0:T(8,128)(2,1)}, bf16[352,2048]{1,0:T(8,128)(2,1)}, u32[]{:S(2)}, u32[]{:S(2)}) %collective-permute-start.23) | collective-permute-done | bytes 1441824 | tf_op jit(solution)/shard_map/ppermute | solution.py:60
  125.5 0.5 shard_map.46.token
  126.0 3.9 %shard_map.48 = (bf16[352,2048]{1,0:T(8,128)(2,1)}, bf16[352,2048]{1,0:T(8,128)(2,1)}) custom-call(s32[2]{0:T(128)S(1)} %pad_add_fusion.pick, s32[1]{0:T(128)} %shard_map.46.token, bf16[352,2048]{1,0:T(8,128)(2,1)} %shard_map.47.own, bf16[352,2048]{1,0:T(8,128)(2,1)S(1)} %collective-permute-done.24.over, ...), custom_call_target="tpu_custom_call" | custom-call | tf_op jit(solution)/shard_map/pallas_call | solution.py:295
  (31 shorter events, 1.2 us)
Async XLA Ops:
  0.6 25.5 %collective-permute-start = (bf16[352,2048]{1,0:T(8,128)(2,1)}, bf16[352,2048]{1,0:T(8,128)(2,1)}, u32[]{:S(2)}, u32[]{:S(2)}) collective-permute-start(bf16[352,2048]{1,0:T(8,128)(2,1)} %bitcast.18), channel_id=1, source_target_pairs={{4,0},{5,1},{6,2},{7,3},{8,12},{9,13},{10,14},{11,15},{16,4},{17,5... | collective-permute-start | bytes 4325384 | tf_op jit(solution)/shard_map/ppermute | solution.py:60
  6.4 20.6 %collective-permute-start.1 = (bf16[352,2048]{1,0:T(8,128)(2,1)}, bf16[352,2048]{1,0:T(8,128)(2,1)}, u32[]{:S(2)}, u32[]{:S(2)}) collective-permute-start(bf16[352,2048]{1,0:T(8,128)(2,1)} %bitcast.21), channel_id=1, source_target_pairs={{1,16},{2,19},{5,20},{6,23},{9,24},{10,27},{13,28},{14,31},{16,17}... | collective-permute-start | bytes 4325384 | tf_op jit(solution)/shard_map/ppermute | solution.py:60
  11.9 7.9 %copy-start = (bf16[2048,352]{0,1:T(8,128)(2,1)S(1)}, bf16[2048,352]{0,1:T(8,128)(2,1)}, u32[]{:S(2)}) copy-start(bf16[2048,352]{0,1:T(8,128)(2,1)} %param.10) | copy-start | bytes 4325380
  11.9 7.9 %copy-start.1 = (bf16[2048,352]{0,1:T(8,128)(2,1)S(1)}, bf16[2048,352]{0,1:T(8,128)(2,1)}, u32[]{:S(2)}) copy-start(bf16[2048,352]{0,1:T(8,128)(2,1)} %param.11) | copy-start | bytes 4325380
  13.1 4.5 %collective-permute-start.2 = (bf16[176,2048]{1,0:T(8,128)(2,1)}, bf16[176,2048]{1,0:T(8,128)(2,1)}, u32[]{:S(2)}, u32[]{:S(2)}) collective-permute-start(bf16[176,2048]{1,0:T(8,128)(2,1)} %get-tuple-element.81), channel_id=1, source_target_pairs={{0,16},{3,19},{4,20},{7,23},{8,24},{11,27},{12,28},{15,31},{20,4},... | collective-permute-start | bytes 2162696 | tf_op jit(solution)/shard_map/ppermute | solution.py:60
  14.5 5.3 %collective-permute-start.3 = (bf16[176,2048]{1,0:T(8,128)(2,1)}, bf16[176,2048]{1,0:T(8,128)(2,1)}, u32[]{:S(2)}, u32[]{:S(2)}) collective-permute-start(bf16[176,2048]{1,0:T(8,128)(2,1)} %get-tuple-element.80), channel_id=1, source_target_pairs={{0,16},{3,19},{4,20},{7,23},{8,24},{11,27},{12,28},{15,31},{20,4},... | collective-permute-start | bytes 2162696 | tf_op jit(solution)/shard_map/ppermute | solution.py:60
  29.9 7.9 %collective-permute-start.6 = (bf16[1,128,1152]{2,1,0:T(8,128)(2,1)S(1)}, bf16[1,128,1152]{2,1,0:T(8,128)(2,1)S(1)}, u32[]{:S(2)}, u32[]{:S(2)}) collective-permute-start(bf16[1,128,1152]{2,1,0:T(8,128)(2,1)S(1)} %get-tuple-element.71), channel_id=1, source_target_pairs={{0,1},{1,0},{2,3},{3,2},{4,5},{5,4},{6,7},{7,6},{8,9},{9,8},{10,11... | collective-permute-start | bytes 884744 | tf_op jit(solution)/shard_map/ppermute | solution.py:60
  30.0 10.0 %collective-permute-start.4 = (bf16[1,128,1152]{2,1,0:T(8,128)(2,1)S(1)}, bf16[1,128,1152]{2,1,0:T(8,128)(2,1)S(1)}, u32[]{:S(2)}, u32[]{:S(2)}) collective-permute-start(bf16[1,128,1152]{2,1,0:T(8,128)(2,1)S(1)} %get-tuple-element.69), channel_id=1, source_target_pairs={{0,3},{1,2},{2,1},{3,0},{4,7},{5,6},{6,5},{7,4},{8,11},{9,10},{10,... | collective-permute-start | bytes 884744 | tf_op jit(solution)/shard_map/ppermute | solution.py:60
  31.9 8.2 %collective-permute-start.12 = (bf16[1,128,1152]{2,1,0:T(8,128)(2,1)S(1)}, bf16[1,128,1152]{2,1,0:T(8,128)(2,1)S(1)}, u32[]{:S(2)}, u32[]{:S(2)}) collective-permute-start(bf16[1,128,1152]{2,1,0:T(8,128)(2,1)S(1)} %get-tuple-element.76), channel_id=1, source_target_pairs={{0,1},{1,0},{2,3},{3,2},{4,5},{5,4},{6,7},{7,6},{8,9},{9,8},{10,11... | collective-permute-start | bytes 884744 | tf_op jit(solution)/shard_map/ppermute | solution.py:60
  32.7 8.4 %collective-permute-start.10 = (bf16[1,128,1152]{2,1,0:T(8,128)(2,1)S(1)}, bf16[1,128,1152]{2,1,0:T(8,128)(2,1)S(1)}, u32[]{:S(2)}, u32[]{:S(2)}) collective-permute-start(bf16[1,128,1152]{2,1,0:T(8,128)(2,1)S(1)} %get-tuple-element.74), channel_id=1, source_target_pairs={{0,3},{1,2},{2,1},{3,0},{4,7},{5,6},{6,5},{7,4},{8,11},{9,10},{10,... | collective-permute-start | bytes 884744 | tf_op jit(solution)/shard_map/ppermute | solution.py:60
  37.9 10.3 %collective-permute-start.7 = (bf16[2,128,1152]{2,1,0:T(8,128)(2,1)S(1)}, bf16[2,128,1152]{2,1,0:T(8,128)(2,1)S(1)}, u32[]{:S(2)}, u32[]{:S(2)}) collective-permute-start(bf16[2,128,1152]{2,1,0:T(8,128)(2,1)S(1)} %fusion.1), channel_id=1, source_target_pairs={{0,3},{1,2},{2,1},{3,0},{4,7},{5,6},{6,5},{7,4},{8,11},{9,10},{10,... | collective-permute-start | bytes 1769480 | tf_op jit(solution)/shard_map/ppermute | solution.py:60
  40.0 9.1 %collective-permute-start.5 = (bf16[2,128,1152]{2,1,0:T(8,128)(2,1)S(1)}, bf16[2,128,1152]{2,1,0:T(8,128)(2,1)S(1)}, u32[]{:S(2)}, u32[]{:S(2)}) collective-permute-start(bf16[2,128,1152]{2,1,0:T(8,128)(2,1)S(1)} %fusion), channel_id=1, source_target_pairs={{0,1},{1,0},{2,3},{3,2},{4,5},{5,4},{6,7},{7,6},{8,9},{9,8},{10,11... | collective-permute-start | bytes 1769480 | tf_op jit(solution)/shard_map/ppermute | solution.py:60
  40.3 14.3 %collective-permute-start.13 = (bf16[2,128,1152]{2,1,0:T(8,128)(2,1)S(1)}, bf16[2,128,1152]{2,1,0:T(8,128)(2,1)S(1)}, u32[]{:S(2)}, u32[]{:S(2)}) collective-permute-start(bf16[2,128,1152]{2,1,0:T(8,128)(2,1)S(1)} %fusion.3), channel_id=1, source_target_pairs={{0,3},{1,2},{2,1},{3,0},{4,7},{5,6},{6,5},{7,4},{8,11},{9,10},{10,... | collective-permute-start | bytes 1769480 | tf_op jit(solution)/shard_map/ppermute | solution.py:60
  41.3 14.2 %collective-permute-start.11 = (bf16[2,128,1152]{2,1,0:T(8,128)(2,1)S(1)}, bf16[2,128,1152]{2,1,0:T(8,128)(2,1)S(1)}, u32[]{:S(2)}, u32[]{:S(2)}) collective-permute-start(bf16[2,128,1152]{2,1,0:T(8,128)(2,1)S(1)} %fusion.2), channel_id=1, source_target_pairs={{0,1},{1,0},{2,3},{3,2},{4,5},{5,4},{6,7},{7,6},{8,9},{9,8},{10,11... | collective-permute-start | bytes 1769480 | tf_op jit(solution)/shard_map/ppermute | solution.py:60
  49.4 12.9 %collective-permute-start.8 = (bf16[2,128,1152]{2,1,0:T(8,128)(2,1)S(1)}, bf16[2,128,1152]{2,1,0:T(8,128)(2,1)S(1)}, u32[]{:S(2)}, u32[]{:S(2)}) collective-permute-start(bf16[2,128,1152]{2,1,0:T(8,128)(2,1)S(1)} %add_convert_fusion.3), channel_id=1, source_target_pairs={{0,12},{1,13},{2,14},{3,15},{4,8},{5,9},{6,10},{7,11},{8,4},{9,5},... | collective-permute-start | bytes 1769480 | tf_op jit(solution)/shard_map/ppermute | solution.py:60
  55.7 12.9 %collective-permute-start.14 = (bf16[2,128,1152]{2,1,0:T(8,128)(2,1)S(1)}, bf16[2,128,1152]{2,1,0:T(8,128)(2,1)S(1)}, u32[]{:S(2)}, u32[]{:S(2)}) collective-permute-start(bf16[2,128,1152]{2,1,0:T(8,128)(2,1)S(1)} %add_convert_fusion.1), channel_id=1, source_target_pairs={{0,12},{1,13},{2,14},{3,15},{4,8},{5,9},{6,10},{7,11},{8,4},{9,5},... | collective-permute-start | bytes 1769480 | tf_op jit(solution)/shard_map/ppermute | solution.py:60
  62.4 13.2 %collective-permute-start.9 = (bf16[2,128,1152]{2,1,0:T(8,128)(2,1)S(1)}, bf16[2,128,1152]{2,1,0:T(8,128)(2,1)S(1)}, u32[]{:S(2)}, u32[]{:S(2)}) collective-permute-start(bf16[2,128,1152]{2,1,0:T(8,128)(2,1)S(1)} %add_convert_fusion.2.rest_4_), channel_id=1, source_target_pairs={{0,1},{1,0},{2,3},{3,2},{4,5},{5,4},{6,7},{7,6},{8,9},{9,8},{10,11... | collective-permute-start | bytes 1769480 | tf_op jit(solution)/shard_map/ppermute | solution.py:60
  62.5 12.9 %collective-permute-start.16 = (bf16[2,128,1152]{2,1,0:T(8,128)(2,1)S(1)}, bf16[2,128,1152]{2,1,0:T(8,128)(2,1)S(1)}, u32[]{:S(2)}, u32[]{:S(2)}) collective-permute-start(bf16[2,128,1152]{2,1,0:T(8,128)(2,1)S(1)} %add_convert_fusion.2.rest_4_), channel_id=1, source_target_pairs={{0,3},{1,2},{2,1},{3,0},{4,7},{5,6},{6,5},{7,4},{8,11},{9,10},{10,... | collective-permute-start | bytes 1769480 | tf_op jit(solution)/shard_map/ppermute | solution.py:60
  68.7 13.3 %collective-permute-start.17 = (bf16[2,128,1152]{2,1,0:T(8,128)(2,1)S(1)}, bf16[2,128,1152]{2,1,0:T(8,128)(2,1)S(1)}, u32[]{:S(2)}, u32[]{:S(2)}) collective-permute-start(bf16[2,128,1152]{2,1,0:T(8,128)(2,1)S(1)} %add_convert_fusion.rest_5_), channel_id=1, source_target_pairs={{0,3},{1,2},{2,1},{3,0},{4,7},{5,6},{6,5},{7,4},{8,11},{9,10},{10,... | collective-permute-start | bytes 1769480 | tf_op jit(solution)/shard_map/ppermute | solution.py:60
  71.6 10.5 %collective-permute-start.15 = (bf16[2,128,1152]{2,1,0:T(8,128)(2,1)S(1)}, bf16[2,128,1152]{2,1,0:T(8,128)(2,1)S(1)}, u32[]{:S(2)}, u32[]{:S(2)}) collective-permute-start(bf16[2,128,1152]{2,1,0:T(8,128)(2,1)S(1)} %add_convert_fusion.rest_5_), channel_id=1, source_target_pairs={{0,1},{1,0},{2,3},{3,2},{4,5},{5,4},{6,7},{7,6},{8,9},{9,8},{10,11... | collective-permute-start | bytes 1769480 | tf_op jit(solution)/shard_map/ppermute | solution.py:60
  75.5 11.4 %collective-permute-start.18 = (bf16[1,128,1152]{2,1,0:T(8,128)(2,1)S(1)}, bf16[1,128,1152]{2,1,0:T(8,128)(2,1)S(1)}, u32[]{:S(2)}, u32[]{:S(2)}) collective-permute-start(bf16[1,128,1152]{2,1,0:T(8,128)(2,1)S(1)} %slice.130), channel_id=1, source_target_pairs={{0,1},{1,0},{2,3},{3,2},{4,5},{5,4},{6,7},{7,6},{8,9},{9,8},{10,11... | collective-permute-start | bytes 884744 | tf_op jit(solution)/shard_map/ppermute | solution.py:60
  75.6 11.3 %collective-permute-start.19 = (bf16[1,128,1152]{2,1,0:T(8,128)(2,1)S(1)}, bf16[1,128,1152]{2,1,0:T(8,128)(2,1)S(1)}, u32[]{:S(2)}, u32[]{:S(2)}) collective-permute-start(bf16[1,128,1152]{2,1,0:T(8,128)(2,1)S(1)} %slice.131), channel_id=1, source_target_pairs={{0,3},{1,2},{2,1},{3,0},{4,7},{5,6},{6,5},{7,4},{8,11},{9,10},{10,... | collective-permute-start | bytes 884744 | tf_op jit(solution)/shard_map/ppermute | solution.py:60
  82.1 5.9 %collective-permute-start.20 = (bf16[1,128,1152]{2,1,0:T(8,128)(2,1)S(1)}, bf16[1,128,1152]{2,1,0:T(8,128)(2,1)S(1)}, u32[]{:S(2)}, u32[]{:S(2)}) collective-permute-start(bf16[1,128,1152]{2,1,0:T(8,128)(2,1)S(1)} %slice.132), channel_id=1, source_target_pairs={{0,1},{1,0},{2,3},{3,2},{4,5},{5,4},{6,7},{7,6},{8,9},{9,8},{10,11... | collective-permute-start | bytes 884744 | tf_op jit(solution)/shard_map/ppermute | solution.py:60
  82.2 7.0 %collective-permute-start.21 = (bf16[1,128,1152]{2,1,0:T(8,128)(2,1)S(1)}, bf16[1,128,1152]{2,1,0:T(8,128)(2,1)S(1)}, u32[]{:S(2)}, u32[]{:S(2)}) collective-permute-start(bf16[1,128,1152]{2,1,0:T(8,128)(2,1)S(1)} %slice.133), channel_id=1, source_target_pairs={{0,3},{1,2},{2,1},{3,0},{4,7},{5,6},{6,5},{7,4},{8,11},{9,10},{10,... | collective-permute-start | bytes 884744 | tf_op jit(solution)/shard_map/ppermute | solution.py:60
  98.9 21.5 %collective-permute-start.22 = (bf16[352,2048]{1,0:T(8,128)(2,1)}, bf16[352,2048]{1,0:T(8,128)(2,1)}, u32[]{:S(2)}, u32[]{:S(2)}) collective-permute-start(bf16[352,2048]{1,0:T(8,128)(2,1)} %shard_map.45), channel_id=1, source_target_pairs={{0,4},{1,5},{2,6},{3,7},{12,8},{13,9},{14,10},{15,11},{4,16},{5,17... | collective-permute-start | bytes 4325384 | tf_op jit(solution)/shard_map/ppermute | solution.py:60
  100.2 25.3 %collective-permute-start.23 = (bf16[352,2048]{1,0:T(8,128)(2,1)}, bf16[352,2048]{1,0:T(8,128)(2,1)}, u32[]{:S(2)}, u32[]{:S(2)}) collective-permute-start(bf16[352,2048]{1,0:T(8,128)(2,1)} %shard_map.45), channel_id=1, source_target_pairs={{16,1},{19,2},{20,5},{23,6},{24,9},{27,10},{28,13},{31,14},{17,16}... | collective-permute-start | bytes 4325384 | tf_op jit(solution)/shard_map/ppermute | solution.py:60
  119.0 7.0 %collective-permute-start.24 = (bf16[352,2048]{1,0:T(8,128)(2,1)}, bf16[352,2048]{1,0:T(8,128)(2,1)S(1)}, u32[]{:S(2)}, u32[]{:S(2)}) collective-permute-start(bf16[352,2048]{1,0:T(8,128)(2,1)} %shard_map.47.own), channel_id=1, source_target_pairs={{16,0},{19,3},{20,4},{23,7},{24,8},{27,11},{28,12},{31,15},{4,20},... | collective-permute-start | bytes 4325384 | tf_op jit(solution)/shard_map/ppermute | solution.py:60
